TPU v7x, 32 devices: a whole 2x2x4 slice. The times are simulated.
32 devices in a mesh: depth: 2 (over x), lat: 16 (over z, y, core).
Axes of the slice: x: 2, y: 2, z: 4, core: 2. Of those that a mesh axis runs over, the one named last changes fastest.
Arguments:
- fem_disp: float32 [3, 8, 128, 256], P(None, 'depth', 'lat'), may hold values from -6 to 6
- fem_vel: float32 [3, 8, 128, 256], P(None, 'depth', 'lat'), may hold values from -6 to 6
- modulus: float32 [8, 128, 256], P('depth', 'lat'), may hold values from 0.5 to 5
- inv_mass: float32 [8, 128, 256], P('depth', 'lat'), may hold values from 0.5 to 2
- element_stiffness: float32 [24, 24], replicated, may hold values from -1.25 to 1.25
- pd_pos: float32 [3, 65536], P(None, ('depth', 'lat')), may hold values from -4 to 4
- pd_disp: float32 [3, 65536], P(None, ('depth', 'lat')), may hold values from -6 to 6
- pd_vel: float32 [3, 65536], P(None, ('depth', 'lat')), may hold values from -6 to 6
- conv_state: float32 [9, 2048], P(None, ('depth', 'lat')), may hold values from -5 to 5
- conv_owner: int32 [2048, 1], P(('depth', 'lat')), may hold values from 0 to 15; in each aligned block of 64 rows (0 to 63, 64 to 127, ...) at most 8 rows name the same one
- family: int32 [544, 8], P(('depth', 'lat')), may hold values from 0 to 51
- ov_owner: int32 [2048, 1], P(('depth', 'lat')), may hold values from 0 to 15; in each aligned block of 64 rows (0 to 63, 64 to 127, ...) at most 8 rows name the same one
- ov_node: int32 [2048], P(('depth', 'lat')), may hold values from 0 to 8191
- ov_target: int32 [2048], P(('depth', 'lat')), may hold values from 0 to 2047
- ov_stiff: float32 [2048], P(('depth', 'lat')), may hold values from 0.5 to 4
Outputs:
- fem_vel_new: float32 [3, 8, 128, 256], P(None, 'depth', 'lat')
- pd_vel_new: float32 [3, 69632], P(None, ('depth', 'lat'))
Inputs may be any that keep to these rules, and one draw needn't show every extreme that they name: `conv_owner`: among the 64 rows of one device at most 8 name the same owner, and some owner gets exactly 8 of them. `ov_owner`: among the 64 entries of one device at most 8 name the same owner, and some owner gets exactly 8 of them. `family`: values below 17 number blocks of the previous lat index's table, the next 17 the device's own, the next 17 the following lat index's; 51 is the empty block.
All inputs are finite; a program needn't handle non-finite values.
Results may differ from a plain program's by a relative error of at most 0.0003.
Values sent between devices are 32-bit elements; how exact they have to be, the bound alone decides.
No kernel may reach another device: no remote copies, remote signals or barrier semaphores. Data moves between devices by JAX's collectives and lax.ppermute only.
A program may use at most 64 MiB of HBM per device.

v0:
```python
import jax
import jax.numpy as jnp
from jax import lax
from jax.sharding import PartitionSpec as P

BLOCK = 128
CAP = 8
OCAP = 8


time_step = 0.5
horizon_sq = 2.0
bond_gain = 8.0
highest = lax.Precision.HIGHEST


def padded_2(block, sides, width):
    for axis, dim in sides:
        count = lax.axis_size(axis)
        forward = [(i, i + 1) for i in range(count - 1)]
        backward = [(target, source) for source, target in forward]
        low = lax.ppermute(
            lax.slice_in_dim(block, block.shape[dim] - width, None, axis=dim), axis, forward
        )
        high = lax.ppermute(lax.slice_in_dim(block, 0, width, axis=dim), axis, backward)
        block = jnp.concatenate([low, block, high], axis=dim)
    return block


def element_forces(padded, stiffness):
    span_x = padded.shape[1] - 2
    span_y = padded.shape[2] - 2
    span_z = padded.shape[3] - 2
    element = None
    for corner in range(8):
        shift_x = corner // 4
        shift_y = corner // 2 % 2
        shift_z = corner % 2
        shifted = padded[
            0:3,
            shift_x : shift_x + span_x + 1,
            shift_y : shift_y + span_y + 1,
            shift_z : shift_z + span_z + 1,
        ]
        product = jnp.einsum(
            "ij,jxyz->ixyz", stiffness[:, 3 * corner : 3 * corner + 3], shifted, precision=highest
        )
        element = product if element is None else element + product
    modulus = padded[3, 0 : span_x + 1, 0 : span_y + 1, 0 : span_z + 1]
    element = element * modulus[None]
    force = jnp.zeros((3, span_x, span_y, span_z), jnp.float32)
    for corner in range(8):
        shift_x = corner // 4
        shift_y = corner // 2 % 2
        shift_z = corner % 2
        force = (
            force
            + element[
                3 * corner : 3 * corner + 3,
                1 - shift_x : 1 - shift_x + span_x,
                1 - shift_y : 1 - shift_y + span_y,
                1 - shift_z : 1 - shift_z + span_z,
            ]
        )
    return force


def bond_forces(table, extended, family):
    count = table.shape[1] // BLOCK
    own_blocks = table.reshape(7, count, BLOCK)
    ext_blocks = extended.reshape(7, -1, BLOCK)
    scale = bond_gain / (BLOCK * family.shape[1])

    def one_block(index, result):
        current = lax.dynamic_index_in_dim(own_blocks, index, 1, keepdims=False)
        members = lax.dynamic_index_in_dim(family, index, 0, keepdims=False)
        others = jnp.take(ext_blocks, members, axis=1)
        distance = jnp.zeros((members.shape[0], BLOCK, BLOCK), jnp.float32)
        for component in range(3):
            offset = others[component][:, None, :] - current[component][None, :, None]
            distance = distance + offset * offset
        weight = jnp.exp(-distance / horizon_sq) * current[6][None, :, None] * others[6][:, None, :]
        pulled = jnp.einsum("fij,cfj->ci", weight, others[3:6], precision=highest)
        totals = jnp.sum(weight, axis=(0, 2))
        forces = scale * (pulled - current[3:6] * totals[None, :])
        return lax.dynamic_update_index_in_dim(result, forces, index, 1)

    result = lax.fori_loop(0, count, one_block, jnp.zeros((3, count, BLOCK), jnp.float32))
    return result.reshape(3, -1)


def slot_numbers(owner, peers, capacity):
    match = (owner[:, None] == jnp.arange(peers, dtype=jnp.int32)[None, :]).astype(jnp.int32)
    rank = jnp.sum((jnp.cumsum(match, axis=0) - 1) * match, axis=1)
    return owner * capacity + rank


def shards(
    fem_disp,
    fem_vel,
    modulus,
    inv_mass,
    element_stiffness,
    pd_pos,
    pd_disp,
    pd_vel,
    conv_state,
    conv_owner,
    family,
    ov_owner,
    ov_node,
    ov_target,
    ov_stiff,
):
    peers = lax.axis_size("lat")
    stacked = jnp.concatenate([fem_disp, modulus[None]], axis=0)
    across = padded_2(stacked, (("lat", 2),), 1)
    widened = padded_2(across, (("depth", 1),), 1)
    widened = jnp.pad(widened, ((0, 0), (0, 0), (0, 0), (1, 1)))
    conv_rows = conv_state.shape[1]
    tail_slots = peers * CAP
    owner = conv_owner[:, 0]
    slots = slot_numbers(owner, peers, CAP)
    payload = jnp.concatenate([conv_state, jnp.ones((1, conv_rows), jnp.float32)], axis=0)
    outgoing = jnp.zeros((10, tail_slots), jnp.float32).at[:, slots].set(payload)
    arrived = lax.all_to_all(outgoing, "lat", split_axis=1, concat_axis=1, tiled=True)
    own_count = pd_pos.shape[1]
    own_rows = jnp.concatenate([pd_pos, pd_disp, jnp.ones((1, own_count), jnp.float32)], axis=0)
    tail_rows = jnp.concatenate([arrived[0:6], arrived[9:10]], axis=0)
    table = jnp.concatenate([own_rows, tail_rows], axis=1)
    extended = padded_2(table, (("lat", 1),), table.shape[1])
    extended = jnp.pad(extended, ((0, 0), (0, BLOCK)))
    bond = bond_forces(table, extended, family)
    flat_disp = fem_disp.reshape(3, -1)
    ov_slots = slot_numbers(ov_owner[:, 0], peers, OCAP)
    ov_width = peers * OCAP
    ov_payload = jnp.concatenate(
        [jnp.take(flat_disp, ov_node, axis=1), ov_stiff[None], ov_target.astype(jnp.float32)[None]],
        axis=0,
    )
    ov_base = jnp.concatenate(
        [jnp.zeros((4, ov_width), jnp.float32), -jnp.ones((1, ov_width), jnp.float32)], axis=0
    )
    ov_outgoing = ov_base.at[:, ov_slots].set(ov_payload)
    incoming = lax.all_to_all(ov_outgoing, "lat", split_axis=1, concat_axis=1, tiled=True)
    target = incoming[4].astype(jnp.int32)
    live = (target >= 0).astype(jnp.float32)
    safe = jnp.maximum(target, 0)
    coupling = incoming[3][None] * (incoming[0:3] - jnp.take(pd_disp, safe, axis=1)) * live[None]
    pd_couple = jnp.zeros((3, own_count), jnp.float32).at[:, safe].add(coupling)
    returned = lax.all_to_all(coupling, "lat", split_axis=1, concat_axis=1, tiled=True)
    entry_force = jnp.take(returned, ov_slots, axis=1)
    fem_couple = jnp.zeros_like(flat_disp).at[:, ov_node].add(-entry_force).reshape(fem_disp.shape)
    internal = element_forces(widened, element_stiffness)
    fem_vel_new = fem_vel + time_step * inv_mass[None] * (fem_couple - internal)
    own_new = pd_vel + time_step * (bond[:, :own_count] + pd_couple)
    tail_new = arrived[6:9] + time_step * bond[:, own_count:]
    pd_vel_new = jnp.concatenate([own_new, tail_new], axis=1)
    return (fem_vel_new, pd_vel_new)


def solution(mesh):
    return jax.shard_map(
        shards,
        mesh=mesh,
        in_specs=(
            P(None, "depth", "lat", None),
            P(None, "depth", "lat", None),
            P("depth", "lat", None),
            P("depth", "lat", None),
            P(),
            P(None, ("depth", "lat")),
            P(None, ("depth", "lat")),
            P(None, ("depth", "lat")),
            P(None, ("depth", "lat")),
            P(("depth", "lat"), None),
            P(("depth", "lat"), None),
            P(("depth", "lat"), None),
            P(("depth", "lat")),
            P(("depth", "lat")),
            P(("depth", "lat")),
        ),
        out_specs=(P(None, "depth", "lat", None), P(None, ("depth", "lat"))),
        check_vma=False,
    )
```

profile of v0, /device:TPU:10, one launch (start us, length us, event | category | flops | bytes accessed | tf_op | source)
XLA Modules:
  0.0 113.6 jit_solution(7380499947471132069)
XLA Ops:
  4.4 3.5 %copy.121 = f32[3,4,8,256]{0,3,2,1:T(8,128)} copy(f32[3,4,8,256]{3,2,1,0:T(8,128)} %param.17) | data formatting | bytes 196608 | tf_op args[0]
  7.9 2.8 %gather_fusion.1 = f32[64,3]{1,0:T(8,128)S(1)} fusion(f32[3,8192]{0,1:T(8,128)} %bitcast.185, s32[1024]{0:T(1024)S(1)} %pad_clamp_fusion.3), kind=kCustom, calls=%fused_computation.1 | custom fusion | bytes 1792 | tf_op jit(solution)/shard_map/jit(_take)/gather | solution.py:138
  12.6 6.3 %all-to-all-start = ((f32[5,16,8]{2,0,1:T(8,128)}), f32[5,16,8]{2,0,1:T(8,128)S(1)}, u32[]{:S(2)}, u32[]{:S(2)}) async-start(f32[5,16,8]{2,0,1:T(8,128)} %copy.124), calls=%async_computation | async-start | bytes 131072 | tf_op jit(solution)/shard_map/all_to_all | solution.py:145
  19.0 2.1 %collective-permute-start = (f32[4,4,1,256]{3,0,2,1:T(4,128)S(1)}, f32[4,4,1,256]{3,0,2,1:T(4,128)S(1)}, u32[]{:S(2)}, u32[]{:S(2)}) collective-permute-start(f32[4,4,1,256]{3,0,2,1:T(4,128)S(1)} %get-tuple-element.147), channel_id=1, source_target_pairs={{0,1},{1,2},{2,3},{3,4},{4,5},{5,6},{6,7},{7,8},{8,9},{9,10},{10,1... | collective-permute-start | bytes 49160 | tf_op jit(solution)/shard_map/ppermute | solution.py:22
  21.1 4.4 %collective-permute-start.1 = (f32[4,4,1,256]{3,0,2,1:T(4,128)S(1)}, f32[4,4,1,256]{3,0,2,1:T(4,128)S(1)}, u32[]{:S(2)}, u32[]{:S(2)}) collective-permute-start(f32[4,4,1,256]{3,0,2,1:T(4,128)S(1)} %get-tuple-element.148), channel_id=1, source_target_pairs={{1,0},{2,1},{3,2},{4,3},{5,4},{6,5},{7,6},{8,7},{9,8},{10,9},{11,1... | collective-permute-start | bytes 49160 | tf_op jit(solution)/shard_map/ppermute | solution.py:25
  28.2 5.1 %all-to-all-start.1 = ((f32[3,16,8]{2,0,1:T(4,128)}), f32[3,16,8]{2,0,1:T(4,128)S(1)}, u32[]{:S(2)}, u32[]{:S(2)}) async-start(f32[3,16,8]{2,0,1:T(4,128)} %get-tuple-element.153), calls=%async_computation.1 | async-start | bytes 65536 | tf_op jit(solution)/shard_map/all_to_all | solution.py:151
  33.4 1.3 %scatter_custom_fusion.2 = f32[10,128]{0,1:T(8,128)} fusion(s32[64]{0:T(128)S(1)} %fusion.80, f32[64,10]{1,0:T(8,128)S(1)} %copy.148, f32[]{:T(128)} %constant.146.clone.1), kind=kCustom, calls=%fused_computation.114 | custom fusion | bytes 5124 | tf_op jit(solution)/shard_map/scatter | solution.py:125
  34.7 3.6 %all-to-all-done.1 = f32[3,16,8]{2,0,1:T(4,128)S(1)} async-done(((f32[3,16,8]{2,0,1:T(4,128)}), f32[3,16,8]{2,0,1:T(4,128)S(1)}, u32[]{:S(2)}, u32[]{:S(2)}) %all-to-all-start.1) | async-done | bytes 1568 | tf_op jit(solution)/shard_map/all_to_all | solution.py:151
  38.4 5.0 %all-to-all-start.2 = ((f32[10,16,8]{0,2,1:T(8,128)}), f32[10,16,8]{0,2,1:T(8,128)S(1)}, u32[]{:S(2)}, u32[]{:S(2)}) async-start(f32[10,16,8]{0,2,1:T(8,128)} %bitcast.55), calls=%async_computation.2 | async-start | bytes 131072 | tf_op jit(solution)/shard_map/all_to_all | solution.py:126
  44.2 3.2 %scatter_custom_fusion.1 = f32[3,8192]{0,1:T(8,128)} fusion(s32[64]{0:T(128)S(1)} %compare_select_fusion.4, f32[]{:T(128)} %constant.146.clone.1, f32[]{:T(128)} %constant.155.clone.1, pred[64]{0:T(512)(128)(4,1)S(1)} %get-tuple-element.135, f32[3,128]{0,1:T(8,128)S(1)} %bitcast.189, s32[1024]{0:T(1024)S(1)} %pad_clamp_fusion.1), kind=kCustom, calls=%fused_computation.39 | custom fusion | flops 576 | bytes 168456 | tf_op jit(solution)/shard_map/scatter-add | solution.py:153
  47.4 2.8 %copy.146 = f32[3,4,8,256]{3,0,2,1:T(4,128)S(1)} copy(f32[3,4,8,256]{0,3,2,1:T(8,128)} %bitcast.182) | data formatting | bytes 196608 | tf_op jit(solution)/shard_map/reshape | solution.py:153
  52.0 4.5 %collective-permute-start.3 = (f32[4,1,10,256]{3,0,2,1:T(4,128)S(1)}, f32[4,1,10,256]{3,0,2,1:T(4,128)S(1)}, u32[]{:S(2)}, u32[]{:S(2)}) collective-permute-start(f32[4,1,10,256]{3,0,2,1:T(4,128)S(1)} %get-tuple-element.146), channel_id=1, source_target_pairs={{16,0},{17,1},{18,2},{19,3},{20,4},{21,5},{22,6},{23,7},{24,8},{25... | collective-permute-start | bytes 122888 | tf_op jit(solution)/shard_map/ppermute | solution.py:25
  56.6 1.9 %collective-permute-start.4 = (f32[7,2176]{1,0:T(8,128)S(1)}, f32[7,2176]{1,0:T(8,128)S(1)}, u32[]{:S(2)}, u32[]{:S(2)}) collective-permute-start(f32[7,2176]{1,0:T(8,128)S(1)} %maximum_maximum_fusion), channel_id=1, source_target_pairs={{0,1},{1,2},{2,3},{3,4},{4,5},{5,6},{6,7},{7,8},{8,9},{9,10},{10,1... | collective-permute-start | bytes 182792 | tf_op jit(solution)/shard_map/ppermute | solution.py:22
  58.5 4.7 %collective-permute-start.5 = (f32[7,2176]{1,0:T(8,128)S(1)}, f32[7,2176]{1,0:T(8,128)S(1)}, u32[]{:S(2)}, u32[]{:S(2)}) collective-permute-start(f32[7,2176]{1,0:T(8,128)S(1)} %maximum_maximum_fusion), channel_id=1, source_target_pairs={{1,0},{2,1},{3,2},{4,3},{5,4},{6,5},{7,6},{8,7},{9,8},{10,9},{11,1... | collective-permute-start | bytes 182792 | tf_op jit(solution)/shard_map/ppermute | solution.py:25
  63.7 1.5 %fusion.21 = f32[5,9,257,24]{2,3,1,0:T(8,128)S(1)} fusion(f32[4,6,10,258]{3,0,2,1:T(4,128)S(1)} %select_maximum_fusion, f32[24,24]{1,0:T(8,128)S(1)} %copy-done), kind=kOutput, calls=%fused_computation.51 | convolution fusion | flops 9992160 | bytes 1399008 | tf_op jit(solution)/shard_map/ij,jxyz->ixyz/dot_general | solution.py:45
  65.2 1.5 %fusion.23 = f32[5,9,257,24]{2,3,1,0:T(8,128)S(1)} fusion(f32[4,6,10,258]{3,0,2,1:T(4,128)S(1)} %select_maximum_fusion, f32[24,24]{1,0:T(8,128)S(1)} %copy-done), kind=kOutput, calls=%fused_computation.53 | convolution fusion | flops 9992160 | bytes 1399008 | tf_op jit(solution)/shard_map/ij,jxyz->ixyz/dot_general | solution.py:45
  66.7 1.5 %fusion.25 = f32[5,9,257,24]{2,3,1,0:T(8,128)S(1)} fusion(f32[4,6,10,258]{3,0,2,1:T(4,128)S(1)} %select_maximum_fusion, f32[24,24]{1,0:T(8,128)S(1)} %copy-done), kind=kOutput, calls=%fused_computation.55 | convolution fusion | flops 9992160 | bytes 1399008 | tf_op jit(solution)/shard_map/ij,jxyz->ixyz/dot_general | solution.py:45
  68.2 1.5 %fusion.27 = f32[5,9,257,24]{2,3,1,0:T(8,128)S(1)} fusion(f32[4,6,10,258]{3,0,2,1:T(4,128)S(1)} %select_maximum_fusion, f32[24,24]{1,0:T(8,128)S(1)} %copy-done), kind=kOutput, calls=%fused_computation.57 | convolution fusion | flops 9992160 | bytes 1399008 | tf_op jit(solution)/shard_map/ij,jxyz->ixyz/dot_general | solution.py:45
  69.7 1.5 %fusion.29 = f32[5,9,257,24]{2,3,1,0:T(8,128)S(1)} fusion(f32[4,6,10,258]{3,0,2,1:T(4,128)S(1)} %select_maximum_fusion, f32[24,24]{1,0:T(8,128)S(1)} %copy-done), kind=kOutput, calls=%fused_computation.59 | convolution fusion | flops 9992160 | bytes 1399008 | tf_op jit(solution)/shard_map/ij,jxyz->ixyz/dot_general | solution.py:45
  71.2 1.5 %fusion.31 = f32[5,9,257,24]{2,3,1,0:T(8,128)S(1)} fusion(f32[4,6,10,258]{3,0,2,1:T(4,128)S(1)} %select_maximum_fusion, f32[24,24]{1,0:T(8,128)S(1)} %copy-done), kind=kOutput, calls=%fused_computation.61 | convolution fusion | flops 9992160 | bytes 1399008 | tf_op jit(solution)/shard_map/ij,jxyz->ixyz/dot_general | solution.py:45
  72.8 1.4 %fusion.33 = f32[5,9,257,24]{2,3,1,0:T(8,128)S(1)} fusion(f32[4,6,10,258]{3,0,2,1:T(4,128)S(1)} %select_maximum_fusion, f32[24,24]{1,0:T(8,128)S(1)} %copy-done), kind=kOutput, calls=%fused_computation.63 | convolution fusion | flops 9992160 | bytes 1399008 | tf_op jit(solution)/shard_map/ij,jxyz->ixyz/dot_general | solution.py:45
  74.3 2.3 %multiply_bitcast_fusion = f32[24,5,9,257]{3,0,2,1:T(8,128)S(1)} fusion(f32[5,9,257,24]{2,3,1,0:T(8,128)S(1)} %fusion.21, f32[5,9,257,24]{2,3,1,0:T(8,128)S(1)} %fusion.23, f32[5,9,257,24]{2,3,1,0:T(8,128)S(1)} %fusion.25, f32[5,9,257,24]{2,3,1,0:T(8,128)S(1)} %fusion.27, f32[5,9,257,24]{2,3,1,0:T(8,128)S(1)} %fusion.29, f32[5,9,257,24]{2,3,1,0:T(8,128)S(1)} %fusion.33, ...), kind=kOutput, calls=%fused_computation.41 | convolution fusion | flops 12212640 | bytes 13134048 | tf_op jit(solution)/shard_map/ij,jxyz->ixyz/dot_general | solution.py:45
  77.7 32.4 %while.13 = (s32[]{:T(128)}, f32[3,17,128]{2,0,1:T(4,128)S(1)}, s32[17,8]{1,0:T(8,128)S(1)}, f32[7,52,128]{2,0,1:T(8,128)S(1)}, f32[7,17,128]{2,0,1:T(8,128)S(1)}, /*index=5*/s32[]{:T(128)}) while((s32[]{:T(128)}, f32[3,17,128]{2,0,1:T(4,128)S(1)}, s32[17,8]{1,0:T(8,128)S(1)}, f32[7,52,128]{2,0,1:T(8,128)S(1)}, f32[7,17,128]{2,0,1:T(8,128)S(1)}, ...), condition=%wide.region_9.10_spmd, body=%wide.region_7.9_spmd.sunk | while | flops 8004682 | bytes 221445 | solution.py:88
  110.6 1.8 %scatter_custom_fusion.3 = f32[3,2048]{0,1:T(8,128)S(1)} fusion(f32[3,2048]{0,1:T(8,128)S(1)} %slice.278, s32[128]{0:T(128)S(1)} %reshape.193, f32[3,16,8]{0,2,1:T(8,128)S(1)} %copy.153, f32[128,3]{1,0:T(8,128)S(1)} %gather_fusion.2, f32[128]{0:T(128)S(1)} %reshape.174, f32[]{:T(128)} %constant.155.clone.1, f32[128]{0:T(128)S(1)} %mul.194, ...), kind=kCustom, calls=%fused_computation.93 | custom fusion | flops 1920 | bytes 157188 | tf_op jit(solution)/shard_map/scatter-add | solution.py:150
  (274 shorter events, 45.6 us)
Async XLA Ops:
  4.3 6.5 %copy-start.13 = (s32[64]{0:T(128)S(1)}, s32[64]{0:T(128)}, u32[]{:S(2)}) copy-start(s32[64]{0:T(128)} %param.30) | copy-start | bytes 772
  4.3 6.5 %copy-start.12 = (f32[64]{0:T(128)S(1)}, f32[64]{0:T(128)}, u32[]{:S(2)}) copy-start(f32[64]{0:T(128)} %param.31) | copy-start | bytes 772
  4.3 6.6 %copy-start.1 = (f32[5,128]{0,1:T(8,128)S(1)}, f32[5,128]{0,1:T(8,128)}, u32[]{:S(2)}) copy-start(f32[5,128]{0,1:T(8,128)} %constant.153.clone.1) | copy-start | bytes 7684
  4.3 14.5 %copy-start.2 = (f32[3,4,8,256]{3,2,1,0:T(8,128)S(1)}, f32[3,4,8,256]{3,2,1,0:T(8,128)}, u32[]{:S(2)}) copy-start(f32[3,4,8,256]{3,2,1,0:T(8,128)} %param.17) | copy-start | bytes 294916
  4.3 14.6 %copy-start.7 = (f32[4,8,256]{2,1,0:T(8,128)S(1)}, f32[4,8,256]{2,1,0:T(8,128)}, u32[]{:S(2)}) copy-start(f32[4,8,256]{2,1,0:T(8,128)} %param.19) | copy-start | bytes 98308
  4.4 21.1 %copy-start.11 = (s32[64,1]{0,1:T(1,128)S(1)}, s32[64,1]{0,1:T(1,128)}, u32[]{:S(2)}) copy-start(s32[64,1]{0,1:T(1,128)} %param.26) | copy-start | bytes 772
  4.4 21.5 %copy-start.8 = (f32[4,8,256]{2,1,0:T(8,128)S(1)}, f32[4,8,256]{2,1,0:T(8,128)}, u32[]{:S(2)}) copy-start(f32[4,8,256]{2,1,0:T(8,128)} %param.20) | copy-start | bytes 98308
  4.4 21.5 %copy-start.3 = (f32[3,2048]{1,0:T(4,128)S(1)}, f32[3,2048]{1,0:T(4,128)}, u32[]{:S(2)}) copy-start(f32[3,2048]{1,0:T(4,128)} %param.23) | copy-start | bytes 73732
  7.9 25.5 %copy-start.9 = (f32[9,64]{1,0:T(8,128)S(1)}, f32[9,64]{1,0:T(8,128)}, u32[]{:S(2)}) copy-start(f32[9,64]{1,0:T(8,128)} %param.25) | copy-start | bytes 6916
  7.9 35.5 %copy-start.10 = (s32[17,8]{0,1:T(8,128)S(1)}, s32[17,8]{0,1:T(8,128)}, u32[]{:S(2)}) copy-start(s32[17,8]{0,1:T(8,128)} %param.27) | copy-start | bytes 1636
  12.6 13.7 %all-to-all-start = ((f32[5,16,8]{2,0,1:T(8,128)}), f32[5,16,8]{2,0,1:T(8,128)S(1)}, u32[]{:S(2)}, u32[]{:S(2)}) async-start(f32[5,16,8]{2,0,1:T(8,128)} %copy.124), calls=%async_computation | async-start | bytes 131072 | tf_op jit(solution)/shard_map/all_to_all | solution.py:145
  19.0 31.6 %collective-permute-start = (f32[4,4,1,256]{3,0,2,1:T(4,128)S(1)}, f32[4,4,1,256]{3,0,2,1:T(4,128)S(1)}, u32[]{:S(2)}, u32[]{:S(2)}) collective-permute-start(f32[4,4,1,256]{3,0,2,1:T(4,128)S(1)} %get-tuple-element.147), channel_id=1, source_target_pairs={{0,1},{1,2},{2,3},{3,4},{4,5},{5,6},{6,7},{7,8},{8,9},{9,10},{10,1... | collective-permute-start | bytes 49160 | tf_op jit(solution)/shard_map/ppermute | solution.py:22
  21.1 29.6 %collective-permute-start.1 = (f32[4,4,1,256]{3,0,2,1:T(4,128)S(1)}, f32[4,4,1,256]{3,0,2,1:T(4,128)S(1)}, u32[]{:S(2)}, u32[]{:S(2)}) collective-permute-start(f32[4,4,1,256]{3,0,2,1:T(4,128)S(1)} %get-tuple-element.148), channel_id=1, source_target_pairs={{1,0},{2,1},{3,2},{4,3},{5,4},{6,5},{7,6},{8,7},{9,8},{10,9},{11,1... | collective-permute-start | bytes 49160 | tf_op jit(solution)/shard_map/ppermute | solution.py:25
  28.2 10.2 %all-to-all-start.1 = ((f32[3,16,8]{2,0,1:T(4,128)}), f32[3,16,8]{2,0,1:T(4,128)S(1)}, u32[]{:S(2)}, u32[]{:S(2)}) async-start(f32[3,16,8]{2,0,1:T(4,128)} %get-tuple-element.153), calls=%async_computation.1 | async-start | bytes 65536 | tf_op jit(solution)/shard_map/all_to_all | solution.py:151
  38.4 11.9 %all-to-all-start.2 = ((f32[10,16,8]{0,2,1:T(8,128)}), f32[10,16,8]{0,2,1:T(8,128)S(1)}, u32[]{:S(2)}, u32[]{:S(2)}) async-start(f32[10,16,8]{0,2,1:T(8,128)} %bitcast.55), calls=%async_computation.2 | async-start | bytes 131072 | tf_op jit(solution)/shard_map/all_to_all | solution.py:126
  47.4 9.1 %copy-start.4 = (f32[3,2048]{1,0:T(4,128)S(1)}, f32[3,2048]{1,0:T(4,128)}, u32[]{:S(2)}) copy-start(f32[3,2048]{1,0:T(4,128)} %param.22) | copy-start | bytes 73732
  47.4 16.2 %copy-start = (f32[24,24]{1,0:T(8,128)S(1)}, f32[24,24]{1,0:T(8,128)}, u32[]{:S(2)}) copy-start(f32[24,24]{1,0:T(8,128)} %param.21) | copy-start | bytes 6916
  50.7 12.6 %collective-permute-start.2 = (f32[4,1,10,256]{3,0,2,1:T(4,128)S(1)}, f32[4,1,10,256]{3,0,2,1:T(4,128)S(1)}, u32[]{:S(2)}, u32[]{:S(2)}) collective-permute-start(f32[4,1,10,256]{3,0,2,1:T(4,128)S(1)} %get-tuple-element.145), channel_id=1, source_target_pairs={{0,16},{1,17},{2,18},{3,19},{4,20},{5,21},{6,22},{7,23},{8,24},{9,... | collective-permute-start | bytes 122888 | tf_op jit(solution)/shard_map/ppermute | solution.py:22
  52.0 11.3 %collective-permute-start.3 = (f32[4,1,10,256]{3,0,2,1:T(4,128)S(1)}, f32[4,1,10,256]{3,0,2,1:T(4,128)S(1)}, u32[]{:S(2)}, u32[]{:S(2)}) collective-permute-start(f32[4,1,10,256]{3,0,2,1:T(4,128)S(1)} %get-tuple-element.146), channel_id=1, source_target_pairs={{16,0},{17,1},{18,2},{19,3},{20,4},{21,5},{22,6},{23,7},{24,8},{25... | collective-permute-start | bytes 122888 | tf_op jit(solution)/shard_map/ppermute | solution.py:25
  56.6 21.1 %collective-permute-start.4 = (f32[7,2176]{1,0:T(8,128)S(1)}, f32[7,2176]{1,0:T(8,128)S(1)}, u32[]{:S(2)}, u32[]{:S(2)}) collective-permute-start(f32[7,2176]{1,0:T(8,128)S(1)} %maximum_maximum_fusion), channel_id=1, source_target_pairs={{0,1},{1,2},{2,3},{3,4},{4,5},{5,6},{6,7},{7,8},{8,9},{9,10},{10,1... | collective-permute-start | bytes 182792 | tf_op jit(solution)/shard_map/ppermute | solution.py:22
  58.5 19.1 %collective-permute-start.5 = (f32[7,2176]{1,0:T(8,128)S(1)}, f32[7,2176]{1,0:T(8,128)S(1)}, u32[]{:S(2)}, u32[]{:S(2)}) collective-permute-start(f32[7,2176]{1,0:T(8,128)S(1)} %maximum_maximum_fusion), channel_id=1, source_target_pairs={{1,0},{2,1},{3,2},{4,3},{5,4},{6,5},{7,6},{8,7},{9,8},{10,9},{11,1... | collective-permute-start | bytes 182792 | tf_op jit(solution)/shard_map/ppermute | solution.py:25
  74.3 2.3 %copy-start.5 = (f32[3,4,8,256]{3,2,1,0:T(8,128)S(1)}, f32[3,4,8,256]{3,2,1,0:T(8,128)}, u32[]{:S(2)}) copy-start(f32[3,4,8,256]{3,2,1,0:T(8,128)} %param.18) | copy-start | bytes 294916
  110.6 2.3 %copy-start.6 = (f32[3,2048]{1,0:T(4,128)S(1)}, f32[3,2048]{1,0:T(4,128)}, u32[]{:S(2)}) copy-start(f32[3,2048]{1,0:T(4,128)} %param.24) | copy-start | bytes 73732
where the time goes:
time: 114 us
  starting transfers between devices  35.4 us (31%)
  local copies, waits for them, and re-layouts  26.8 us (24%)
  matrix products  25.7 us (23%)
  other arithmetic  20 us (18%)
  waiting for transfers between devices  3.64 us (3%)
  between operations  1.19 us (1%)
    ppermute x3, starting transfers between devices, padded_2(): lax.ppermute(lax.slice_in_dim(block, 0, width, axis=dim), axis, backward)  13.7 us
    dot_general x17, matrix products, one_block(): pulled = jnp.einsum('fij,cfj->ci', weight, others[3:6], precision=highest)  12.9 us
    dot_general x8, matrix products, element_forces(): jnp.einsum('ij,jxyz->ixyz', stiffness[:, 3 * corner:3 * corner + 3], shif...  12.8 us
    gather x17, local copies, waits for them, and re-layouts, one_block(): others = jnp.take(ext_blocks, members, axis=1)  9.43 us
    reduce_sum x17, other arithmetic, one_block(): totals = jnp.sum(weight, axis=(0, 2))  6.74 us
    all_to_all x1, starting transfers between devices, shards(): lax.all_to_all(ov_outgoing, 'lat', split_axis=1, concat_axis=1, tiled=True)  6.3 us
    ppermute x3, starting transfers between devices, padded_2(): lax.ppermute(lax.slice_in_dim(block, block.shape[dim] - width, None, axis...  5.27 us
    all_to_all x1, starting transfers between devices, shards(): lax.all_to_all(coupling, 'lat', split_axis=1, concat_axis=1, tiled=True)  5.12 us
  transfers between devices with their start and end apart: 9, of which 1 were waited for; matrix products, arithmetic and copies ran while one was open for 23% of the time, Pallas kernels for 0%

commit v1 on v0

v1 whole, which is shorter than its diff:
```python
import functools
import math

import jax
import jax.numpy as jnp
from jax import lax
from jax.experimental import pallas as pl
from jax.experimental.pallas import tpu as pltpu
from jax.sharding import PartitionSpec as P

BLOCK = 128
CAP = 8
HALF = 0.5
GAIN = 8.0
LOG2E = math.log2(math.e)
F32 = jnp.float32
BF16 = jnp.bfloat16

VMEM = pl.BlockSpec(memory_space=pltpu.VMEM)
SMEM = pl.BlockSpec(memory_space=pltpu.SMEM)


def params():
    return pltpu.CompilerParams(vmem_limit_bytes=40 * 1024 * 1024)


def split3(value):
    high = value.astype(BF16)
    rest = value - high.astype(F32)
    mid = rest.astype(BF16)
    low = (rest - mid.astype(F32)).astype(BF16)
    return high, mid, low


def dot(a, b):
    return jnp.dot(a, b, preferred_element_type=F32)


def dot_nt(a, b):
    return lax.dot_general(a, b, (((1,), (1,)), ((), ())), preferred_element_type=F32)


def dot3(value, hot):
    high, mid, low = split3(value)
    return (dot(high, hot) + dot(mid, hot)) + dot(low, hot)


def dot3_nt(value, hot):
    high, mid, low = split3(value)
    return (dot_nt(high, hot) + dot_nt(mid, hot)) + dot_nt(low, hot)


def iota(shape, axis):
    return lax.broadcasted_iota(jnp.int32, shape, axis)


def one_hot(condition):
    return jnp.where(condition, 1.0, 0.0).astype(BF16)


def shift_of(size):
    assert size & (size - 1) == 0
    return size.bit_length() - 1


def point_rows(pos, disp):
    norm = (-0.5 * LOG2E) * (pos[0:1] * pos[0:1] + pos[1:2] * pos[1:2] + pos[2:3] * pos[2:3])
    return jnp.concatenate([disp, jnp.ones_like(norm), pos, norm], axis=0)


def slots_of(owner_ref):
    owner = owner_ref[...].astype(F32)
    rows = owner.shape[0]
    wide = jnp.broadcast_to(owner, (rows, rows))
    down, across = iota((rows, rows), 0), iota((rows, rows), 1)
    named = jnp.sum(jnp.where(down == across, wide, 0.0), axis=0, keepdims=True)
    earlier = jnp.where((wide == named) & (across < down), 1.0, 0.0)
    rank = jnp.sum(earlier, axis=1, keepdims=True)
    return owner * CAP + rank, named


def pack_kernel(
    peers,
    both_faces,
    info,
    fem_disp,
    modulus,
    pd_disp,
    conv_state,
    conv_owner,
    ov_owner,
    ov_node,
    ov_target,
    ov_stiff,
    chunk,
    faces,
    entries,
    rows_ref,
):
    nx, ny, nz = modulus.shape
    width = peers * CAP
    blocks = pd_disp.shape[1] // BLOCK
    count = ov_node.shape[1]
    for face, number in enumerate((0, nx - 1)):
        if both_faces:
            faces[face, 0:3] = fem_disp[:, number]
            faces[face, 3] = modulus[number]
    if not both_faces:
        upper = info[1] == 0
        faces[0, 0:3] = jnp.where(upper, fem_disp[:, nx - 1], fem_disp[:, 0])
        faces[0, 3] = jnp.where(upper, modulus[nx - 1], modulus[0])
    node = ov_node[...]
    hot_z = one_hot(iota((nz, count), 0) == (node & (nz - 1)))
    picked = dot3(fem_disp[...].reshape(3 * nx * ny, nz), hot_z)
    hot_xy = jnp.where(iota((nx * ny, count), 0) == (node >> shift_of(nz)), 1.0, 0.0)
    at_node = jnp.sum(picked.reshape(3, nx * ny, count) * hot_xy[None], axis=1)
    conv_slot, _ = slots_of(conv_owner)
    ov_slot, ov_named = slots_of(ov_owner)
    lane = iota((conv_slot.shape[0], width), 1).astype(F32)
    state = conv_state[...]
    points = point_rows(state[0:3], state[3:6])
    blank = jnp.zeros((5, state.shape[1]), F32)
    conv_rows = jnp.concatenate([points, state[6:9], blank], axis=0)
    stiff = ov_stiff[...]
    target = ov_target[...].astype(F32)
    ov_rows = jnp.concatenate([jnp.zeros((3, count), F32), at_node, stiff, target], axis=0)
    conv_out = dot3(conv_rows, one_hot(conv_slot == lane))
    ov_out = dot3(ov_rows, one_hot(ov_slot == lane))
    entries[...] = jnp.concatenate(
        [at_node, stiff, ov_named, target, node.astype(F32), jnp.zeros((1, count), F32)], axis=0
    )
    for block in range(blocks):
        for comp in range(3):
            rows_ref[comp * blocks + block : comp * blocks + block + 1] = pd_disp[
                comp : comp + 1, block * BLOCK : (block + 1) * BLOCK
            ]
    base = 3 * blocks
    for tile in range(width // BLOCK):
        part = slice(tile * BLOCK, (tile + 1) * BLOCK)
        rows_ref[base + 16 * tile : base + 16 * tile + 8] = conv_out[0:8, part]
        rows_ref[base + 16 * tile + 8 : base + 16 * tile + 16] = conv_out[8:16, part] + ov_out[:, part]
    value = rows_ref[...]
    for copy in range(chunk.shape[0]):
        chunk[copy] = value


def side_kernel(depth, info, fem_disp, modulus, pd_pos, pd_disp, low_x, high_x, pay_even, pay_odd):
    nx, ny, nz = modulus.shape
    blocks = pd_disp.shape[1] // BLOCK
    points = point_rows(pd_pos[...], pd_disp[...])
    for pair in range(blocks // 2):
        part = points[:, 2 * BLOCK * pair : 2 * BLOCK * (pair + 1)]
        pay_even[8 * pair : 8 * pair + 8] = part
        pay_odd[8 * pair : 8 * pair + 8] = part
    even = (info[0] & 1) == 0
    low_on = jnp.where(info[1] > 0, 1.0, 0.0)
    high_on = jnp.where(info[1] < depth - 1, 1.0, 0.0)
    base = 4 * blocks
    for pay, top in ((pay_even, even), (pay_odd, jnp.logical_not(even))):
        row = jnp.where(top, ny - 1, 0)
        for comp in range(4):
            at = base + comp
            pay[at : at + 1] = low_x[comp, pl.ds(row, 1)] * low_on
            for x in range(nx):
                at = base + 4 * (x + 1) + comp
                pay[at : at + 1] = fem_disp[comp, x, pl.ds(row, 1)] if comp < 3 else modulus[x, pl.ds(row, 1)]
            at = base + 4 * (nx + 1) + comp
            pay[at : at + 1] = high_x[comp, pl.ds(row, 1)] * high_on


def side_table(ref, block):
    return ref[8 * (block // 2) : 8 * (block // 2) + 8, BLOCK * (block % 2) : BLOCK * (block % 2 + 1)]


def own_features(points):
    row = iota(points.shape, 0)
    turned = pltpu.roll(points, 4, 0)
    value = jnp.where(row == 3, turned, jnp.where(row < 3, 0.0, jnp.where(row == 7, 1.0, LOG2E * points)))
    high, mid, low = (part.astype(F32) for part in split3(value))
    return jnp.concatenate([high, mid, high, mid, low, high], axis=0).astype(BF16)


def other_features(points):
    high, mid, low = (part.astype(F32) for part in split3(points))
    left = jnp.concatenate([high, high, mid, mid, high, low], axis=0)
    sums = jnp.concatenate([high, mid, low, jnp.zeros_like(low)], axis=0)
    return left.T.astype(BF16), sums.astype(BF16)


def pair_sums(left, sums, own):
    weight = jnp.exp2(dot(left, own))
    high = weight.astype(BF16)
    low = (weight - high.astype(F32)).astype(BF16)
    return dot(jnp.concatenate([sums, sums], axis=1), jnp.concatenate([high, low], axis=0))


def fold(total):
    return total[0:8] + total[8:16] + total[16:24]


def bond_kernel(tail_blocks, info, family, own, even_side, odd_side, sums_out, pairs, left_ref, sums_ref):
    blocks = sums_out.shape[0]
    table = blocks + tail_blocks
    members = family.shape[1]
    even = (info[0] & 1) == 0
    for block in range(blocks):
        first = side_table(even_side, block)
        second = side_table(odd_side, block)
        three = (jnp.where(even, second, first), side_table(own, block), jnp.where(even, first, second))
        for side, points in enumerate(three):
            left, sums = other_features(points)
            left_ref[side * blocks + block] = left
            sums_ref[side * blocks + block] = sums
    left_ref[3 * blocks] = jnp.zeros(left_ref.shape[1:], BF16)
    sums_ref[3 * blocks] = jnp.zeros(sums_ref.shape[1:], BF16)
    shift = shift_of(64)
    for block in range(blocks, table):
        for k in range(members):
            pairs[1 + (block - blocks) * members + k] = (block << shift) + family[block, k]

    def one(index, found):
        pair = index // 2
        points = own[pl.ds(pl.multiple_of(8 * index, 8), 8), :]
        for part in range(2):
            block = 2 * index + part
            mine = own_features(points[:, BLOCK * part : BLOCK * (part + 1)])
            total = jnp.zeros((32, BLOCK), F32)
            for k in range(members):
                member = family[block, k]
                side = jnp.where(member >= table, 1, 0) + jnp.where(member >= 2 * table, 1, 0)
                local = member - side * table
                outside = local >= blocks
                is_tail = outside & (member < 3 * table)
                pairs[1 + found] = (block << shift) + member
                found = found + jnp.where(is_tail, 1, 0)
                where = jnp.where(outside, 3 * blocks, side * blocks + local)
                total = total + pair_sums(left_ref[where], sums_ref[where], mine)
            sums_out[block] = fold(total)
        return found

    found = lax.fori_loop(0, blocks // 2, one, tail_blocks * members)
    for extra in range(4):
        pairs[1 + found + extra] = 3 * table
    pairs[0] = (found + 3) // 4


def stiffness_rows(stiffness):
    new, old = iota((32, 24), 0), iota((32, 24), 1)
    place = sum(
        jnp.where(old == k, (k // 3 // 2) * 8 + (k // 3 % 2) * 4 + k % 3, 0) for k in range(24)
    )
    hot = one_hot(new == place)
    parts = [dot_nt(dot(hot, part).astype(BF16), hot) for part in split3(stiffness)]
    high, mid, low = parts
    pieces = []
    for corner in range(4):
        part = slice(8 * corner, 8 * corner + 8)
        for piece in (high, high, mid, mid, high, low):
            pieces.append(piece[:, part])
    return jnp.concatenate(pieces, axis=1).astype(BF16)


def rock_kernel(
    depth,
    halo,
    info,
    fem_disp,
    fem_vel,
    modulus,
    inv_mass,
    stiffness,
    low_x,
    high_x,
    even_side,
    odd_side,
    out,
    nodes,
    first_ref,
    second_ref,
    force_ref,
):
    nx, ny, nz = modulus.shape
    wide = ny + 2
    even = (info[0] & 1) == 0
    low_on = jnp.where(info[1] > 0, 1.0, 0.0)
    high_on = jnp.where(info[1] < depth - 1, 1.0, 0.0)
    lane_end = iota((8, nz), 1) == nz - 1

    def ahead(value):
        return jnp.where(lane_end[0 : value.shape[0]], 0.0, pltpu.roll(value, nz - 1, 1))

    halves = [slice(h * BLOCK, (h + 1) * BLOCK) for h in range(nz // BLOCK)]
    for x in range(nx + 2):
        for comp in range(4):
            if x == 0:
                value = low_x[comp] * low_on
            elif x == nx + 1:
                value = high_x[comp] * high_on
            else:
                value = fem_disp[comp, x - 1] if comp < 3 else modulus[x - 1]
            at = (x * wide + 1) * 8 + comp
            shifted = ahead(value)
            for half, part in enumerate(halves):
                nodes[half, pl.ds(at, ny, stride=8), :] = value[:, part]
                nodes[half, pl.ds(at + 4, ny, stride=8), :] = shifted[:, part]
        for y, from_even in ((0, jnp.logical_not(even)), (ny + 1, even)):
            rows = slice(halo + 4 * x, halo + 4 * x + 4)
            value = jnp.where(from_even, even_side[rows], odd_side[rows])
            at = (x * wide + y) * 8
            shifted = ahead(value)
            for half, part in enumerate(halves):
                nodes[half, at : at + 4, :] = value[:, part]
                nodes[half, at + 4 : at + 8, :] = shifted[:, part]

    row8 = iota((8, nz), 0)
    keep = (row8 != 3) & (row8 != 7)

    def node_row(x, y):
        at = (x * wide + y) * 8
        return jnp.concatenate([nodes[h, at : at + 8, :] for h in range(len(halves))], axis=1)

    for x in range(nx + 2):
        for y in range(wide):
            value = jnp.where(keep, node_row(x, y), 0.0)
            high, mid, low = (part.astype(F32) for part in split3(value))
            first_ref[x * wide + y] = jnp.concatenate([high, mid], axis=0).astype(BF16)
            second_ref[x * wide + y] = jnp.concatenate([low, high], axis=0).astype(BF16)
    left = stiffness_rows(stiffness[...])

    def element(x, y):
        pieces = []
        for a in range(2):
            for b in range(2):
                at = (x + a) * wide + y + b
                pieces += [first_ref[at], first_ref[at], second_ref[at]]
        force = dot(left, jnp.concatenate(pieces, axis=0))
        return force * node_row(x, y)[3:4]

    row_keep = iota((8, nz), 1) != 0
    before = None
    for x in range(nx + 1):
        line = [element(x, y) for y in range(ny + 1)]
        if x > 0:
            for y in range(1, ny + 1):
                total = line[y][0:8] + line[y - 1][8:16] + before[y][16:24] + before[y - 1][24:32]
                turned = pltpu.roll(pltpu.roll(total, 4, 0), 1, 1)
                total = total + jnp.where(row_keep, turned, 0.0)
                at = ((x - 1) * ny + y - 1) * 8
                for half, part in enumerate(halves):
                    force_ref[half, at : at + 8, :] = total[:, part]
        before = line
    for x in range(nx):
        for comp in range(3):
            force = jnp.concatenate(
                [force_ref[h, pl.ds(x * ny * 8 + comp, ny, stride=8), :] for h in range(len(halves))], axis=1
            )
            out[comp, x] = fem_vel[comp, x] - HALF * inv_mass[x] * force


def final_kernel(
    peers,
    members,
    info,
    pairs,
    mine_in,
    mate_in,
    entries,
    rock,
    inv_mass,
    sums_in,
    own,
    even_side,
    odd_side,
    pd_vel,
    fem_out,
    pd_out,
    table_ref,
    sums_ref,
):
    nx, ny, nz = inv_mass.shape
    width = peers * CAP
    tail_blocks = width // BLOCK
    blocks = sums_in.shape[0]
    table = blocks + tail_blocks
    base = 3 * blocks
    place = info[0]
    core = place & 1
    even = core == 0
    for block in range(blocks):
        first = side_table(even_side, block)
        second = side_table(odd_side, block)
        table_ref[block] = jnp.where(even, second, first)
        table_ref[table + block] = side_table(own, block)
        table_ref[2 * table + block] = jnp.where(even, first, second)
        sums_ref[block] = sums_in[block]
    table_ref[3 * table] = jnp.zeros((8, BLOCK), F32)
    for block in range(blocks, table):
        sums_ref[block] = jnp.zeros((8, BLOCK), F32)

    def slot_rows(ref, k):
        tiles = [ref[k, base + 16 * tile : base + 16 * tile + 16, :] for tile in range(tail_blocks)]
        return tiles[0] if tail_blocks == 1 else jnp.concatenate(tiles, axis=1)

    lane = iota((16, width), 1)
    back = lax.rem(width - CAP * (place - 1) + width, width)
    tails = [jnp.zeros((16, width), F32) for _ in range(3)]
    for ref, odd in ((mine_in, core), (mate_in, 1 - core)):
        gathered = [jnp.zeros((16, width), F32) for _ in range(3)]
        for k in range(peers // 2):
            turned = pltpu.roll(slot_rows(ref, k), back, 1)
            for side in range(3):
                window = jnp.where((lane >= CAP * side) & (lane < CAP * side + CAP), turned, 0.0)
                amount = (2 * CAP * k - CAP * side) % width
                gathered[side] = gathered[side] + (pltpu.roll(window, amount, 1) if amount else window)
        for side in range(3):
            tails[side] = tails[side] + pltpu.roll(gathered[side], CAP * odd, 1)
    on = (jnp.where(place > 0, 1.0, 0.0), 1.0, jnp.where(place < peers - 1, 1.0, 0.0))
    for side in range(3):
        for tile in range(tail_blocks):
            part = tails[side][0:8, tile * BLOCK : (tile + 1) * BLOCK]
            table_ref[side * table + blocks + tile] = part * on[side]
    tail_rows = tails[1]

    shift = shift_of(64)

    def some(index, carry):
        results = []
        for lane_of in range(4):
            code = pairs[1 + 4 * index + lane_of]
            block = code >> shift
            left, sums = other_features(table_ref[code & 63])
            results.append((block, fold(pair_sums(left, sums, own_features(table_ref[table + block])))))
        for block, total in results:
            sums_ref[block] = sums_ref[block] + total
        return carry

    lax.fori_loop(0, pairs[0], some, 0)

    stiff = tail_rows[14:15]
    target = tail_rows[15:16].astype(jnp.int32)
    hot_lane = one_hot(iota((BLOCK, width), 0) == (target & (BLOCK - 1)))
    target_block = target >> shift_of(BLOCK)
    tables = jnp.concatenate([table_ref[table + block] for block in range(blocks)], axis=0)
    looked = dot3(tables, hot_lane)
    found = jnp.zeros((8, width), F32)
    for block in range(blocks):
        found = found + jnp.where(target_block == block, looked[8 * block : 8 * block + 8], 0.0)
    coupling = stiff * (tail_rows[11:14] - found[0:3])
    coupling = jnp.concatenate([coupling, jnp.zeros((5, width), F32)], axis=0)
    spread = jnp.concatenate([jnp.where(target_block == block, coupling, 0.0) for block in range(blocks)], axis=0)
    couple = dot3_nt(spread, hot_lane)

    scale = GAIN / (BLOCK * members)
    for block in range(table):
        total = sums_ref[block]
        points = table_ref[table + block]
        part = slice(block * BLOCK, (block + 1) * BLOCK)
        force = scale * points[3:4] * (total[0:3] - points[0:3] * total[3:4])
        if block < blocks:
            pd_out[:, part] = pd_vel[:, part] + HALF * (force + couple[8 * block : 8 * block + 3])
        else:
            tile = block - blocks
            pd_out[:, part] = tail_rows[8:11, tile * BLOCK : (tile + 1) * BLOCK] + HALF * force

    entry = entries[...]
    count = entry.shape[1]
    owner = entry[4:5].astype(jnp.int32)
    goal = entry[5:6].astype(jnp.int32)
    node = entry[6:7].astype(jnp.int32)
    pick = one_hot(iota((BLOCK, count), 0) == (goal & (BLOCK - 1)))
    goal_row = (owner >> 1) * blocks + (goal >> shift_of(BLOCK))
    from_mine = (owner & 1) == core
    rows = peers // 2 * blocks
    hit = iota((rows, count), 0) == goal_row
    values = []
    for comp in range(3):
        part = slice(comp * blocks, (comp + 1) * blocks)
        value = jnp.zeros((1, count), F32)
        for ref, wanted in ((mine_in, from_mine), (mate_in, jnp.logical_not(from_mine))):
            got = dot3(ref[:, part, :].reshape(rows, BLOCK), pick)
            value = value + jnp.sum(jnp.where(hit & wanted, got, 0.0), axis=0, keepdims=True)
        values.append(value)
    z_hot = one_hot(iota((nz, count), 0) == (node & (nz - 1)))
    xy_hit = iota((nx * ny, count), 0) == (node >> shift_of(nz))
    spread = jnp.concatenate(
        [jnp.where(xy_hit, entry[3:4] * (entry[c : c + 1] - values[c]), 0.0) for c in range(3)], axis=0
    )
    pull = dot3_nt(spread, z_hot).reshape(3, nx, ny, nz)
    fem_out[...] = rock[...] - HALF * inv_mass[...][None] * pull


def call(kernel, outs, specs, scratch, flops, nbytes, args, name, out_specs=None):
    return pl.pallas_call(
        kernel,
        out_shape=outs,
        in_specs=specs,
        out_specs=out_specs or jax.tree.map(lambda _: VMEM, outs),
        scratch_shapes=scratch,
        compiler_params=params(),
        cost_estimate=pl.CostEstimate(flops=flops, bytes_accessed=nbytes, transcendentals=0),
        name=name,
    )(*args)


def shards(
    fem_disp,
    fem_vel,
    modulus,
    inv_mass,
    element_stiffness,
    pd_pos,
    pd_disp,
    pd_vel,
    conv_state,
    conv_owner,
    family,
    ov_owner,
    ov_node,
    ov_target,
    ov_stiff,
):
    peers = lax.axis_size("lat")
    depth = lax.axis_size("depth")
    nx, ny, nz = modulus.shape
    blocks = pd_pos.shape[1] // BLOCK
    tail_blocks = peers * CAP // BLOCK
    table = blocks + tail_blocks
    members = family.shape[1]
    count = ov_node.shape[0]
    chips = peers // 2
    chunk_rows = 3 * blocks + 16 * tail_blocks
    shaped = jax.ShapeDtypeStruct
    info = jnp.stack([lax.axis_index("lat"), lax.axis_index("depth")]).astype(jnp.int32)

    both_faces = depth > 2
    chunk, faces, entries = call(
        functools.partial(pack_kernel, peers, both_faces),
        (
            shaped((chips, chunk_rows, BLOCK), F32),
            shaped((2 if both_faces else 1, 4, ny, nz), F32),
            shaped((8, count), F32),
        ),
        [SMEM] + [VMEM] * 9,
        [pltpu.VMEM((chunk_rows, BLOCK), F32)],
        4_000_000,
        400_000,
        (
            info,
            fem_disp,
            modulus,
            pd_disp,
            conv_state,
            conv_owner,
            ov_owner,
            ov_node.reshape(1, -1),
            ov_target.reshape(1, -1),
            ov_stiff.reshape(1, -1),
        ),
        "pack",
    )
    if both_faces:
        low_x = lax.ppermute(faces[1], "depth", [(i, i + 1) for i in range(depth - 1)])
        high_x = lax.ppermute(faces[0], "depth", [(i + 1, i) for i in range(depth - 1)])
    else:
        low_x = high_x = lax.ppermute(faces[0], "depth", [(0, 1), (1, 0)])
    groups = [[side + 2 * k for k in range(chips)] for side in range(2)]
    mine = lax.all_to_all(chunk, "lat", split_axis=0, concat_axis=0, tiled=True, axis_index_groups=groups)

    halo = 4 * blocks
    pay_rows = halo + 4 * (nx + 2)
    pay_even, pay_odd = call(
        functools.partial(side_kernel, depth),
        (shaped((pay_rows, nz), F32),) * 2,
        [SMEM] + [VMEM] * 6,
        [],
        1_000_000,
        400_000,
        (info, fem_disp, modulus, pd_pos, pd_disp, low_x, high_x),
        "side",
    )
    swap = [(i, i ^ 1) for i in range(peers)]
    cross = [(i, i + 1) for i in range(1, peers - 1, 2)] + [(i + 1, i) for i in range(1, peers - 1, 2)]
    odd_side = lax.ppermute(pay_odd, "lat", cross)
    even_side = lax.ppermute(pay_even, "lat", swap)

    sums, pairs = call(
        functools.partial(bond_kernel, tail_blocks),
        (shaped((blocks, 8, BLOCK), F32), shaped((table * members + 8,), jnp.int32)),
        [SMEM, SMEM] + [VMEM] * 3,
        [pltpu.VMEM((3 * blocks + 1, BLOCK, 48), BF16), pltpu.VMEM((3 * blocks + 1, 32, BLOCK), BF16)],
        200_000_000,
        10_000_000,
        (info, family, pay_even, even_side, odd_side),
        "bond",
        out_specs=(VMEM, SMEM),
    )
    mine, sums = lax.optimization_barrier((mine, sums))
    mate = lax.ppermute(mine, "lat", swap)
    rock = call(
        functools.partial(rock_kernel, depth, halo),
        shaped(fem_vel.shape, F32),
        [SMEM] + [VMEM] * 9,
        [
            pltpu.VMEM((nz // BLOCK, (nx + 2) * (ny + 2) * 8, BLOCK), F32),
            pltpu.VMEM(((nx + 2) * (ny + 2), 16, nz), BF16),
            pltpu.VMEM(((nx + 2) * (ny + 2), 16, nz), BF16),
            pltpu.VMEM((nz // BLOCK, nx * ny * 8, BLOCK), F32),
        ],
        100_000_000,
        5_000_000,
        (info, fem_disp, fem_vel, modulus, inv_mass, element_stiffness, low_x, high_x, even_side, odd_side),
        "rock",
    )
    return call(
        functools.partial(final_kernel, peers, members),
        (shaped(fem_vel.shape, F32), shaped((3, table * BLOCK), F32)),
        [SMEM, SMEM] + [VMEM] * 10,
        [pltpu.VMEM((3 * table + 1, 8, BLOCK), F32), pltpu.VMEM((table, 8, BLOCK), F32)],
        20_000_000,
        2_000_000,
        (info, pairs, mine, mate, entries, rock, inv_mass, sums, pay_even, even_side, odd_side, pd_vel),
        "final",
    )


def solution(mesh):
    lat = P(None, ("depth", "lat"))
    rows = P(("depth", "lat"), None)
    flat = P(("depth", "lat"))
    nodes = P(None, "depth", "lat", None)
    grid = P("depth", "lat", None)
    return jax.shard_map(
        shards,
        mesh=mesh,
        in_specs=(nodes, nodes, grid, grid, P(), lat, lat, lat, lat, rows, rows, rows, flat, flat, flat),
        out_specs=(nodes, lat),
        check_vma=False,
    )
```

time: 114 us -> 39.7 us (0.35)
  the two profiles are of different devices: /device:TPU:10 before, /device:TPU:0 now
where the time goes in v1:
time: 39.7 us; the launch traced here: 38.9 us
  Pallas kernels  17.8 us (45%)
  starting transfers between devices  14.5 us (37%)
  waiting for transfers between devices  3.26 us (8%)
  local copies, waits for them, and re-layouts  2.53 us (6%)
  between operations  0.74 us (2%)
    pallas_call x5, Pallas kernels, call(): pl.pallas_call(kernel, out_shape=outs, in_specs=specs, out_specs=out_spec...  17.8 us
    all_to_all x1, starting transfers between devices, shards(): lax.all_to_all(chunk, 'lat', split_axis=0, concat_axis=0, tiled=True, axi...  7.41 us
    ppermute x1, starting transfers between devices, shards(): even_side = lax.ppermute(pay_even, 'lat', swap)  3.44 us
    unnamed x35, local copies, waits for them, and re-layouts  2.53 us
    ppermute x1, waiting for transfers between devices, shards(): low_x = high_x = lax.ppermute(faces[0], 'depth', [(0, 1), (1, 0)])  2.42 us
    ppermute x1, starting transfers between devices, shards(): low_x = high_x = lax.ppermute(faces[0], 'depth', [(0, 1), (1, 0)])  1.49 us
    ppermute x1, starting transfers between devices, shards(): mate = lax.ppermute(mine, 'lat', swap)  1.49 us
    ppermute x1, waiting for transfers between devices, shards(): even_side = lax.ppermute(pay_even, 'lat', swap)  0.83 us
  transfers between devices with their start and end apart: 5, of which 2 were waited for; matrix products, arithmetic and copies ran while one was open for 0% of the time, Pallas kernels for 30%

profile of v1, /device:TPU:0, one launch (start us, length us, event | category | flops | bytes accessed | tf_op | source)
XLA Modules:
  0.0 38.9 jit_solution(3799465472798626618)
XLA Ops:
  0.7 0.6 %copy-done.14 = s32[64,1]{0,1:T(1,128)S(1)} copy-done((s32[64,1]{0,1:T(1,128)S(1)}, s32[64,1]{0,1:T(1,128)}, u32[]{:S(2)}) %copy-start.14) | copy-done | bytes 280
  1.3 0.1 copy.17.conv_owner
  1.4 0.1 copy.18.ov_owner
  1.5 0.1 pad_add_fusion.info
  1.6 0.5 %copy-done.2 = f32[4,8,256]{2,1,0:T(8,128)S(1)} copy-done((f32[4,8,256]{2,1,0:T(8,128)S(1)}, f32[4,8,256]{2,1,0:T(8,128)}, u32[]{:S(2)}) %copy-start.2) | copy-done | bytes 32792
  2.1 0.0 copy-done.4
  2.1 0.1 copy-done.9
  2.2 0.0 copy-done.10
  2.2 0.0 copy-done.11
  2.2 0.0 copy-done.12
  2.3 0.9 %copy-done = f32[3,4,8,256]{3,2,1,0:T(8,128)S(1)} copy-done((f32[3,4,8,256]{3,2,1,0:T(8,128)S(1)}, f32[3,4,8,256]{3,2,1,0:T(8,128)}, u32[]{:S(2)}) %copy-start) | copy-done | bytes 98328
  3.2 1.7 %pack.1 = (f32[8,64,128]{2,1,0:T(8,128)}, f32[1,4,8,256]{3,2,1,0:T(8,128)S(1)}, f32[8,64]{1,0:T(8,128)S(1)}) custom-call(s32[2]{0:T(128)S(1)} %pad_add_fusion.info, f32[3,4,8,256]{3,2,1,0:T(8,128)S(1)} %copy-done, f32[4,8,256]{2,1,0:T(8,128)S(1)} %copy-done.2, f32[3,2048]{1,0:T(4,128)S(1)} %copy-done.4, f32[9,64]{1,0:T(8,128)S(1)} %copy-done.9, ...), custom_call_target="tpu_custom_call" | custom-call | flops 4000000 | bytes 400000 | tf_op jit(solution)/shard_map/pack/pallas_call | solution.py:493
  4.8 7.4 %all-to-all-start = ((f32[8,64,128]{2,1,0:T(8,128)}), f32[8,64,128]{2,1,0:T(8,128)S(1)}, u32[]{:S(2)}, u32[]{:S(2)}) async-start(f32[8,64,128]{2,1,0:T(8,128)} %get-tuple-element.15), calls=%async_computation | async-start | bytes 524288 | tf_op jit(solution)/shard_map/all_to_all | solution.py:567
  12.2 1.5 %collective-permute-start = (f32[4,8,256]{2,1,0:T(8,128)S(1)}, f32[4,8,256]{2,1,0:T(8,128)S(1)}, u32[]{:S(2)}, u32[]{:S(2)}) collective-permute-start(f32[4,8,256]{2,1,0:T(8,128)S(1)} %bitcast.9), channel_id=1, source_target_pairs={{0,16},{16,0},{1,17},{17,1},{2,18},{18,2},{3,19},{19,3},{4,20},{20... | collective-permute-start | bytes 98312 | tf_op jit(solution)/shard_map/ppermute | solution.py:565
  13.7 2.4 %collective-permute-done.low_x.high_x = f32[4,8,256]{2,1,0:T(8,128)S(1)} collective-permute-done((f32[4,8,256]{2,1,0:T(8,128)S(1)}, f32[4,8,256]{2,1,0:T(8,128)S(1)}, u32[]{:S(2)}, u32[]{:S(2)}) %collective-permute-start) | collective-permute-done | bytes 32800 | tf_op jit(solution)/shard_map/ppermute | solution.py:565
  16.2 0.6 %side.1 = (f32[88,256]{1,0:T(8,128)S(1)}, f32[88,256]{1,0:T(8,128)S(1)}) custom-call(s32[2]{0:T(128)S(1)} %pad_add_fusion.info, f32[3,4,8,256]{3,2,1,0:T(8,128)S(1)} %copy-done.1, f32[4,8,256]{2,1,0:T(8,128)S(1)} %copy-done.2, f32[3,2048]{1,0:T(4,128)S(1)} %copy-done.7, f32[3,2048]{1,0:T(4,128)S(1)} %copy-done.4, ...), custom_call_target="tpu_custom_call" | custom-call | flops 1000000 | bytes 400000 | tf_op jit(solution)/shard_map/side/pallas_call | solution.py:493
  16.8 0.7 %collective-permute-start.2 = (f32[88,256]{1,0:T(8,128)S(1)}, f32[88,256]{1,0:T(8,128)S(1)}, u32[]{:S(2)}, u32[]{:S(2)}) collective-permute-start(f32[88,256]{1,0:T(8,128)S(1)} %get-tuple-element.13), channel_id=1, source_target_pairs={{1,2},{3,4},{5,6},{7,8},{9,10},{11,12},{13,14},{2,1},{4,3},{6,5},{... | collective-permute-start | bytes 270344 | tf_op jit(solution)/shard_map/ppermute | solution.py:583
  17.4 3.4 %collective-permute-start.1 = (f32[88,256]{1,0:T(8,128)S(1)}, f32[88,256]{1,0:T(8,128)S(1)}, u32[]{:S(2)}, u32[]{:S(2)}) collective-permute-start(f32[88,256]{1,0:T(8,128)S(1)} %get-tuple-element.12.own), channel_id=1, source_target_pairs={{0,1},{1,0},{2,3},{3,2},{4,5},{5,4},{6,7},{7,6},{8,9},{9,8},{10,11... | collective-permute-start | bytes 270344 | tf_op jit(solution)/shard_map/ppermute | solution.py:584
  20.9 0.1 copy.19.family
  21.0 0.8 %collective-permute-done.1.even_side = f32[88,256]{1,0:T(8,128)S(1)} collective-permute-done((f32[88,256]{1,0:T(8,128)S(1)}, f32[88,256]{1,0:T(8,128)S(1)}, u32[]{:S(2)}, u32[]{:S(2)}) %collective-permute-start.1) | collective-permute-done | bytes 90144 | tf_op jit(solution)/shard_map/ppermute | solution.py:584
  21.8 9.2 %bond.1 = (f32[16,8,128]{2,1,0:T(8,128)S(1)}, s32[144]{0:T(256)S(1)}) custom-call(s32[2]{0:T(128)S(1)} %pad_add_fusion.info, s32[17,8]{1,0:T(8,128)S(1)} %copy.19.family, f32[88,256]{1,0:T(8,128)S(1)} %get-tuple-element.12.own, f32[88,256]{1,0:T(8,128)S(1)} %collective-permute-done.1.even_side, f32[88,256]{1,0:T(8,128)S(1)} %collective-permute-done.2.odd_side), custom_call_target="tpu_custom_call" | custom-call | flops 200000000 | bytes 10000000 | tf_op jit(solution)/shard_map/bond/pallas_call | solution.py:493
  31.1 1.5 %collective-permute-start.3 = (f32[8,64,128]{2,1,0:T(8,128)S(1)}, f32[8,64,128]{2,1,0:T(8,128)S(1)}, u32[]{:S(2)}, u32[]{:S(2)}) collective-permute-start(f32[8,64,128]{2,1,0:T(8,128)S(1)} %all-to-all-done.mine_in), channel_id=1, source_target_pairs={{0,1},{1,0},{2,3},{3,2},{4,5},{5,4},{6,7},{7,6},{8,9},{9,8},{10,11... | collective-permute-start | bytes 786440 | tf_op jit(solution)/shard_map/ppermute | solution.py:598
  32.6 2.0 %rock.1 = f32[3,4,8,256]{3,2,1,0:T(8,128)S(1)} custom-call(s32[2]{0:T(128)S(1)} %pad_add_fusion.info, f32[3,4,8,256]{3,2,1,0:T(8,128)S(1)} %copy-done.1, f32[3,4,8,256]{3,2,1,0:T(8,128)S(1)} %copy-done.5, f32[4,8,256]{2,1,0:T(8,128)S(1)} %copy-done.2, f32[4,8,256]{2,1,0:T(8,128)S(1)} %copy-done.3, f32[24,24]{1,0:T(8,128)S(1)} %copy-done.8, ...), custom_call_target="tpu_custom_call" | custom-call | flops 100000000 | bytes 5000000 | tf_op jit(solution)/shard_map/rock/pallas_call | solution.py:493
  34.6 4.3 %final.1 = (f32[3,4,8,256]{3,2,1,0:T(8,128)}, f32[3,2176]{1,0:T(4,128)}) custom-call(s32[2]{0:T(128)S(1)} %pad_add_fusion.info, s32[144]{0:T(256)S(1)} %get-tuple-element.14.pairs, f32[8,64,128]{2,1,0:T(8,128)S(1)} %all-to-all-done.mine_in, f32[8,64,128]{2,1,0:T(8,128)S(1)} %collective-permute-done.3.mate_in, f32[8,64]{1,0:T(8,128)S(1)} %get-tuple-element.18.entries, ...), custom_call_target="tpu_custom_call" | custom-call | flops 20000000 | bytes 2000000 | tf_op jit(solution)/shard_map/final/pallas_call | solution.py:493
  (27 shorter events, 0.1 us)
Async XLA Ops:
  0.6 0.7 %copy-start.14 = (s32[64,1]{0,1:T(1,128)S(1)}, s32[64,1]{0,1:T(1,128)}, u32[]{:S(2)}) copy-start(s32[64,1]{0,1:T(1,128)} %param.24) | copy-start | bytes 772
  0.6 0.7 %copy-start.15 = (s32[64,1]{0,1:T(1,128)S(1)}, s32[64,1]{0,1:T(1,128)}, u32[]{:S(2)}) copy-start(s32[64,1]{0,1:T(1,128)} %param.26) | copy-start | bytes 772
  1.3 0.8 %copy-start.2 = (f32[4,8,256]{2,1,0:T(8,128)S(1)}, f32[4,8,256]{2,1,0:T(8,128)}, u32[]{:S(2)}) copy-start(f32[4,8,256]{2,1,0:T(8,128)} %modulus.5) | copy-start | bytes 98308
  1.3 0.8 %copy-start.4 = (f32[3,2048]{1,0:T(4,128)S(1)}, f32[3,2048]{1,0:T(4,128)}, u32[]{:S(2)}) copy-start(f32[3,2048]{1,0:T(4,128)} %pd_disp.3) | copy-start | bytes 73732
  1.5 0.7 %copy-start.9 = (f32[9,64]{1,0:T(8,128)S(1)}, f32[9,64]{1,0:T(8,128)}, u32[]{:S(2)}) copy-start(f32[9,64]{1,0:T(8,128)} %conv_state.1) | copy-start | bytes 6916
  1.6 0.7 %copy-start.10 = (s32[64]{0:T(128)S(1)}, s32[64]{0:T(128)}, u32[]{:S(2)}) copy-start(s32[64]{0:T(128)} %param.27) | copy-start | bytes 772
  1.6 0.7 %copy-start.11 = (s32[64]{0:T(128)S(1)}, s32[64]{0:T(128)}, u32[]{:S(2)}) copy-start(s32[64]{0:T(128)} %param.28) | copy-start | bytes 772
  1.6 0.7 %copy-start.12 = (f32[64]{0:T(128)S(1)}, f32[64]{0:T(128)}, u32[]{:S(2)}) copy-start(f32[64]{0:T(128)} %param.29) | copy-start | bytes 772
  2.3 0.9 %copy-start = (f32[3,4,8,256]{3,2,1,0:T(8,128)S(1)}, f32[3,4,8,256]{3,2,1,0:T(8,128)}, u32[]{:S(2)}) copy-start(f32[3,4,8,256]{3,2,1,0:T(8,128)} %fem_disp.5) | copy-start | bytes 294916
  4.8 11.3 %copy-start.1 = (f32[3,4,8,256]{3,2,1,0:T(8,128)S(1)}, f32[3,4,8,256]{3,2,1,0:T(8,128)}, u32[]{:S(2)}) copy-start(f32[3,4,8,256]{3,2,1,0:T(8,128)} %fem_disp.5) | copy-start | bytes 294916
  4.8 11.3 %copy-start.7 = (f32[3,2048]{1,0:T(4,128)S(1)}, f32[3,2048]{1,0:T(4,128)}, u32[]{:S(2)}) copy-start(f32[3,2048]{1,0:T(4,128)} %pd_pos.1) | copy-start | bytes 73732
  4.8 26.2 %all-to-all-start = ((f32[8,64,128]{2,1,0:T(8,128)}), f32[8,64,128]{2,1,0:T(8,128)S(1)}, u32[]{:S(2)}, u32[]{:S(2)}) async-start(f32[8,64,128]{2,1,0:T(8,128)} %get-tuple-element.15), calls=%async_computation | async-start | bytes 524288 | tf_op jit(solution)/shard_map/all_to_all | solution.py:567
  12.2 3.9 %collective-permute-start = (f32[4,8,256]{2,1,0:T(8,128)S(1)}, f32[4,8,256]{2,1,0:T(8,128)S(1)}, u32[]{:S(2)}, u32[]{:S(2)}) collective-permute-start(f32[4,8,256]{2,1,0:T(8,128)S(1)} %bitcast.9), channel_id=1, source_target_pairs={{0,16},{16,0},{1,17},{17,1},{2,18},{18,2},{3,19},{19,3},{4,20},{20... | collective-permute-start | bytes 98312 | tf_op jit(solution)/shard_map/ppermute | solution.py:565
  16.2 4.7 %copy-start.13 = (s32[17,8]{0,1:T(8,128)S(1)}, s32[17,8]{0,1:T(8,128)}, u32[]{:S(2)}) copy-start(s32[17,8]{0,1:T(8,128)} %param.25) | copy-start | bytes 1636
  16.8 4.2 %collective-permute-start.2 = (f32[88,256]{1,0:T(8,128)S(1)}, f32[88,256]{1,0:T(8,128)S(1)}, u32[]{:S(2)}, u32[]{:S(2)}) collective-permute-start(f32[88,256]{1,0:T(8,128)S(1)} %get-tuple-element.13), channel_id=1, source_target_pairs={{1,2},{3,4},{5,6},{7,8},{9,10},{11,12},{13,14},{2,1},{4,3},{6,5},{... | collective-permute-start | bytes 270344 | tf_op jit(solution)/shard_map/ppermute | solution.py:583
  17.4 4.4 %collective-permute-start.1 = (f32[88,256]{1,0:T(8,128)S(1)}, f32[88,256]{1,0:T(8,128)S(1)}, u32[]{:S(2)}, u32[]{:S(2)}) collective-permute-start(f32[88,256]{1,0:T(8,128)S(1)} %get-tuple-element.12.own), channel_id=1, source_target_pairs={{0,1},{1,0},{2,3},{3,2},{4,5},{5,4},{6,7},{7,6},{8,9},{9,8},{10,11... | collective-permute-start | bytes 270344 | tf_op jit(solution)/shard_map/ppermute | solution.py:584
  21.0 11.6 %copy-start.3 = (f32[4,8,256]{2,1,0:T(8,128)S(1)}, f32[4,8,256]{2,1,0:T(8,128)}, u32[]{:S(2)}) copy-start(f32[4,8,256]{2,1,0:T(8,128)} %inv_mass.3) | copy-start | bytes 98308
  21.0 11.6 %copy-start.5 = (f32[3,4,8,256]{3,2,1,0:T(8,128)S(1)}, f32[3,4,8,256]{3,2,1,0:T(8,128)}, u32[]{:S(2)}) copy-start(f32[3,4,8,256]{3,2,1,0:T(8,128)} %fem_vel.1) | copy-start | bytes 294916
  21.0 11.6 %copy-start.8 = (f32[24,24]{1,0:T(8,128)S(1)}, f32[24,24]{1,0:T(8,128)}, u32[]{:S(2)}) copy-start(f32[24,24]{1,0:T(8,128)} %stiffness.1) | copy-start | bytes 6916
  31.1 3.5 %copy-start.6 = (f32[3,2048]{1,0:T(4,128)S(1)}, f32[3,2048]{1,0:T(4,128)}, u32[]{:S(2)}) copy-start(f32[3,2048]{1,0:T(4,128)} %pd_vel.1) | copy-start | bytes 73732
  31.1 3.5 %collective-permute-start.3 = (f32[8,64,128]{2,1,0:T(8,128)S(1)}, f32[8,64,128]{2,1,0:T(8,128)S(1)}, u32[]{:S(2)}, u32[]{:S(2)}) collective-permute-start(f32[8,64,128]{2,1,0:T(8,128)S(1)} %all-to-all-done.mine_in), channel_id=1, source_target_pairs={{0,1},{1,0},{2,3},{3,2},{4,5},{5,4},{6,7},{7,6},{8,9},{9,8},{10,11... | collective-permute-start | bytes 786440 | tf_op jit(solution)/shard_map/ppermute | solution.py:598

commit v2 on v1

v2 whole, which is shorter than its diff:
```python
import functools
import math

import jax
import jax.numpy as jnp
from jax import lax
from jax.experimental import pallas as pl
from jax.experimental.pallas import tpu as pltpu
from jax.sharding import PartitionSpec as P

BLOCK = 128
CAP = 8
HALF = 0.5
GAIN = 8.0
LOG2E = math.log2(math.e)
F32 = jnp.float32
BF16 = jnp.bfloat16
LAG = 8
BATCH = 8
PAIR_SHIFT = 6
SIDE_VMEM = 63

VMEM = pl.BlockSpec(memory_space=pltpu.VMEM)
SMEM = pl.BlockSpec(memory_space=pltpu.SMEM)
FAR = pl.BlockSpec(memory_space=pltpu.HBM)
ANY = pl.BlockSpec(memory_space=pl.ANY)


def params(mebibytes):
    return pltpu.CompilerParams(vmem_limit_bytes=int(mebibytes * 1024 * 1024))


def split3(value):
    high = value.astype(BF16)
    rest = value - high.astype(F32)
    mid = rest.astype(BF16)
    low = (rest - mid.astype(F32)).astype(BF16)
    return high, mid, low


def dot(a, b):
    return jnp.dot(a, b, preferred_element_type=F32)


def dot_nt(a, b):
    return lax.dot_general(a, b, (((1,), (1,)), ((), ())), preferred_element_type=F32)


def dot3(value, hot):
    high, mid, low = split3(value)
    return (dot(high, hot) + dot(mid, hot)) + dot(low, hot)


def dot3_nt(value, hot):
    high, mid, low = split3(value)
    return (dot_nt(high, hot) + dot_nt(mid, hot)) + dot_nt(low, hot)


def iota(shape, axis):
    return lax.broadcasted_iota(jnp.int32, shape, axis)


def one_hot(condition):
    return jnp.where(condition, 1.0, 0.0).astype(BF16)


def shift_of(size):
    assert size & (size - 1) == 0
    return size.bit_length() - 1


def point_rows(pos, disp):
    norm = (-0.5 * LOG2E) * (pos[0:1] * pos[0:1] + pos[1:2] * pos[1:2] + pos[2:3] * pos[2:3])
    return jnp.concatenate([disp, jnp.ones_like(norm), pos, norm], axis=0)


def slots_of(owner_ref):
    named = owner_ref[...].astype(F32)
    rows = named.shape[1]
    wide = jnp.broadcast_to(named, (rows, rows))
    down, across = iota((rows, rows), 0), iota((rows, rows), 1)
    owner = jnp.sum(jnp.where(down == across, wide, 0.0), axis=1, keepdims=True)
    earlier = jnp.where((wide == owner) & (across < down), 1.0, 0.0)
    rank = jnp.sum(earlier, axis=1, keepdims=True)
    return owner * CAP + rank, named


def fetch(sources, places, sems):
    copies = [pltpu.make_async_copy(f, t, sems.at[i]) for i, (f, t) in enumerate(zip(sources, places))]
    for copy in copies:
        copy.start()
    for copy in copies:
        copy.wait()


def pack_kernel(
    peers,
    fem_disp,
    pd_disp,
    conv_state,
    conv_owner,
    ov_owner,
    ov_node,
    ov_target,
    ov_stiff,
    chunk,
    entries,
    rows_ref,
):
    _, nx, ny, nz = fem_disp.shape
    width = peers * CAP
    blocks = pd_disp.shape[1] // BLOCK
    count = ov_node.shape[1]
    node = ov_node[...]
    hot_z = one_hot(iota((nz, count), 0) == (node & (nz - 1)))
    picked = dot3(fem_disp[...].reshape(3 * nx * ny, nz), hot_z)
    hot_xy = jnp.where(iota((nx * ny, count), 0) == (node >> shift_of(nz)), 1.0, 0.0)
    at_node = jnp.sum(picked.reshape(3, nx * ny, count) * hot_xy[None], axis=1)
    conv_slot, _ = slots_of(conv_owner)
    ov_slot, ov_named = slots_of(ov_owner)
    lane = iota((conv_slot.shape[0], width), 1).astype(F32)
    state = conv_state[...]
    points = point_rows(state[0:3], state[3:6])
    blank = jnp.zeros((5, state.shape[1]), F32)
    conv_rows = jnp.concatenate([points, state[6:9], blank], axis=0)
    stiff = ov_stiff[...]
    target = ov_target[...].astype(F32)
    ov_rows = jnp.concatenate([jnp.zeros((3, count), F32), at_node, stiff, target], axis=0)
    conv_out = dot3(conv_rows, one_hot(conv_slot == lane))
    ov_out = dot3(ov_rows, one_hot(ov_slot == lane))
    entries[...] = jnp.concatenate(
        [at_node, stiff, ov_named, target, node.astype(F32), jnp.zeros((1, count), F32)], axis=0
    )
    for block in range(blocks):
        for comp in range(3):
            rows_ref[comp * blocks + block : comp * blocks + block + 1] = pd_disp[
                comp : comp + 1, block * BLOCK : (block + 1) * BLOCK
            ]
    base = 3 * blocks
    for tile in range(width // BLOCK):
        part = slice(tile * BLOCK, (tile + 1) * BLOCK)
        rows_ref[base + 16 * tile : base + 16 * tile + 8] = conv_out[0:8, part]
        rows_ref[base + 16 * tile + 8 : base + 16 * tile + 16] = conv_out[8:16, part] + ov_out[:, part]
    value = rows_ref[...]
    for copy in range(chunk.shape[0]):
        chunk[copy] = value


def side_kernel(
    fem_disp_in, modulus_in, pd_pos_in, pd_disp_in, pay_even, pay_odd, fem_disp, modulus, pd_pos, pd_disp, sems
):
    fetch((fem_disp_in, modulus_in, pd_pos_in, pd_disp_in), (fem_disp, modulus, pd_pos, pd_disp), sems)
    nx, ny, nz = modulus.shape
    blocks = pd_disp.shape[1] // BLOCK
    points = point_rows(pd_pos[...], pd_disp[...])
    for pair in range(blocks // 2):
        part = points[:, 2 * BLOCK * pair : 2 * BLOCK * (pair + 1)]
        pay_even[8 * pair : 8 * pair + 8] = part
        pay_odd[8 * pair : 8 * pair + 8] = part
    even = (lax.axis_index("lat") & 1) == 0
    for pay, top in ((pay_even, even), (pay_odd, jnp.logical_not(even))):
        row = jnp.where(top, ny - 1, 0)
        for x in range(nx):
            for comp in range(4):
                at = halo_row(4 * x + comp)
                pay[at : at + 1] = fem_disp[comp, x, pl.ds(row, 1)] if comp < 3 else modulus[x, pl.ds(row, 1)]


def halo_row(number):
    return 8 * (number // 2) + 3 + 4 * (number % 2)


def halo_rows(ref, x):
    return jnp.concatenate([ref[halo_row(4 * x + c) : halo_row(4 * x + c) + 1] for c in range(4)], axis=0)


def face_kernel(both_faces, info, fem_disp, modulus, even_side, odd_side, faces):
    nx, ny, nz = modulus.shape
    even = (info[0] & 1) == 0

    def rows_at(number):
        upper = halo_rows(even_side, number), halo_rows(odd_side, number)
        return jnp.where(even, upper[1], upper[0]), jnp.where(even, upper[0], upper[1])

    def put(face, chosen, low, high):
        for comp in range(4):
            faces[face, comp, 0:ny] = chosen(comp)
            faces[face, comp, ny : ny + 1] = low[comp : comp + 1]
            faces[face, comp, ny + 1 : ny + 2] = high[comp : comp + 1]

    def layer(number):
        return lambda comp: fem_disp[comp, number] if comp < 3 else modulus[number]

    if both_faces:
        for face, number in ((0, 0), (1, nx - 1)):
            put(face, layer(number), *rows_at(number))
    else:
        upper = info[1] == 0
        first, second = rows_at(nx - 1), rows_at(0)
        put(
            0,
            lambda comp: jnp.where(upper, layer(nx - 1)(comp), layer(0)(comp)),
            jnp.where(upper, first[0], second[0]),
            jnp.where(upper, first[1], second[1]),
        )


def side_table(ref, block):
    rows = ref[8 * (block // 2) : 8 * (block // 2) + 8, BLOCK * (block % 2) : BLOCK * (block % 2 + 1)]
    row = iota(rows.shape, 0)
    squares = jnp.where((row >= 4) & (row < 7), rows * rows, 0.0)
    norm = (-0.5 * LOG2E) * jnp.sum(squares, axis=0, keepdims=True)
    return jnp.where(row == 3, 1.0, jnp.where(row == 7, norm, rows))


def own_features(points):
    row = iota(points.shape, 0)
    turned = pltpu.roll(points, 4, 0)
    value = jnp.where(row == 3, turned, jnp.where(row < 3, 0.0, jnp.where(row == 7, 1.0, LOG2E * points)))
    high, mid, low = (part.astype(F32) for part in split3(value))
    return jnp.concatenate([high, mid, high, mid, low, high], axis=0).astype(BF16)


def other_features(points):
    high, mid, low = (part.astype(F32) for part in split3(points))
    left = jnp.concatenate([high, high, mid, mid, high, low], axis=0)
    sums = jnp.concatenate([high, mid, low, jnp.zeros_like(low)], axis=0)
    return left.astype(BF16).T, sums.astype(BF16)


def pair_weights(left, own):
    weight = jnp.exp2(dot(left, own))
    high = weight.astype(BF16)
    low = (weight - high.astype(F32)).astype(BF16)
    return jnp.concatenate([high, low], axis=0)


def weighted(sums, weights):
    return dot(jnp.concatenate([sums, sums], axis=1), weights)


def fold(total):
    return total[0:8] + total[8:16] + total[16:24]


def neighbours(peers, place, first, second):
    even = (place & 1) == 0
    before = jnp.where(place > 0, jnp.where(even, second, first), 0.0)
    return before, jnp.where(place < peers - 1, jnp.where(even, first, second), 0.0)


def bond_kernel(peers, tail_blocks, members, info, family, own, even_side, odd_side, after, sums_out, pairs, left_ref, sums_ref):
    blocks = sums_out.shape[0]
    table = blocks + tail_blocks
    for block in range(blocks):
        first = side_table(even_side, block)
        second = side_table(odd_side, block)
        before, after = neighbours(peers, info[0], first, second)
        three = (before, side_table(own, block), after)
        for side, points in enumerate(three):
            left, sums = other_features(points)
            left_ref[side * blocks + block] = left
            sums_ref[side * blocks + block] = sums
    left_ref[3 * blocks] = jnp.zeros(left_ref.shape[1:], BF16)
    sums_ref[3 * blocks] = jnp.zeros(sums_ref.shape[1:], BF16)
    found = jnp.int32(0)
    mine, totals, places, weights = {}, {}, {}, {}
    units = blocks * members
    for unit in range(units + LAG):
        if unit < units:
            block, k = divmod(unit, members)
            if k == 0:
                mine[block] = own_features(side_table(own, block))
            member = family[k, block]
            side = jnp.where(member >= table, 1, 0) + jnp.where(member >= 2 * table, 1, 0)
            local = member - side * table
            outside = local >= blocks
            pairs[1 + found] = (block << PAIR_SHIFT) + member
            found = found + jnp.where(outside & (member < 3 * table), 1, 0)
            places[unit] = jnp.where(outside, 3 * blocks, side * blocks + local)
            weights[unit] = pair_weights(left_ref[places[unit]], mine[block])
        if unit >= LAG:
            done = unit - LAG
            block, k = divmod(done, members)
            total = weighted(sums_ref[places[done]], weights.pop(done))
            totals[block] = total if k == 0 else totals[block] + total
            if k == members - 1:
                sums_out[block] = fold(totals.pop(block))
    for extra in range(BATCH):
        pairs[1 + found + extra] = 3 * table
    pairs[0] = (found + BATCH - 1) // BATCH


def stiffness_rows(stiffness):
    new, old = iota((32, 24), 0), iota((32, 24), 1)
    place = sum(
        jnp.where(old == k, (k // 3 // 2) * 8 + (k // 3 % 2) * 4 + k % 3, 0) for k in range(24)
    )
    hot = one_hot(new == place)
    parts = [dot_nt(dot(hot, part).astype(BF16), hot) for part in split3(stiffness)]
    high, mid, low = parts
    pieces = []
    for corner in range(4):
        part = slice(8 * corner, 8 * corner + 8)
        for piece in (high, high, mid, mid, high, low):
            pieces.append(piece[:, part])
    return jnp.concatenate(pieces, axis=1).astype(BF16)


def ahead(value):
    last = value.shape[1] - 1
    return jnp.where(iota(value.shape, 1) == last, 0.0, pltpu.roll(value, last, 1))


def node_parts(node):
    row = iota(node.shape, 0)
    value = jnp.where((row != 3) & (row != 7), node, 0.0)
    high, mid, low = (part.astype(F32) for part in split3(value))
    first = jnp.concatenate([high, mid], axis=0).astype(BF16)
    return first, jnp.concatenate([low, high], axis=0).astype(BF16)


def gathered_force(total):
    turned = pltpu.roll(pltpu.roll(total, 4, 0), 1, 1)
    return total + jnp.where(iota(total.shape, 1) != 0, turned, 0.0)


def rock_kernel(
    depth,
    info,
    fem_disp,
    fem_vel,
    modulus,
    inv_mass,
    stiffness,
    low_x,
    high_x,
    after,
    out,
    edge_nodes,
    left_out,
    nodes,
    first_ref,
    second_ref,
    force_ref,
):
    nx, ny, nz = modulus.shape
    low_on = jnp.where(info[1] > 0, 1.0, 0.0)
    high_on = jnp.where(info[1] < depth - 1, 1.0, 0.0)
    halves = [slice(h * BLOCK, (h + 1) * BLOCK) for h in range(nz // BLOCK)]
    left = stiffness_rows(stiffness[...])
    left_out[...] = left
    for x in range(nx + 2):
        for comp in range(4):
            if x == 0:
                value = low_x[comp, 0:ny] * low_on
            elif x == nx + 1:
                value = high_x[comp, 0:ny] * high_on
            else:
                value = fem_disp[comp, x - 1] if comp < 3 else modulus[x - 1]
            at = x * ny * 8 + comp
            shifted = ahead(value)
            for half, part in enumerate(halves):
                nodes[half, pl.ds(at, ny, stride=8), :] = value[:, part]
                nodes[half, pl.ds(at + 4, ny, stride=8), :] = shifted[:, part]

    def node_row(x, y):
        at = (x * ny + y) * 8
        return jnp.concatenate([nodes[h, at : at + 8, :] for h in range(len(halves))], axis=1)

    for x in range(nx + 2):
        for y in range(ny):
            node = node_row(x, y)
            if y in (0, ny - 1):
                edge_nodes[0 if y == 0 else 1, x] = node
            first, second = node_parts(node)
            first_ref[x * ny + y] = first
            second_ref[x * ny + y] = second

    def element(x, y):
        pieces = []
        for a in range(2):
            for b in range(2):
                at = (x + a) * ny + y + b
                pieces += [first_ref[at], first_ref[at], second_ref[at]]
        return dot(left, jnp.concatenate(pieces, axis=0)) * node_row(x, y)[3:4]

    before = None
    for x in range(nx + 1):
        line = [element(x, y) for y in range(ny - 1)]
        if x > 0:
            for y in range(ny):
                terms = []
                if y < ny - 1:
                    terms += [line[y][0:8], before[y][16:24]]
                if y > 0:
                    terms += [line[y - 1][8:16], before[y - 1][24:32]]
                total = gathered_force(sum(terms[1:], terms[0]))
                at = ((x - 1) * ny + y) * 8
                for half, part in enumerate(halves):
                    force_ref[half, at : at + 8, :] = total[:, part]
        before = line
    for x in range(nx):
        for comp in range(3):
            force = jnp.concatenate(
                [force_ref[h, pl.ds(x * ny * 8 + comp, ny, stride=8), :] for h in range(len(halves))], axis=1
            )
            out[comp, x] = fem_vel[comp, x] - HALF * inv_mass[x] * force


def received(ref, peers, blocks, place, odd, wanted, row, pick):
    width = peers * CAP
    base = 3 * blocks

    def slot_rows(k):
        tiles = [ref[k, base + 16 * t : base + 16 * t + 16, :] for t in range(width // BLOCK)]
        return tiles[0] if len(tiles) == 1 else jnp.concatenate(tiles, axis=1)

    lane = iota((16, width), 1)
    back = lax.rem(width - CAP * (place - 1) + width, width)
    gathered = [jnp.zeros((16, width), F32) for _ in range(3)]
    for k in range(peers // 2):
        turned = pltpu.roll(slot_rows(k), back, 1)
        for side in range(3):
            window = jnp.where((lane >= CAP * side) & (lane < CAP * side + CAP), turned, 0.0)
            amount = (2 * CAP * k - CAP * side) % width
            gathered[side] = gathered[side] + (pltpu.roll(window, amount, 1) if amount else window)
    tails = [pltpu.roll(part, CAP * odd, 1) for part in gathered]
    rows = peers // 2 * blocks
    hit = (iota((rows, pick.shape[1]), 0) == row) & wanted
    values = []
    for comp in range(3):
        got = dot3(ref[:, comp * blocks : (comp + 1) * blocks, :].reshape(rows, BLOCK), pick)
        values.append(jnp.sum(jnp.where(hit, got, 0.0), axis=0, keepdims=True))
    return tails, values


def entry_places(entry, blocks):
    owner = entry[4:5].astype(jnp.int32)
    goal = entry[5:6].astype(jnp.int32)
    pick = one_hot(iota((BLOCK, entry.shape[1]), 0) == (goal & (BLOCK - 1)))
    return owner & 1, (owner >> 1) * blocks + (goal >> shift_of(BLOCK)), pick


def edge_kernel(
    peers,
    depth,
    blocks,
    info,
    mine_in,
    entries,
    rock,
    inv_mass,
    edge_nodes,
    left_in,
    low_x,
    high_x,
    even_side,
    odd_side,
    out,
    tails_out,
    values_out,
):
    nx, ny, nz = inv_mass.shape
    place = info[0]
    core = place & 1
    even = core == 0
    entry = entries[...]
    odd_owner, row, pick = entry_places(entry, blocks)
    tails, values = received(mine_in, peers, blocks, place, core, odd_owner == core, row, pick)
    for side in range(3):
        tails_out[side] = tails[side]
    values_out[...] = jnp.concatenate(values + [jnp.zeros((5, entry.shape[1]), F32)], axis=0)

    left = left_in[...]
    low_on = jnp.where(info[1] > 0, 1.0, 0.0)
    high_on = jnp.where(info[1] < depth - 1, 1.0, 0.0)
    for edge, from_even, node_y in ((0, jnp.logical_not(even), 0), (1, even, ny - 1)):
        inner, outer, lower = [], [], []
        for x in range(nx + 2):
            if x == 0:
                value = low_x[:, ny + edge] * low_on
            elif x == nx + 1:
                value = high_x[:, ny + edge] * high_on
            else:
                value = jnp.where(from_even, halo_rows(even_side, x - 1), halo_rows(odd_side, x - 1))
            other = jnp.concatenate([value, ahead(value)], axis=0)
            node = edge_nodes[edge, x]
            lower.append((other if edge == 0 else node)[3:4])
            inner.append(node_parts(node))
            outer.append(node_parts(other))
        forces = []
        for x in range(nx + 1):
            pieces = []
            for a in range(2):
                for b in range(2):
                    first, second = (outer if (b == 0) == (edge == 0) else inner)[x + a]
                    pieces += [first, first, second]
            forces.append(dot(left, jnp.concatenate(pieces, axis=0)) * lower[x])
        start = 8 if edge == 0 else 0
        for x in range(nx):
            total = forces[x + 1][start : start + 8] + forces[x][start + 16 : start + 24]
            force = gathered_force(total)
            rest = slice(1, ny - 1)
            for comp in range(3):
                scaled = HALF * inv_mass[x, node_y : node_y + 1] * force[comp : comp + 1]
                out[comp, x, node_y : node_y + 1] = rock[comp, x, node_y : node_y + 1] - scaled
                if edge == 0:
                    out[comp, x, rest] = rock[comp, x, rest]


def final_kernel(
    peers,
    members,
    info,
    pairs,
    family,
    mate_in,
    entries,
    rock,
    inv_mass,
    tails_in,
    values_in,
    sums_in,
    own,
    even_side,
    odd_side,
    pd_vel,
    fem_out,
    pd_out,
    table_ref,
    sums_ref,
):
    nx, ny, nz = inv_mass.shape
    width = peers * CAP
    tail_blocks = width // BLOCK
    blocks = sums_in.shape[0]
    table = blocks + tail_blocks
    place = info[0]
    core = place & 1
    for block in range(blocks):
        first = side_table(even_side, block)
        second = side_table(odd_side, block)
        before, after = neighbours(peers, place, first, second)
        table_ref[block] = before
        table_ref[table + block] = side_table(own, block)
        table_ref[2 * table + block] = after
        sums_ref[block] = sums_in[block]
    table_ref[3 * table] = jnp.zeros((8, BLOCK), F32)

    entry = entries[...]
    count = entry.shape[1]
    odd_owner, row, pick = entry_places(entry, blocks)
    tails, values = received(mate_in, peers, blocks, place, 1 - core, odd_owner != core, row, pick)
    tails = [tails[side] + tails_in[side] for side in range(3)]
    on = (jnp.where(place > 0, 1.0, 0.0), 1.0, jnp.where(place < peers - 1, 1.0, 0.0))
    for side in range(3):
        for tile in range(tail_blocks):
            part = tails[side][0:8, tile * BLOCK : (tile + 1) * BLOCK]
            table_ref[side * table + blocks + tile] = part * on[side]
    tail_rows = tails[1]

    def several(codes):
        ready = []
        for block, member in codes:
            left, sums = other_features(table_ref[member])
            ready.append((block, sums, pair_weights(left, own_features(table_ref[table + block]))))
        return [(block, fold(weighted(sums, weights))) for block, sums, weights in ready]

    for block in range(blocks, table):
        results = several([(block, family[k, block]) for k in range(members)])
        sums_ref[block] = sum((total for _, total in results[1:]), results[0][1])

    def some(index, carry):
        codes = [pairs[1 + BATCH * index + k] for k in range(BATCH)]
        for block, total in several([(code >> PAIR_SHIFT, code & ((1 << PAIR_SHIFT) - 1)) for code in codes]):
            sums_ref[block] = sums_ref[block] + total
        return carry

    node = entry[6:7].astype(jnp.int32)
    z_hot = one_hot(iota((nz, count), 0) == (node & (nz - 1)))
    xy_hit = iota((nx * ny, count), 0) == (node >> shift_of(nz))
    spread = []
    for comp in range(3):
        value = values[comp] + values_in[comp : comp + 1]
        spread.append(jnp.where(xy_hit, entry[3:4] * (entry[comp : comp + 1] - value), 0.0))
    pull = dot3_nt(jnp.concatenate(spread, axis=0), z_hot).reshape(3, nx, ny, nz)
    fem_out[...] = rock[...] - HALF * inv_mass[...][None] * pull

    stiff = tail_rows[14:15]
    target = tail_rows[15:16].astype(jnp.int32)
    hot_lane = one_hot(iota((BLOCK, width), 0) == (target & (BLOCK - 1)))
    target_block = target >> shift_of(BLOCK)
    tables = jnp.concatenate([side_table(own, block) for block in range(blocks)], axis=0)
    looked = dot3(tables, hot_lane)
    found = jnp.zeros((8, width), F32)
    for block in range(blocks):
        found = found + jnp.where(target_block == block, looked[8 * block : 8 * block + 8], 0.0)
    coupling = stiff * (tail_rows[11:14] - found[0:3])
    coupling = jnp.concatenate([coupling, jnp.zeros((5, width), F32)], axis=0)
    spread = jnp.concatenate([jnp.where(target_block == block, coupling, 0.0) for block in range(blocks)], axis=0)
    couple = dot3_nt(spread, hot_lane)

    lax.fori_loop(0, pairs[0], some, 0)

    scale = GAIN / (BLOCK * members)
    for block in range(table):
        total = sums_ref[block]
        points = table_ref[table + block]
        part = slice(block * BLOCK, (block + 1) * BLOCK)
        force = scale * points[3:4] * (total[0:3] - points[0:3] * total[3:4])
        if block < blocks:
            pd_out[:, part] = pd_vel[:, part] + HALF * (force + couple[8 * block : 8 * block + 3])
        else:
            tile = block - blocks
            pd_out[:, part] = tail_rows[8:11, tile * BLOCK : (tile + 1) * BLOCK] + HALF * force


def call(kernel, outs, specs, scratch, microseconds, args, name, out_specs=None, vmem=24):
    return pl.pallas_call(
        kernel,
        out_shape=outs,
        in_specs=specs,
        out_specs=out_specs or jax.tree.map(lambda _: VMEM, outs),
        scratch_shapes=scratch,
        compiler_params=params(vmem),
        cost_estimate=pl.CostEstimate(flops=0, bytes_accessed=int(3.6e6 * microseconds), transcendentals=0),
        name=name,
    )(*args)


def shards(
    fem_disp,
    fem_vel,
    modulus,
    inv_mass,
    element_stiffness,
    pd_pos,
    pd_disp,
    pd_vel,
    conv_state,
    conv_owner,
    family,
    ov_owner,
    ov_node,
    ov_target,
    ov_stiff,
):
    peers = lax.axis_size("lat")
    depth = lax.axis_size("depth")
    nx, ny, nz = modulus.shape
    blocks = pd_pos.shape[1] // BLOCK
    tail_blocks = peers * CAP // BLOCK
    table = blocks + tail_blocks
    members = family.shape[1]
    count = ov_node.shape[0]
    chips = peers // 2
    chunk_rows = 3 * blocks + 16 * tail_blocks
    shaped = jax.ShapeDtypeStruct
    info = jnp.stack([lax.axis_index("lat"), lax.axis_index("depth")]).astype(jnp.int32)

    both_faces = depth > 2
    family = family.T
    sources = (fem_disp, modulus, pd_pos, pd_disp)
    pay_even, pay_odd = call(
        side_kernel,
        (shaped((4 * blocks, nz), F32),) * 2,
        [FAR] * 4,
        [pltpu.VMEM(value.shape, value.dtype) for value in sources] + [pltpu.SemaphoreType.DMA((4,))],
        1.5,
        sources,
        "side",
        vmem=SIDE_VMEM,
    )
    swap = [(i, i ^ 1) for i in range(peers)]
    cross = [(i, i + 1) for i in range(1, peers - 1, 2)] + [(i + 1, i) for i in range(1, peers - 1, 2)]
    odd_side = lax.ppermute(pay_odd, "lat", cross)
    even_side = lax.ppermute(pay_even, "lat", swap)
    inputs = (
        fem_disp,
        pd_disp,
        conv_state,
        conv_owner.reshape(1, -1),
        ov_owner.reshape(1, -1),
        ov_node.reshape(1, -1),
        ov_target.reshape(1, -1),
        ov_stiff.reshape(1, -1),
    )
    chunk, entries = call(
        functools.partial(pack_kernel, peers),
        (shaped((chips, chunk_rows, BLOCK), F32), shaped((8, count), F32)),
        [VMEM] * 8,
        [pltpu.VMEM((chunk_rows, BLOCK), F32)],
        2.0,
        inputs,
        "pack",
    )
    chunk, even_side, odd_side = lax.optimization_barrier((chunk, even_side, odd_side))
    groups = [[side + 2 * k for k in range(chips)] for side in range(2)]
    mine = lax.all_to_all(chunk, "lat", split_axis=0, concat_axis=0, tiled=True, axis_index_groups=groups)

    count_faces = 2 if both_faces else 1
    faces = call(
        functools.partial(face_kernel, both_faces),
        shaped((count_faces, 4, ny + 2, nz), F32),
        [SMEM] + [VMEM] * 4,
        [],
        0.6,
        (info, fem_disp, modulus, even_side, odd_side),
        "face",
    )
    faces, pay_even, even_side, odd_side = lax.optimization_barrier((faces, pay_even, even_side, odd_side))
    if both_faces:
        low_x = lax.ppermute(faces[1], "depth", [(i, i + 1) for i in range(depth - 1)])
        high_x = lax.ppermute(faces[0], "depth", [(i + 1, i) for i in range(depth - 1)])
    else:
        low_x = high_x = lax.ppermute(faces[0], "depth", [(0, 1), (1, 0)])

    sums, pairs = call(
        functools.partial(bond_kernel, peers, tail_blocks, members),
        (shaped((blocks, 8, BLOCK), F32), shaped((table * members + BATCH + 1,), jnp.int32)),
        [SMEM, SMEM] + [VMEM] * 3 + [ANY],
        [pltpu.VMEM((3 * blocks + 1, BLOCK, 48), BF16), pltpu.VMEM((3 * blocks + 1, 32, BLOCK), BF16)],
        4.3,
        (info, family, pay_even, even_side, odd_side, faces),
        "bond",
        out_specs=(VMEM, SMEM),
    )
    node_rows = (nx + 2) * ny
    rock, edge_nodes, left = call(
        functools.partial(rock_kernel, depth),
        (shaped(fem_vel.shape, F32), shaped((2, nx + 2, 8, nz), F32), shaped((32, 192), BF16)),
        [SMEM] + [VMEM] * 7 + [ANY],
        [
            pltpu.VMEM((nz // BLOCK, node_rows * 8, BLOCK), F32),
            pltpu.VMEM((node_rows, 16, nz), BF16),
            pltpu.VMEM((node_rows, 16, nz), BF16),
            pltpu.VMEM((nz // BLOCK, nx * ny * 8, BLOCK), F32),
        ],
        1.8,
        (info, fem_disp, fem_vel, modulus, inv_mass, element_stiffness, low_x, high_x, sums),
        "rock",
    )
    mine, rock = lax.optimization_barrier((mine, rock))
    mate = lax.ppermute(mine, "lat", swap)
    rock, tails, values = call(
        functools.partial(edge_kernel, peers, depth, blocks),
        (shaped(fem_vel.shape, F32), shaped((3, 16, peers * CAP), F32), shaped((8, count), F32)),
        [SMEM] + [VMEM] * 10,
        [],
        1.0,
        (info, mine, entries, rock, inv_mass, edge_nodes, left, low_x, high_x, even_side, odd_side),
        "edge",
    )
    return call(
        functools.partial(final_kernel, peers, members),
        (shaped(fem_vel.shape, F32), shaped((3, table * BLOCK), F32)),
        [SMEM] * 3 + [VMEM] * 11,
        [pltpu.VMEM((3 * table + 1, 8, BLOCK), F32), pltpu.VMEM((table, 8, BLOCK), F32)],
        2.6,
        (
            info,
            pairs,
            family,
            mate,
            entries,
            rock,
            inv_mass,
            tails,
            values,
            sums,
            pay_even,
            even_side,
            odd_side,
            pd_vel,
        ),
        "final",
    )


def solution(mesh):
    lat = P(None, ("depth", "lat"))
    rows = P(("depth", "lat"), None)
    flat = P(("depth", "lat"))
    nodes = P(None, "depth", "lat", None)
    grid = P("depth", "lat", None)
    return jax.shard_map(
        shards,
        mesh=mesh,
        in_specs=(nodes, nodes, grid, grid, P(), lat, lat, lat, lat, rows, rows, rows, flat, flat, flat),
        out_specs=(nodes, lat),
        check_vma=False,
    )
```

time: 39.7 us -> 28.9 us (0.73); the launches traced: 38.9 us -> 28.5 us
  Pallas kernels: 17.8 us -> 13.1 us
  waiting for transfers between devices: 3.26 us -> 0.89 us
  local copies, waits for them, and re-layouts: 2.53 us -> 0.72 us
  starting transfers between devices: 14.5 us -> 13 us
    pallas_call x5 -> x7, Pallas kernels: 17.8 us -> 13.1 us  [call(): pl.pallas_call(kernel, out_shape=outs, in_specs=specs, out_specs=out_spec...]
    ppermute x1, waiting for transfers between devices: 2.42 us -> 0.01 us  [shards(): low_x = high_x = lax.ppermute(faces[0], 'depth', [(0, 1), (1, 0)])]
    unnamed x35 -> x30, local copies, waits for them, and re-layouts: 2.53 us -> 0.72 us
    ppermute x1, starting transfers between devices: 1.49 us -> 0.01 us  [shards(): mate = lax.ppermute(mine, 'lat', swap)]
    all_to_all x1, starting transfers between devices: 7.41 us -> 6.38 us  [shards(): lax.all_to_all(chunk, 'lat', split_axis=0, concat_axis=0, tiled=True, axi...]
    ppermute x1, starting transfers between devices: 3.44 us -> 4.39 us  [shards(): even_side = lax.ppermute(pay_even, 'lat', swap)]
    ppermute x1, waiting for transfers between devices: 0.83 us -> 0.01 us  [shards(): even_side = lax.ppermute(pay_even, 'lat', swap)]
    ppermute x1, waiting for transfers between devices: 0.01 us -> 0.53 us  [shards(): mate = lax.ppermute(mine, 'lat', swap)]
  transfers between devices with their start and end apart: 5 -> 5, of which waited for: 2 -> 2; matrix products, arithmetic and copies ran while one was open for 0% -> 0% of each run, Pallas kernels for 30% -> 31%
where the time goes in v2:
time: 28.9 us; the launch traced here: 28.5 us
  Pallas kernels  13.1 us (45%)
  starting transfers between devices  13 us (45%)
  waiting for transfers between devices  0.89 us (3%)
  between operations  0.79 us (3%)
  local copies, waits for them, and re-layouts  0.72 us (2%)
    pallas_call x7, Pallas kernels, call(): pl.pallas_call(kernel, out_shape=outs, in_specs=specs, out_specs=out_spec...  13.1 us
    all_to_all x1, starting transfers between devices, shards(): lax.all_to_all(chunk, 'lat', split_axis=0, concat_axis=0, tiled=True, axi...  6.38 us
    ppermute x1, starting transfers between devices, shards(): even_side = lax.ppermute(pay_even, 'lat', swap)  4.39 us
    ppermute x1, starting transfers between devices, shards(): low_x = high_x = lax.ppermute(faces[0], 'depth', [(0, 1), (1, 0)])  1.56 us
    unnamed x30, local copies, waits for them, and re-layouts  0.72 us
    ppermute x1, starting transfers between devices, shards(): odd_side = lax.ppermute(pay_odd, 'lat', cross)  0.66 us
  transfers between devices with their start and end apart: 5, of which 2 were waited for; matrix products, arithmetic and copies ran while one was open for 0% of the time, Pallas kernels for 31%

profile of v2, /device:TPU:0, one launch (start us, length us, event | category | flops | bytes accessed | tf_op | source)
XLA Modules:
  0.0 28.5 jit_solution(4150650660369474552)
XLA Ops:
  0.6 1.7 %side.1 = (f32[64,256]{1,0:T(8,128)}, f32[64,256]{1,0:T(8,128)}) custom-call(f32[3,4,8,256]{3,2,1,0:T(8,128)} %fem_disp.5, f32[4,8,256]{2,1,0:T(8,128)} %modulus.3, f32[3,2048]{1,0:T(4,128)} %pd_pos_in.1, f32[3,2048]{1,0:T(4,128)} %pd_disp_in.1), custom_call_target="tpu_custom_call" | custom-call | bytes 5400000 | tf_op jit(solution)/shard_map/side/pallas_call | solution.py:620
  2.3 0.0 copy-start.9
  2.3 0.7 %collective-permute-start.1 = (f32[64,256]{1,0:T(8,128)}, f32[64,256]{1,0:T(8,128)S(1)}, u32[]{:S(2)}, u32[]{:S(2)}) collective-permute-start(f32[64,256]{1,0:T(8,128)} %get-tuple-element.25), channel_id=1, source_target_pairs={{1,2},{3,4},{5,6},{7,8},{9,10},{11,12},{13,14},{2,1},{4,3},{6,5},{... | collective-permute-start | bytes 196616 | tf_op jit(solution)/shard_map/ppermute | solution.py:677
  3.0 4.4 %collective-permute-start = (f32[64,256]{1,0:T(8,128)}, f32[64,256]{1,0:T(8,128)S(1)}, u32[]{:S(2)}, u32[]{:S(2)}) collective-permute-start(f32[64,256]{1,0:T(8,128)} %get-tuple-element.28.own), channel_id=1, source_target_pairs={{0,1},{1,0},{2,3},{3,2},{4,5},{5,4},{6,7},{7,6},{8,9},{9,8},{10,11... | collective-permute-start | bytes 196616 | tf_op jit(solution)/shard_map/ppermute | solution.py:678
  7.4 0.0 copy-start.12
  7.5 0.6 %copy-done.13 = s32[64]{0:T(128)S(1)} copy-done((s32[64]{0:T(128)S(1)}, s32[64]{0:T(128)}, u32[]{:S(2)}) %copy-start.13) | copy-done | bytes 280
  8.1 0.0 copy-done.14
  8.1 0.0 copy-done.10
  8.1 0.0 copy-done.11
  8.1 0.0 copy-done.12
  8.1 1.0 %pack.1 = (f32[8,64,128]{2,1,0:T(8,128)}, f32[8,64]{1,0:T(8,128)S(1)}) custom-call(f32[3,4,8,256]{3,2,1,0:T(8,128)S(1)} %copy-done, f32[3,2048]{1,0:T(4,128)S(1)} %copy-done.4, f32[9,64]{1,0:T(8,128)S(1)} %copy-done.9, s32[1,64]{1,0:T(1,128)S(1)} %bitcast.12, s32[1,64]{1,0:T(1,128)S(1)} %bitcast.13, s32[1,64]{1,0:T(1,128)S(1)} %bitcast.14, ...), custom_call_target="tpu_custom_call" | custom-call | bytes 7200000 | tf_op jit(solution)/shard_map/pack/pallas_call | solution.py:620
  9.2 0.0 collective-permute-done.1.odd_side
  9.2 0.0 collective-permute-done.even_side
  9.2 6.4 %all-to-all-start = ((f32[8,64,128]{2,1,0:T(8,128)}), f32[8,64,128]{2,1,0:T(8,128)S(1)}, u32[]{:S(2)}, u32[]{:S(2)}) async-start(f32[8,64,128]{2,1,0:T(8,128)} %get-tuple-element.33), calls=%async_computation | async-start | bytes 524288 | tf_op jit(solution)/shard_map/all_to_all | solution.py:700
  15.6 0.1 pad_add_fusion.info
  15.6 0.6 %face.1.after = f32[1,4,10,256]{3,2,1,0:T(8,128)S(1)} custom-call(s32[2]{0:T(128)S(1)} %pad_add_fusion.info, f32[3,4,8,256]{3,2,1,0:T(8,128)S(1)} %copy-done, f32[4,8,256]{2,1,0:T(8,128)S(1)} %copy-done.1, f32[64,256]{1,0:T(8,128)S(1)} %collective-permute-done.even_side, f32[64,256]{1,0:T(8,128)S(1)} %collective-permute-done.1.odd_side), custom_call_target="tpu_custom_call" | custom-call | bytes 2160000 | tf_op jit(solution)/shard_map/face/pallas_call | solution.py:620
  16.2 1.6 %collective-permute-start.2 = (f32[4,10,256]{2,1,0:T(8,128)S(1)}, f32[4,10,256]{2,1,0:T(8,128)S(1)}, u32[]{:S(2)}, u32[]{:S(2)}) collective-permute-start(f32[4,10,256]{2,1,0:T(8,128)S(1)} %bitcast.9), channel_id=1, source_target_pairs={{0,16},{16,0},{1,17},{17,1},{2,18},{18,2},{3,19},{19,3},{4,20},{20... | collective-permute-start | bytes 122888 | tf_op jit(solution)/shard_map/ppermute | solution.py:717
  17.8 0.0 copy-start.8
  17.8 4.3 %bond.1 = (f32[16,8,128]{2,1,0:T(8,128)S(1)}, s32[145]{0:T(256)S(1)}) custom-call(s32[2]{0:T(128)S(1)} %pad_add_fusion.info, s32[8,17]{1,0:T(8,128)S(1)} %bitcast.10, f32[64,256]{1,0:T(8,128)S(1)} %copy-done.3, f32[64,256]{1,0:T(8,128)S(1)} %collective-permute-done.even_side, f32[64,256]{1,0:T(8,128)S(1)} %collective-permute-done.1.odd_side, ...), custom_call_target="tpu_custom_call" | custom-call | bytes 15480000 | tf_op jit(solution)/shard_map/bond/pallas_call | solution.py:620
  22.2 1.8 %rock.1 = (f32[3,4,8,256]{3,2,1,0:T(8,128)S(1)}, f32[2,6,8,256]{3,2,1,0:T(8,128)S(1)}, bf16[32,192]{1,0:T(8,128)(2,1)S(1)}) custom-call(s32[2]{0:T(128)S(1)} %pad_add_fusion.info, f32[3,4,8,256]{3,2,1,0:T(8,128)S(1)} %copy-done, f32[3,4,8,256]{3,2,1,0:T(8,128)S(1)} %copy-done.5, f32[4,8,256]{2,1,0:T(8,128)S(1)} %copy-done.1, f32[4,8,256]{2,1,0:T(8,128)S(1)} %copy-done.2, ...), custom_call_target="tpu_custom_call" | custom-call | bytes 6480000 | tf_op jit(solution)/shard_map/rock/pallas_call | solution.py:620
  24.0 0.3 %all-to-all-done.mine_in = f32[8,64,128]{2,1,0:T(8,128)S(1)} async-done(((f32[8,64,128]{2,1,0:T(8,128)}), f32[8,64,128]{2,1,0:T(8,128)S(1)}, u32[]{:S(2)}, u32[]{:S(2)}) %all-to-all-start) | async-done | bytes 262176 | tf_op jit(solution)/shard_map/all_to_all | solution.py:700
  24.4 1.0 %edge.1 = (f32[3,4,8,256]{3,2,1,0:T(8,128)S(1)}, f32[3,16,128]{2,1,0:T(8,128)S(1)}, f32[8,64]{1,0:T(8,128)S(1)}) custom-call(s32[2]{0:T(128)S(1)} %pad_add_fusion.info, f32[8,64,128]{2,1,0:T(8,128)S(1)} %all-to-all-done.mine_in, f32[8,64]{1,0:T(8,128)S(1)} %get-tuple-element.37.entries, f32[3,4,8,256]{3,2,1,0:T(8,128)S(1)} %get-tuple-element.38.rock, ...), custom_call_target="tpu_custom_call" | custom-call | bytes 3600000 | tf_op jit(solution)/shard_map/edge/pallas_call | solution.py:620
  25.4 0.5 %collective-permute-done.3.mate_in = f32[8,64,128]{2,1,0:T(8,128)S(1)} collective-permute-done((f32[8,64,128]{2,1,0:T(8,128)S(1)}, f32[8,64,128]{2,1,0:T(8,128)S(1)}, u32[]{:S(2)}, u32[]{:S(2)}) %collective-permute-start.3) | collective-permute-done | bytes 262176 | tf_op jit(solution)/shard_map/ppermute | solution.py:745
  25.9 2.6 %final.1 = (f32[3,4,8,256]{3,2,1,0:T(8,128)}, f32[3,2176]{1,0:T(4,128)}) custom-call(s32[2]{0:T(128)S(1)} %pad_add_fusion.info, s32[145]{0:T(256)S(1)} %get-tuple-element.32.pairs, s32[8,17]{1,0:T(8,128)S(1)} %bitcast.11, f32[8,64,128]{2,1,0:T(8,128)S(1)} %collective-permute-done.3.mate_in, f32[8,64]{1,0:T(8,128)S(1)} %get-tuple-element.37.entries, ...), custom_call_target="tpu_custom_call" | custom-call | bytes 9360000 | tf_op jit(solution)/shard_map/final/pallas_call | solution.py:620
  (24 shorter events, 0.0 us)
Async XLA Ops:
  0.6 6.8 %copy-start = (f32[3,4,8,256]{3,2,1,0:T(8,128)S(1)}, f32[3,4,8,256]{3,2,1,0:T(8,128)}, u32[]{:S(2)}) copy-start(f32[3,4,8,256]{3,2,1,0:T(8,128)} %fem_disp.5) | copy-start | bytes 294916
  0.6 6.8 %copy-start.4 = (f32[3,2048]{1,0:T(4,128)S(1)}, f32[3,2048]{1,0:T(4,128)}, u32[]{:S(2)}) copy-start(f32[3,2048]{1,0:T(4,128)} %pd_disp_in.1) | copy-start | bytes 73732
  2.3 5.1 %copy-start.9 = (f32[9,64]{1,0:T(8,128)S(1)}, f32[9,64]{1,0:T(8,128)}, u32[]{:S(2)}) copy-start(f32[9,64]{1,0:T(8,128)} %conv_state.1) | copy-start | bytes 6916
  2.3 6.8 %collective-permute-start.1 = (f32[64,256]{1,0:T(8,128)}, f32[64,256]{1,0:T(8,128)S(1)}, u32[]{:S(2)}, u32[]{:S(2)}) collective-permute-start(f32[64,256]{1,0:T(8,128)} %get-tuple-element.25), channel_id=1, source_target_pairs={{1,2},{3,4},{5,6},{7,8},{9,10},{11,12},{13,14},{2,1},{4,3},{6,5},{... | collective-permute-start | bytes 196616 | tf_op jit(solution)/shard_map/ppermute | solution.py:677
  3.0 6.2 %collective-permute-start = (f32[64,256]{1,0:T(8,128)}, f32[64,256]{1,0:T(8,128)S(1)}, u32[]{:S(2)}, u32[]{:S(2)}) collective-permute-start(f32[64,256]{1,0:T(8,128)} %get-tuple-element.28.own), channel_id=1, source_target_pairs={{0,1},{1,0},{2,3},{3,2},{4,5},{5,4},{6,7},{7,6},{8,9},{9,8},{10,11... | collective-permute-start | bytes 196616 | tf_op jit(solution)/shard_map/ppermute | solution.py:678
  7.4 0.7 %copy-start.13 = (s32[64]{0:T(128)S(1)}, s32[64]{0:T(128)}, u32[]{:S(2)}) copy-start(s32[64]{0:T(128)} %param.28) | copy-start | bytes 772
  7.4 0.7 %copy-start.14 = (f32[64]{0:T(128)S(1)}, f32[64]{0:T(128)}, u32[]{:S(2)}) copy-start(f32[64]{0:T(128)} %param.29) | copy-start | bytes 772
  7.4 0.7 %copy-start.10 = (s32[64,1]{0,1:T(1,128)S(1)}, s32[64,1]{0,1:T(1,128)}, u32[]{:S(2)}) copy-start(s32[64,1]{0,1:T(1,128)} %param.24) | copy-start | bytes 772
  7.4 0.7 %copy-start.11 = (s32[64,1]{0,1:T(1,128)S(1)}, s32[64,1]{0,1:T(1,128)}, u32[]{:S(2)}) copy-start(s32[64,1]{0,1:T(1,128)} %param.26) | copy-start | bytes 772
  7.4 0.7 %copy-start.12 = (s32[64]{0:T(128)S(1)}, s32[64]{0:T(128)}, u32[]{:S(2)}) copy-start(s32[64]{0:T(128)} %param.27) | copy-start | bytes 772
  9.2 6.5 %copy-start.1 = (f32[4,8,256]{2,1,0:T(8,128)S(1)}, f32[4,8,256]{2,1,0:T(8,128)}, u32[]{:S(2)}) copy-start(f32[4,8,256]{2,1,0:T(8,128)} %modulus.3) | copy-start | bytes 98308
  9.2 15.2 %all-to-all-start = ((f32[8,64,128]{2,1,0:T(8,128)}), f32[8,64,128]{2,1,0:T(8,128)S(1)}, u32[]{:S(2)}, u32[]{:S(2)}) async-start(f32[8,64,128]{2,1,0:T(8,128)} %get-tuple-element.33), calls=%async_computation | async-start | bytes 524288 | tf_op jit(solution)/shard_map/all_to_all | solution.py:700
  15.6 2.1 %copy-start.3 = (f32[64,256]{1,0:T(8,128)S(1)}, f32[64,256]{1,0:T(8,128)}, u32[]{:S(2)}) copy-start(f32[64,256]{1,0:T(8,128)} %get-tuple-element.28.own) | copy-start | bytes 196612
  15.6 2.1 %copy-start.7 = (s32[17,8]{0,1:T(8,128)S(1)}, s32[17,8]{0,1:T(8,128)}, u32[]{:S(2)}) copy-start(s32[17,8]{0,1:T(8,128)} %param.25) | copy-start | bytes 1636
  16.2 5.9 %collective-permute-start.2 = (f32[4,10,256]{2,1,0:T(8,128)S(1)}, f32[4,10,256]{2,1,0:T(8,128)S(1)}, u32[]{:S(2)}, u32[]{:S(2)}) collective-permute-start(f32[4,10,256]{2,1,0:T(8,128)S(1)} %bitcast.9), channel_id=1, source_target_pairs={{0,16},{16,0},{1,17},{17,1},{2,18},{18,2},{3,19},{19,3},{4,20},{20... | collective-permute-start | bytes 122888 | tf_op jit(solution)/shard_map/ppermute | solution.py:717
  17.8 4.4 %copy-start.2 = (f32[4,8,256]{2,1,0:T(8,128)S(1)}, f32[4,8,256]{2,1,0:T(8,128)}, u32[]{:S(2)}) copy-start(f32[4,8,256]{2,1,0:T(8,128)} %inv_mass.5) | copy-start | bytes 98308
  17.8 4.4 %copy-start.5 = (f32[3,4,8,256]{3,2,1,0:T(8,128)S(1)}, f32[3,4,8,256]{3,2,1,0:T(8,128)}, u32[]{:S(2)}) copy-start(f32[3,4,8,256]{3,2,1,0:T(8,128)} %fem_vel.1) | copy-start | bytes 294916
  17.8 4.4 %copy-start.8 = (f32[24,24]{1,0:T(8,128)S(1)}, f32[24,24]{1,0:T(8,128)}, u32[]{:S(2)}) copy-start(f32[24,24]{1,0:T(8,128)} %stiffness.1) | copy-start | bytes 6916
  24.4 1.5 %collective-permute-start.3 = (f32[8,64,128]{2,1,0:T(8,128)S(1)}, f32[8,64,128]{2,1,0:T(8,128)S(1)}, u32[]{:S(2)}, u32[]{:S(2)}) collective-permute-start(f32[8,64,128]{2,1,0:T(8,128)S(1)} %all-to-all-done.mine_in), channel_id=1, source_target_pairs={{0,1},{1,0},{2,3},{3,2},{4,5},{5,4},{6,7},{7,6},{8,9},{9,8},{10,11... | collective-permute-start | bytes 786440 | tf_op jit(solution)/shard_map/ppermute | solution.py:745
  24.4 1.5 %copy-start.6 = (f32[3,2048]{1,0:T(4,128)S(1)}, f32[3,2048]{1,0:T(4,128)}, u32[]{:S(2)}) copy-start(f32[3,2048]{1,0:T(4,128)} %pd_vel.1) | copy-start | bytes 73732

commit v3 on v2

--- a/solution.py
+++ b/solution.py
@@ -16,8 +16,9 @@
 F32 = jnp.float32
 BF16 = jnp.bfloat16
 LAG = 8
-BATCH = 8
+BATCH = 16
 PAIR_SHIFT = 6
+PAIR_SLOTS = 256
 SIDE_VMEM = 63
 
 VMEM = pl.BlockSpec(memory_space=pltpu.VMEM)
@@ -85,28 +86,63 @@
     return owner * CAP + rank, named
 
 
-def fetch(sources, places, sems):
+def pack_kernel(
+    peers,
+    ov_node_in,
+    fem_disp_in,
+    conv_owner_in,
+    ov_owner_in,
+    conv_state_in,
+    ov_target_in,
+    ov_stiff_in,
+    pd_disp_in,
+    pd_pos_in,
+    modulus_in,
+    chunk,
+    pay_even,
+    pay_odd,
+    rows_ref,
+    ov_node,
+    fem_disp,
+    conv_owner,
+    ov_owner,
+    conv_state,
+    ov_target,
+    ov_stiff,
+    pd_disp,
+    pd_pos,
+    modulus,
+    sems,
+):
+    sources = (
+        ov_node_in,
+        fem_disp_in,
+        conv_owner_in,
+        ov_owner_in,
+        conv_state_in,
+        ov_target_in,
+        ov_stiff_in,
+        pd_disp_in,
+        pd_pos_in,
+        modulus_in,
+    )
+    places = (
+        ov_node,
+        fem_disp,
+        conv_owner,
+        ov_owner,
+        conv_state,
+        ov_target,
+        ov_stiff,
+        pd_disp,
+        pd_pos,
+        modulus,
+    )
     copies = [pltpu.make_async_copy(f, t, sems.at[i]) for i, (f, t) in enumerate(zip(sources, places))]
     for copy in copies:
         copy.start()
     for copy in copies:
         copy.wait()
-
-
-def pack_kernel(
-    peers,
-    fem_disp,
-    pd_disp,
-    conv_state,
-    conv_owner,
-    ov_owner,
-    ov_node,
-    ov_target,
-    ov_stiff,
-    chunk,
-    entries,
-    rows_ref,
-):
     _, nx, ny, nz = fem_disp.shape
     width = peers * CAP
     blocks = pd_disp.shape[1] // BLOCK
@@ -128,7 +164,7 @@
     ov_rows = jnp.concatenate([jnp.zeros((3, count), F32), at_node, stiff, target], axis=0)
     conv_out = dot3(conv_rows, one_hot(conv_slot == lane))
     ov_out = dot3(ov_rows, one_hot(ov_slot == lane))
-    entries[...] = jnp.concatenate(
+    pay_even[4 * blocks : 4 * blocks + 8, 0:count] = jnp.concatenate(
         [at_node, stiff, ov_named, target, node.astype(F32), jnp.zeros((1, count), F32)], axis=0
     )
     for block in range(blocks):
@@ -145,13 +181,6 @@
     for copy in range(chunk.shape[0]):
         chunk[copy] = value
 
-
-def side_kernel(
-    fem_disp_in, modulus_in, pd_pos_in, pd_disp_in, pay_even, pay_odd, fem_disp, modulus, pd_pos, pd_disp, sems
-):
-    fetch((fem_disp_in, modulus_in, pd_pos_in, pd_disp_in), (fem_disp, modulus, pd_pos, pd_disp), sems)
-    nx, ny, nz = modulus.shape
-    blocks = pd_disp.shape[1] // BLOCK
     points = point_rows(pd_pos[...], pd_disp[...])
     for pair in range(blocks // 2):
         part = points[:, 2 * BLOCK * pair : 2 * BLOCK * (pair + 1)]
@@ -174,7 +203,7 @@
     return jnp.concatenate([ref[halo_row(4 * x + c) : halo_row(4 * x + c) + 1] for c in range(4)], axis=0)
 
 
-def face_kernel(both_faces, info, fem_disp, modulus, even_side, odd_side, faces):
+def face_kernel(both_faces, info, fem_disp, modulus, even_side, odd_side, after, faces):
     nx, ny, nz = modulus.shape
     even = (info[0] & 1) == 0
 
@@ -249,36 +278,50 @@
     return before, jnp.where(place < peers - 1, jnp.where(even, first, second), 0.0)
 
 
-def bond_kernel(peers, tail_blocks, members, info, family, own, even_side, odd_side, after, sums_out, pairs, left_ref, sums_ref):
+def member_codes(family, blocks, tail_blocks):
+    table = blocks + tail_blocks
+    side = (family >= table).astype(jnp.int32) + (family >= 2 * table).astype(jnp.int32)
+    local = family - side * table
+    outside = local >= blocks
+    where = jnp.where(outside, 3 * blocks, side * blocks + local)
+    is_tail = (outside & (family < 3 * table)).astype(jnp.int32)
+    number = is_tail * (side * tail_blocks + local - blocks)
+    return (((is_tail << PAIR_SHIFT) + number) << PAIR_SHIFT) + where
+
+
+def low_bits(code):
+    return code & ((1 << PAIR_SHIFT) - 1)
+
+
+def bond_kernel(
+    peers, tail_blocks, members, info, codes, own, even_side, odd_side, after, sums_out, tables, left_ref, sums_ref
+):
     blocks = sums_out.shape[0]
-    table = blocks + tail_blocks
+    mine = []
     for block in range(blocks):
         first = side_table(even_side, block)
         second = side_table(odd_side, block)
-        before, after = neighbours(peers, info[0], first, second)
-        three = (before, side_table(own, block), after)
-        for side, points in enumerate(three):
+        before, following = neighbours(peers, info[0], first, second)
+        mine.append(side_table(own, block))
+        for side, points in enumerate((before, mine[block], following)):
             left, sums = other_features(points)
             left_ref[side * blocks + block] = left
             sums_ref[side * blocks + block] = sums
+            tables[side * blocks + block] = points
     left_ref[3 * blocks] = jnp.zeros(left_ref.shape[1:], BF16)
     sums_ref[3 * blocks] = jnp.zeros(sums_ref.shape[1:], BF16)
-    found = jnp.int32(0)
-    mine, totals, places, weights = {}, {}, {}, {}
+    tables[3 * blocks] = jnp.zeros(tables.shape[1:], F32)
+    totals, places, weights = {}, {}, {}
     units = blocks * members
+
     for unit in range(units + LAG):
         if unit < units:
             block, k = divmod(unit, members)
             if k == 0:
-                mine[block] = own_features(side_table(own, block))
-            member = family[k, block]
-            side = jnp.where(member >= table, 1, 0) + jnp.where(member >= 2 * table, 1, 0)
-            local = member - side * table
-            outside = local >= blocks
-            pairs[1 + found] = (block << PAIR_SHIFT) + member
-            found = found + jnp.where(outside & (member < 3 * table), 1, 0)
-            places[unit] = jnp.where(outside, 3 * blocks, side * blocks + local)
-            weights[unit] = pair_weights(left_ref[places[unit]], mine[block])
+                features = own_features(mine[block])
+            code = codes[k, block]
+            places[unit] = low_bits(code)
+            weights[unit] = pair_weights(left_ref[places[unit]], features)
         if unit >= LAG:
             done = unit - LAG
             block, k = divmod(done, members)
@@ -286,9 +329,24 @@
             totals[block] = total if k == 0 else totals[block] + total
             if k == members - 1:
                 sums_out[block] = fold(totals.pop(block))
-    for extra in range(BATCH):
-        pairs[1 + found + extra] = 3 * table
-    pairs[0] = (found + BATCH - 1) // BATCH
+
+
+def list_tail_pairs(flat, pairs, tail_blocks):
+    row = flat[...]
+    count = row.shape[1]
+    slots = pairs.shape[1]
+    flags = (row >> (2 * PAIR_SHIFT)).astype(F32)
+    entry = (row & ((1 << (2 * PAIR_SHIFT)) - 1)).astype(F32)
+    down, across = iota((count, count), 0), iota((count, count), 1)
+    wide = jnp.broadcast_to(flags, (count, count))
+    rank = jnp.sum(jnp.where(across < down, wide, 0.0), axis=1, keepdims=True)
+    mine = jnp.sum(jnp.where(across == down, wide, 0.0), axis=1, keepdims=True)
+    lane = iota((count, slots), 1).astype(F32)
+    listed = dot3(entry, one_hot((rank == lane) & (mine > 0.5)))
+    found = jnp.sum(flags, axis=1, keepdims=True)
+    slot = iota((1, slots), 1)
+    listed = jnp.where(slot.astype(F32) < found, listed, 3.0 * tail_blocks).astype(jnp.int32)
+    pairs[...] = jnp.where(slot == slots - 1, found.astype(jnp.int32), listed)
 
 
 def stiffness_rows(stiffness):
@@ -325,57 +383,58 @@
     return total + jnp.where(iota(total.shape, 1) != 0, turned, 0.0)
 
 
+def put_nodes(nodes, at, ny, fields, halves):
+    for comp, value in enumerate(fields):
+        shifted = ahead(value)
+        for half, part in enumerate(halves):
+            nodes[half, pl.ds(at + comp, ny, stride=8), :] = value[:, part]
+            nodes[half, pl.ds(at + comp + 4, ny, stride=8), :] = shifted[:, part]
+
+
+def take_tile(ref, at):
+    return jnp.concatenate([ref[h, at : at + 8, :] for h in range(ref.shape[0])], axis=1)
+
+
+def put_tile(ref, at, value):
+    for half in range(ref.shape[0]):
+        ref[half, at : at + 8, :] = value[:, half * BLOCK : (half + 1) * BLOCK]
+
+
+def take_rows(ref, at, count):
+    return jnp.concatenate([ref[h, pl.ds(at, count, stride=8), :] for h in range(ref.shape[0])], axis=1)
+
+
 def rock_kernel(
-    depth,
-    info,
+    tail_blocks,
+    flat,
     fem_disp,
     fem_vel,
     modulus,
     inv_mass,
     stiffness,
-    low_x,
-    high_x,
-    after,
     out,
     edge_nodes,
     left_out,
-    nodes,
     first_ref,
     second_ref,
+    pairs,
+    nodes,
     force_ref,
 ):
     nx, ny, nz = modulus.shape
-    low_on = jnp.where(info[1] > 0, 1.0, 0.0)
-    high_on = jnp.where(info[1] < depth - 1, 1.0, 0.0)
+    list_tail_pairs(flat, pairs, tail_blocks)
     halves = [slice(h * BLOCK, (h + 1) * BLOCK) for h in range(nz // BLOCK)]
     left = stiffness_rows(stiffness[...])
     left_out[...] = left
-    for x in range(nx + 2):
-        for comp in range(4):
-            if x == 0:
-                value = low_x[comp, 0:ny] * low_on
-            elif x == nx + 1:
-                value = high_x[comp, 0:ny] * high_on
-            else:
-                value = fem_disp[comp, x - 1] if comp < 3 else modulus[x - 1]
-            at = x * ny * 8 + comp
-            shifted = ahead(value)
-            for half, part in enumerate(halves):
-                nodes[half, pl.ds(at, ny, stride=8), :] = value[:, part]
-                nodes[half, pl.ds(at + 4, ny, stride=8), :] = shifted[:, part]
-
-    def node_row(x, y):
-        at = (x * ny + y) * 8
-        return jnp.concatenate([nodes[h, at : at + 8, :] for h in range(len(halves))], axis=1)
-
-    for x in range(nx + 2):
+    for x in range(nx):
+        put_nodes(nodes, x * ny * 8, ny, [fem_disp[0, x], fem_disp[1, x], fem_disp[2, x], modulus[x]], halves)
+    for x in range(nx):
         for y in range(ny):
-            node = node_row(x, y)
+            at = x * ny + y
+            node = take_tile(nodes, 8 * at)
             if y in (0, ny - 1):
                 edge_nodes[0 if y == 0 else 1, x] = node
-            first, second = node_parts(node)
-            first_ref[x * ny + y] = first
-            second_ref[x * ny + y] = second
+            first_ref[at], second_ref[at] = node_parts(node)
 
     def element(x, y):
         pieces = []
@@ -383,29 +442,94 @@
             for b in range(2):
                 at = (x + a) * ny + y + b
                 pieces += [first_ref[at], first_ref[at], second_ref[at]]
-        return dot(left, jnp.concatenate(pieces, axis=0)) * node_row(x, y)[3:4]
+        return dot(left, jnp.concatenate(pieces, axis=0)) * take_tile(nodes, 8 * (x * ny + y))[3:4]
 
     before = None
-    for x in range(nx + 1):
-        line = [element(x, y) for y in range(ny - 1)]
-        if x > 0:
-            for y in range(ny):
-                terms = []
-                if y < ny - 1:
-                    terms += [line[y][0:8], before[y][16:24]]
-                if y > 0:
-                    terms += [line[y - 1][8:16], before[y - 1][24:32]]
-                total = gathered_force(sum(terms[1:], terms[0]))
-                at = ((x - 1) * ny + y) * 8
-                for half, part in enumerate(halves):
-                    force_ref[half, at : at + 8, :] = total[:, part]
+    for x in range(nx):
+        line = [element(x, y) for y in range(ny - 1)] if x < nx - 1 else None
+        for y in range(ny):
+            terms = []
+            if line and y < ny - 1:
+                terms.append(line[y][0:8])
+            if line and y > 0:
+                terms.append(line[y - 1][8:16])
+            if before and y < ny - 1:
+                terms.append(before[y][16:24])
+            if before and y > 0:
+                terms.append(before[y - 1][24:32])
+            put_tile(force_ref, (x * ny + y) * 8, gathered_force(sum(terms[1:], terms[0])))
         before = line
     for x in range(nx):
         for comp in range(3):
-            force = jnp.concatenate(
-                [force_ref[h, pl.ds(x * ny * 8 + comp, ny, stride=8), :] for h in range(len(halves))], axis=1
-            )
+            force = take_rows(force_ref, x * ny * 8 + comp, ny)
             out[comp, x] = fem_vel[comp, x] - HALF * inv_mass[x] * force
+
+
+def outer_kernel(
+    depth,
+    info,
+    rock,
+    inv_mass,
+    modulus,
+    left_in,
+    first_in,
+    second_in,
+    low_x,
+    high_x,
+    after,
+    out,
+    edge_nodes,
+    nodes,
+    first_ref,
+    second_ref,
+    force_ref,
+):
+    nx, ny, nz = inv_mass.shape
+    halves = [slice(h * BLOCK, (h + 1) * BLOCK) for h in range(nz // BLOCK)]
+    left = left_in[...]
+    on = (jnp.where(info[1] > 0, 1.0, 0.0), jnp.where(info[1] < depth - 1, 1.0, 0.0))
+    for side, face in enumerate((low_x, high_x)):
+        put_nodes(nodes, side * ny * 8, ny, [face[comp, 0:ny] * on[side] for comp in range(4)], halves)
+    for side in range(2):
+        for y in range(ny):
+            at = side * ny + y
+            node = take_tile(nodes, 8 * at)
+            if y in (0, ny - 1):
+                edge_nodes[0 if y == 0 else 1, side] = node
+            first_ref[at], second_ref[at] = node_parts(node)
+
+    def inner(y, side):
+        at = (nx - 1 if side else 0) * ny + y
+        return first_in[at], second_in[at]
+
+    def outer(y, side):
+        return first_ref[side * ny + y], second_ref[side * ny + y]
+
+    for side in range(2):
+        line = []
+        for y in range(ny - 1):
+            pieces = []
+            for a in range(2):
+                for b in range(2):
+                    first, second = (inner if a != side else outer)(y + b, side)
+                    pieces += [first, first, second]
+            mod = modulus[nx - 1, y : y + 1] if side else take_tile(nodes, 8 * y)[3:4]
+            line.append(dot(left, jnp.concatenate(pieces, axis=0)) * mod)
+        start = 0 if side else 16
+        for y in range(ny):
+            terms = []
+            if y < ny - 1:
+                terms.append(line[y][start : start + 8])
+            if y > 0:
+                terms.append(line[y - 1][start + 8 : start + 16])
+            put_tile(force_ref, (side * ny + y) * 8, gathered_force(sum(terms[1:], terms[0])))
+    for x in range(nx):
+        for comp in range(3):
+            value = rock[comp, x]
+            if x in (0, nx - 1):
+                side = 0 if x == 0 else 1
+                value = value - HALF * inv_mass[x] * take_rows(force_ref, side * ny * 8 + comp, ny)
+            out[comp, x] = value
 
 
 def received(ref, peers, blocks, place, odd, wanted, row, pick):
@@ -428,11 +552,17 @@
     tails = [pltpu.roll(part, CAP * odd, 1) for part in gathered]
     rows = peers // 2 * blocks
     hit = (iota((rows, pick.shape[1]), 0) == row) & wanted
+    looked = dot3(ref[:, 0:base, :].reshape(peers // 2 * base, BLOCK), pick)
+    looked = looked.reshape(peers // 2, base, pick.shape[1])
     values = []
     for comp in range(3):
-        got = dot3(ref[:, comp * blocks : (comp + 1) * blocks, :].reshape(rows, BLOCK), pick)
+        got = looked[:, comp * blocks : (comp + 1) * blocks, :].reshape(rows, pick.shape[1])
         values.append(jnp.sum(jnp.where(hit, got, 0.0), axis=0, keepdims=True))
     return tails, values
+
+
+def entry_rows(side, blocks, count):
+    return side[4 * blocks : 4 * blocks + 8, 0:count]
 
 
 def entry_places(entry, blocks):
@@ -448,10 +578,11 @@
     blocks,
     info,
     mine_in,
-    entries,
+    own_side,
     rock,
     inv_mass,
     edge_nodes,
+    outer_nodes,
     left_in,
     low_x,
     high_x,
@@ -465,7 +596,7 @@
     place = info[0]
     core = place & 1
     even = core == 0
-    entry = entries[...]
+    entry = entry_rows(own_side, blocks, values_out.shape[1])
     odd_owner, row, pick = entry_places(entry, blocks)
     tails, values = received(mine_in, peers, blocks, place, core, odd_owner == core, row, pick)
     for side in range(3):
@@ -485,7 +616,7 @@
             else:
                 value = jnp.where(from_even, halo_rows(even_side, x - 1), halo_rows(odd_side, x - 1))
             other = jnp.concatenate([value, ahead(value)], axis=0)
-            node = edge_nodes[edge, x]
+            node = outer_nodes[edge, x // (nx + 1)] if x in (0, nx + 1) else edge_nodes[edge, x - 1]
             lower.append((other if edge == 0 else node)[3:4])
             inner.append(node_parts(node))
             outer.append(node_parts(other))
@@ -514,22 +645,22 @@
     members,
     info,
     pairs,
-    family,
+    codes,
     mate_in,
-    entries,
+    own_side,
     rock,
     inv_mass,
     tails_in,
     values_in,
     sums_in,
-    own,
-    even_side,
-    odd_side,
+    tables,
     pd_vel,
     fem_out,
     pd_out,
-    table_ref,
     sums_ref,
+    own,
+    tail_left,
+    tail_sums,
 ):
     nx, ny, nz = inv_mass.shape
     width = peers * CAP
@@ -539,41 +670,44 @@
     place = info[0]
     core = place & 1
     for block in range(blocks):
-        first = side_table(even_side, block)
-        second = side_table(odd_side, block)
-        before, after = neighbours(peers, place, first, second)
-        table_ref[block] = before
-        table_ref[table + block] = side_table(own, block)
-        table_ref[2 * table + block] = after
         sums_ref[block] = sums_in[block]
-    table_ref[3 * table] = jnp.zeros((8, BLOCK), F32)
-
-    entry = entries[...]
-    count = entry.shape[1]
+        own[block] = tables[blocks + block]
+
+    count = values_in.shape[1]
+    entry = entry_rows(own_side, blocks, count)
     odd_owner, row, pick = entry_places(entry, blocks)
     tails, values = received(mate_in, peers, blocks, place, 1 - core, odd_owner != core, row, pick)
     tails = [tails[side] + tails_in[side] for side in range(3)]
     on = (jnp.where(place > 0, 1.0, 0.0), 1.0, jnp.where(place < peers - 1, 1.0, 0.0))
     for side in range(3):
         for tile in range(tail_blocks):
-            part = tails[side][0:8, tile * BLOCK : (tile + 1) * BLOCK]
-            table_ref[side * table + blocks + tile] = part * on[side]
+            points = tails[side][0:8, tile * BLOCK : (tile + 1) * BLOCK] * on[side]
+            tail_left[side * tail_blocks + tile], tail_sums[side * tail_blocks + tile] = other_features(points)
+            if side == 1:
+                own[blocks + tile] = points
+    tail_left[3 * tail_blocks] = jnp.zeros(tail_left.shape[1:], BF16)
+    tail_sums[3 * tail_blocks] = jnp.zeros(tail_sums.shape[1:], BF16)
     tail_rows = tails[1]
 
-    def several(codes):
+    for tile in range(tail_blocks):
+        block = blocks + tile
+        features = own_features(own[block])
         ready = []
-        for block, member in codes:
-            left, sums = other_features(table_ref[member])
-            ready.append((block, sums, pair_weights(left, own_features(table_ref[table + block]))))
-        return [(block, fold(weighted(sums, weights))) for block, sums, weights in ready]
-
-    for block in range(blocks, table):
-        results = several([(block, family[k, block]) for k in range(members)])
-        sums_ref[block] = sum((total for _, total in results[1:]), results[0][1])
+        for k in range(members):
+            left, rows = other_features(tables[low_bits(codes[k, block])])
+            ready.append((rows, pair_weights(left, features)))
+        results = [weighted(rows, weights) for rows, weights in ready]
+        sums_ref[block] = fold(sum(results[1:], results[0]))
 
     def some(index, carry):
-        codes = [pairs[1 + BATCH * index + k] for k in range(BATCH)]
-        for block, total in several([(code >> PAIR_SHIFT, code & ((1 << PAIR_SHIFT) - 1)) for code in codes]):
+        ready = []
+        for k in range(BATCH):
+            code = pairs[0, BATCH * index + k]
+            block, number = code >> PAIR_SHIFT, low_bits(code)
+            weights = pair_weights(tail_left[number], own_features(own[block]))
+            ready.append((block, tail_sums[number], weights))
+        results = [(block, fold(weighted(rows, weights))) for block, rows, weights in ready]
+        for block, total in results:
             sums_ref[block] = sums_ref[block] + total
         return carry
 
@@ -591,8 +725,7 @@
     target = tail_rows[15:16].astype(jnp.int32)
     hot_lane = one_hot(iota((BLOCK, width), 0) == (target & (BLOCK - 1)))
     target_block = target >> shift_of(BLOCK)
-    tables = jnp.concatenate([side_table(own, block) for block in range(blocks)], axis=0)
-    looked = dot3(tables, hot_lane)
+    looked = dot3(tables[blocks : 2 * blocks].reshape(blocks * 8, BLOCK), hot_lane)
     found = jnp.zeros((8, width), F32)
     for block in range(blocks):
         found = found + jnp.where(target_block == block, looked[8 * block : 8 * block + 8], 0.0)
@@ -601,12 +734,12 @@
     spread = jnp.concatenate([jnp.where(target_block == block, coupling, 0.0) for block in range(blocks)], axis=0)
     couple = dot3_nt(spread, hot_lane)
 
-    lax.fori_loop(0, pairs[0], some, 0)
+    lax.fori_loop(0, (pairs[0, PAIR_SLOTS - 1] + BATCH - 1) // BATCH, some, 0)
 
     scale = GAIN / (BLOCK * members)
     for block in range(table):
         total = sums_ref[block]
-        points = table_ref[table + block]
+        points = own[block]
         part = slice(block * BLOCK, (block + 1) * BLOCK)
         force = scale * points[3:4] * (total[0:3] - points[0:3] * total[3:4])
         if block < blocks:
@@ -661,54 +794,76 @@
 
     both_faces = depth > 2
     family = family.T
-    sources = (fem_disp, modulus, pd_pos, pd_disp)
-    pay_even, pay_odd = call(
-        side_kernel,
-        (shaped((4 * blocks, nz), F32),) * 2,
-        [FAR] * 4,
-        [pltpu.VMEM(value.shape, value.dtype) for value in sources] + [pltpu.SemaphoreType.DMA((4,))],
-        1.5,
-        sources,
-        "side",
+    inputs = (
+        ov_node.reshape(1, -1),
+        fem_disp,
+        conv_owner.reshape(1, -1),
+        ov_owner.reshape(1, -1),
+        conv_state,
+        ov_target.reshape(1, -1),
+        ov_stiff.reshape(1, -1),
+        pd_disp,
+        pd_pos,
+        modulus,
+    )
+    chunk, pay_even, pay_odd = call(
+        functools.partial(pack_kernel, peers),
+        (
+            shaped((chips, chunk_rows, BLOCK), F32),
+            shaped((4 * blocks + 8, nz), F32),
+            shaped((4 * blocks, nz), F32),
+        ),
+        [FAR] * 10,
+        [pltpu.VMEM((chunk_rows, BLOCK), F32)]
+        + [pltpu.VMEM(value.shape, value.dtype) for value in inputs]
+        + [pltpu.SemaphoreType.DMA((10,))],
+        2.6,
+        inputs,
+        "pack",
         vmem=SIDE_VMEM,
     )
     swap = [(i, i ^ 1) for i in range(peers)]
     cross = [(i, i + 1) for i in range(1, peers - 1, 2)] + [(i + 1, i) for i in range(1, peers - 1, 2)]
     odd_side = lax.ppermute(pay_odd, "lat", cross)
     even_side = lax.ppermute(pay_even, "lat", swap)
-    inputs = (
-        fem_disp,
-        pd_disp,
-        conv_state,
-        conv_owner.reshape(1, -1),
-        ov_owner.reshape(1, -1),
-        ov_node.reshape(1, -1),
-        ov_target.reshape(1, -1),
-        ov_stiff.reshape(1, -1),
-    )
-    chunk, entries = call(
-        functools.partial(pack_kernel, peers),
-        (shaped((chips, chunk_rows, BLOCK), F32), shaped((8, count), F32)),
-        [VMEM] * 8,
-        [pltpu.VMEM((chunk_rows, BLOCK), F32)],
-        2.0,
-        inputs,
-        "pack",
-    )
-    chunk, even_side, odd_side = lax.optimization_barrier((chunk, even_side, odd_side))
     groups = [[side + 2 * k for k in range(chips)] for side in range(2)]
     mine = lax.all_to_all(chunk, "lat", split_axis=0, concat_axis=0, tiled=True, axis_index_groups=groups)
 
+    node_count = nx * ny
+    codes = member_codes(family, blocks, tail_blocks)
+    block_of = jnp.arange(table, dtype=jnp.int32)[None, :]
+    flat = codes >> PAIR_SHIFT
+    flat = ((flat >> PAIR_SHIFT) << (2 * PAIR_SHIFT)) + (block_of << PAIR_SHIFT) + low_bits(flat)
+    rock, edge_nodes, left, first_parts, second_parts, pairs = call(
+        functools.partial(rock_kernel, tail_blocks),
+        (
+            shaped(fem_vel.shape, F32),
+            shaped((2, nx, 8, nz), F32),
+            shaped((32, 192), BF16),
+            shaped((node_count, 16, nz), BF16),
+            shaped((node_count, 16, nz), BF16),
+            shaped((1, PAIR_SLOTS), jnp.int32),
+        ),
+        [VMEM] * 6,
+        [
+            pltpu.VMEM((nz // BLOCK, node_count * 8, BLOCK), F32),
+            pltpu.VMEM((nz // BLOCK, node_count * 8, BLOCK), F32),
+        ],
+        1.2,
+        (flat.reshape(1, -1), fem_disp, fem_vel, modulus, inv_mass, element_stiffness),
+        "rock",
+    )
     count_faces = 2 if both_faces else 1
-    faces = call(
-        functools.partial(face_kernel, both_faces),
-        shaped((count_faces, 4, ny + 2, nz), F32),
-        [SMEM] + [VMEM] * 4,
-        [],
-        0.6,
-        (info, fem_disp, modulus, even_side, odd_side),
-        "face",
-    )
+    rows = jnp.stack([even_side[: 4 * blocks], odd_side]).reshape(2, blocks // 2, 2, 4, nz)[:, :, :, 3]
+    rows = rows.reshape(2, blocks, nz)[:, : 4 * nx].reshape(2, nx, 4, nz)
+    even = (info[0] & 1) == 0
+    ends = jnp.stack([jnp.where(even, rows[1], rows[0]), jnp.where(even, rows[0], rows[1])], axis=2)
+    own = jnp.concatenate([fem_disp, modulus[None]], axis=0)
+    layers = [jnp.concatenate([own[:, x], ends[x]], axis=1) for x in (0, nx - 1)]
+    if both_faces:
+        faces = jnp.stack(layers)
+    else:
+        faces = jnp.where(info[1] == 0, layers[1], layers[0])[None]
     faces, pay_even, even_side, odd_side = lax.optimization_barrier((faces, pay_even, even_side, odd_side))
     if both_faces:
         low_x = lax.ppermute(faces[1], "depth", [(i, i + 1) for i in range(depth - 1)])
@@ -716,64 +871,55 @@
     else:
         low_x = high_x = lax.ppermute(faces[0], "depth", [(0, 1), (1, 0)])
 
-    sums, pairs = call(
+    sums, tables = call(
         functools.partial(bond_kernel, peers, tail_blocks, members),
-        (shaped((blocks, 8, BLOCK), F32), shaped((table * members + BATCH + 1,), jnp.int32)),
+        (
+            shaped((blocks, 8, BLOCK), F32),
+            shaped((3 * blocks + 1, 8, BLOCK), F32),
+        ),
         [SMEM, SMEM] + [VMEM] * 3 + [ANY],
         [pltpu.VMEM((3 * blocks + 1, BLOCK, 48), BF16), pltpu.VMEM((3 * blocks + 1, 32, BLOCK), BF16)],
         4.3,
-        (info, family, pay_even, even_side, odd_side, faces),
+        (info, codes, pay_even, even_side, odd_side, faces),
         "bond",
-        out_specs=(VMEM, SMEM),
-    )
-    node_rows = (nx + 2) * ny
-    rock, edge_nodes, left = call(
-        functools.partial(rock_kernel, depth),
-        (shaped(fem_vel.shape, F32), shaped((2, nx + 2, 8, nz), F32), shaped((32, 192), BF16)),
-        [SMEM] + [VMEM] * 7 + [ANY],
+    )
+    mine, sums, low_x, high_x = lax.optimization_barrier((mine, sums, low_x, high_x))
+    mate = lax.ppermute(mine, "lat", swap)
+    rock, outer_nodes = call(
+        functools.partial(outer_kernel, depth),
+        (shaped(fem_vel.shape, F32), shaped((2, 2, 8, nz), F32)),
+        [SMEM] + [VMEM] * 8 + [ANY],
         [
-            pltpu.VMEM((nz // BLOCK, node_rows * 8, BLOCK), F32),
-            pltpu.VMEM((node_rows, 16, nz), BF16),
-            pltpu.VMEM((node_rows, 16, nz), BF16),
-            pltpu.VMEM((nz // BLOCK, nx * ny * 8, BLOCK), F32),
+            pltpu.VMEM((nz // BLOCK, 2 * ny * 8, BLOCK), F32),
+            pltpu.VMEM((2 * ny, 16, nz), BF16),
+            pltpu.VMEM((2 * ny, 16, nz), BF16),
+            pltpu.VMEM((nz // BLOCK, 2 * ny * 8, BLOCK), F32),
         ],
-        1.8,
-        (info, fem_disp, fem_vel, modulus, inv_mass, element_stiffness, low_x, high_x, sums),
-        "rock",
-    )
-    mine, rock = lax.optimization_barrier((mine, rock))
-    mate = lax.ppermute(mine, "lat", swap)
+        0.8,
+        (info, rock, inv_mass, modulus, left, first_parts, second_parts, low_x, high_x, sums),
+        "outer",
+    )
     rock, tails, values = call(
         functools.partial(edge_kernel, peers, depth, blocks),
         (shaped(fem_vel.shape, F32), shaped((3, 16, peers * CAP), F32), shaped((8, count), F32)),
-        [SMEM] + [VMEM] * 10,
+        [SMEM] + [VMEM] * 11,
         [],
         1.0,
-        (info, mine, entries, rock, inv_mass, edge_nodes, left, low_x, high_x, even_side, odd_side),
+        (info, mine, pay_even, rock, inv_mass, edge_nodes, outer_nodes, left, low_x, high_x, even_side, odd_side),
         "edge",
     )
     return call(
         functools.partial(final_kernel, peers, members),
         (shaped(fem_vel.shape, F32), shaped((3, table * BLOCK), F32)),
-        [SMEM] * 3 + [VMEM] * 11,
-        [pltpu.VMEM((3 * table + 1, 8, BLOCK), F32), pltpu.VMEM((table, 8, BLOCK), F32)],
+        [SMEM] * 3 + [VMEM] * 9,
+        [
+            pltpu.VMEM((table, 8, BLOCK), F32),
+            pltpu.VMEM((table, 8, BLOCK), F32),
+            pltpu.VMEM((3 * tail_blocks + 1, BLOCK, 48), BF16),
+            pltpu.VMEM((3 * tail_blocks + 1, 32, BLOCK), BF16),
+        ],
         2.6,
-        (
-            info,
-            pairs,
-            family,
-            mate,
-            entries,
-            rock,
-            inv_mass,
-            tails,
-            values,
-            sums,
-            pay_even,
-            even_side,
-            odd_side,
-            pd_vel,
-        ),
+        (info, pairs, codes, mate, pay_even, rock, inv_mass, tails, values, sums, tables, pd_vel),
         "final",
     )
 

time: 28.9 us -> 28.4 us (0.983)
  waiting for transfers between devices: 0.89 us -> 3.13 us
  Pallas kernels: 13.1 us -> 11.5 us
  starting transfers between devices: 13 us -> 11.6 us
    ppermute x1, starting transfers between devices: 4.39 us -> 0.52 us  [shards(): even_side = lax.ppermute(pay_even, 'lat', swap)]
    all_to_all x1, waiting for transfers between devices: 0.35 us -> 3.11 us  [shards(): lax.all_to_all(chunk, 'lat', split_axis=0, concat_axis=0, tiled=True, axi...]
    all_to_all x1, starting transfers between devices: 6.38 us -> 8.84 us  [shards(): lax.all_to_all(chunk, 'lat', split_axis=0, concat_axis=0, tiled=True, axi...]
    pallas_call x7 -> x6, Pallas kernels: 13.1 us -> 11.5 us  [call(): pl.pallas_call(kernel, out_shape=outs, in_specs=specs, out_specs=out_spec...]
    ppermute x1, waiting for transfers between devices: 0.53 us -> 0.01 us  [shards(): mate = lax.ppermute(mine, 'lat', swap)]
    unnamed x30 -> x16, local copies, waits for them, and re-layouts: 0.72 us -> 0.7 us
  transfers between devices with their start and end apart: 5 -> 5, of which waited for: 2 -> 1; matrix products, arithmetic and copies ran while one was open for 0% -> 1% of each run, Pallas kernels for 31% -> 24%
where the time goes in v3:
time: 28.4 us; the launch traced here: 28.1 us
  starting transfers between devices  11.6 us (41%)
  Pallas kernels  11.5 us (40%)
  waiting for transfers between devices  3.13 us (11%)
  between operations  0.84 us (3%)
  local copies, waits for them, and re-layouts  0.83 us (3%)
    pallas_call x6, Pallas kernels, call(): pl.pallas_call(kernel, out_shape=outs, in_specs=specs, out_specs=out_spec...  11.5 us
    all_to_all x1, starting transfers between devices, shards(): lax.all_to_all(chunk, 'lat', split_axis=0, concat_axis=0, tiled=True, axi...  8.84 us
    all_to_all x1, waiting for transfers between devices, shards(): lax.all_to_all(chunk, 'lat', split_axis=0, concat_axis=0, tiled=True, axi...  3.11 us
    ppermute x1, starting transfers between devices, shards(): low_x = high_x = lax.ppermute(faces[0], 'depth', [(0, 1), (1, 0)])  1.55 us
    unnamed x16, local copies, waits for them, and re-layouts  0.7 us
    ppermute x1, starting transfers between devices, shards(): odd_side = lax.ppermute(pay_odd, 'lat', cross)  0.65 us
  transfers between devices with their start and end apart: 5, of which 1 were waited for; matrix products, arithmetic and copies ran while one was open for 1% of the time, Pallas kernels for 24%

profile of v3, /device:TPU:0, one launch (start us, length us, event | category | flops | bytes accessed | tf_op | source)
XLA Modules:
  0.0 28.1 jit_solution(4231043173342208952)
XLA Ops:
  0.6 2.1 %pack.1 = (f32[8,64,128]{2,1,0:T(8,128)}, f32[72,256]{1,0:T(8,128)}, f32[64,256]{1,0:T(8,128)}) custom-call(s32[1,64]{1,0:T(1,128)} %bitcast.34, f32[3,4,8,256]{3,2,1,0:T(8,128)} %fem_disp_in.1, s32[1,64]{1,0:T(1,128)} %bitcast.35, s32[1,64]{1,0:T(1,128)} %bitcast.36, f32[9,64]{1,0:T(8,128)} %conv_state_in.1, s32[1,64]{1,0:T(1,128)} %bitcast.37, ...), custom_call_target="tpu_custom_call" | custom-call | bytes 9360000 | tf_op jit(solution)/shard_map/pack/pallas_call | solution.py:753
  2.7 0.5 %collective-permute-start.1 = (f32[72,256]{1,0:T(8,128)}, f32[72,256]{1,0:T(8,128)S(1)}, u32[]{:S(2)}, u32[]{:S(2)}) collective-permute-start(f32[72,256]{1,0:T(8,128)} %get-tuple-element.30.own.own_side), channel_id=1, source_target_pairs={{0,1},{1,0},{2,3},{3,2},{4,5},{5,4},{6,7},{7,6},{8,9},{9,8},{10,11... | collective-permute-start | bytes 221192 | tf_op jit(solution)/shard_map/ppermute | solution.py:828
  3.2 0.7 %collective-permute-start = (f32[64,256]{1,0:T(8,128)}, f32[64,256]{1,0:T(8,128)S(1)}, u32[]{:S(2)}, u32[]{:S(2)}) collective-permute-start(f32[64,256]{1,0:T(8,128)} %get-tuple-element.28), channel_id=1, source_target_pairs={{1,2},{3,4},{5,6},{7,8},{9,10},{11,12},{13,14},{2,1},{4,3},{6,5},{... | collective-permute-start | bytes 196616 | tf_op jit(solution)/shard_map/ppermute | solution.py:827
  3.9 0.0 copy-start
  3.9 0.0 copy-start.3
  3.9 8.8 %all-to-all-start = ((f32[8,64,128]{2,1,0:T(8,128)}), f32[8,64,128]{2,1,0:T(8,128)S(1)}, u32[]{:S(2)}, u32[]{:S(2)}) async-start(f32[8,64,128]{2,1,0:T(8,128)} %get-tuple-element.27), calls=%async_computation | async-start | bytes 524288 | tf_op jit(solution)/shard_map/all_to_all | solution.py:830
  12.8 0.0 copy-start.7
  12.8 0.7 %copy-done.7 = s32[17,8]{0,1:T(8,128)S(1)} copy-done((s32[17,8]{0,1:T(8,128)S(1)}, s32[17,8]{0,1:T(8,128)}, u32[]{:S(2)}) %copy-start.7) | copy-done | bytes 568
  13.5 0.0 collective-permute-done.odd_side
  13.5 0.0 collective-permute-done.1.even_side
  13.6 0.0 copy-start.1
  13.7 1.6 %collective-permute-start.2 = (f32[4,10,256]{2,1,0:T(8,128)S(1)}, f32[4,10,256]{2,1,0:T(8,128)S(1)}, u32[]{:S(2)}, u32[]{:S(2)}) collective-permute-start(f32[4,10,256]{2,1,0:T(8,128)S(1)} %bitcast.31), channel_id=1, source_target_pairs={{0,16},{16,0},{1,17},{17,1},{2,18},{18,2},{3,19},{19,3},{4,20},{20... | collective-permute-start | bytes 122888 | tf_op jit(solution)/shard_map/ppermute | solution.py:872
  15.2 0.1 pad_add_fusion.info
  15.3 3.5 %bond.1 = (f32[16,8,128]{2,1,0:T(8,128)S(1)}, f32[49,8,128]{2,1,0:T(8,128)S(1)}) custom-call(s32[2]{0:T(128)S(1)} %pad_add_fusion.info, s32[8,17]{1,0:T(8,128)S(1)} %get-tuple-element.54.codes, f32[72,256]{1,0:T(8,128)S(1)} %copy-done.1, f32[72,256]{1,0:T(8,128)S(1)} %collective-permute-done.1.even_side, f32[64,256]{1,0:T(8,128)S(1)} %collective-permute-done.odd_side, ...), custom_call_target="tpu_custom_call" | custom-call | bytes 15480000 | tf_op jit(solution)/shard_map/bond/pallas_call | solution.py:753
  18.8 0.0 collective-permute-done.2.low_x.high_x
  18.8 3.1 %all-to-all-done.mine_in = f32[8,64,128]{2,1,0:T(8,128)S(1)} async-done(((f32[8,64,128]{2,1,0:T(8,128)}), f32[8,64,128]{2,1,0:T(8,128)S(1)}, u32[]{:S(2)}, u32[]{:S(2)}) %all-to-all-start) | async-done | bytes 262176 | tf_op jit(solution)/shard_map/all_to_all | solution.py:830
  21.9 0.0 collective-permute-start.3
  21.9 0.1 reshape.127.flat
  22.0 1.3 %rock.1 = (f32[3,4,8,256]{3,2,1,0:T(8,128)S(1)}, f32[2,4,8,256]{3,2,1,0:T(8,128)S(1)}, bf16[32,192]{1,0:T(8,128)(2,1)S(1)}, bf16[32,16,256]{2,1,0:T(8,128)(2,1)S...) custom-call(s32[1,136]{1,0:T(1,128)S(1)} %reshape.127.flat, f32[3,4,8,256]{3,2,1,0:T(8,128)S(1)} %copy-done, ...), custom_call_target="tpu_custom_call" | custom-call | bytes 4320000 | tf_op jit(solution)/shard_map/rock/pallas_call | solution.py:753
  23.3 1.1 %outer.1 = (f32[3,4,8,256]{3,2,1,0:T(8,128)S(1)}, f32[2,2,8,256]{3,2,1,0:T(8,128)S(1)}) custom-call(s32[2]{0:T(128)S(1)} %pad_add_fusion.info, f32[3,4,8,256]{3,2,1,0:T(8,128)S(1)} %get-tuple-element.36.rock, f32[4,8,256]{2,1,0:T(8,128)S(1)} %copy-done.2, f32[4,8,256]{2,1,0:T(8,128)S(1)} %copy-done.3, bf16[32,192]{1,0:T(8,128)(2,1)S(1)} %get-tuple-element.37.left_in, ...), custom_call_target="tpu_custom_call" | custom-call | bytes 2880000 | tf_op jit(solution)/shard_map/outer/pallas_call | solution.py:753
  24.4 0.0 copy-start.5
  24.4 1.0 %edge.1 = (f32[3,4,8,256]{3,2,1,0:T(8,128)S(1)}, f32[3,16,128]{2,1,0:T(8,128)S(1)}, f32[8,64]{1,0:T(8,128)S(1)}) custom-call(s32[2]{0:T(128)S(1)} %pad_add_fusion.info, f32[8,64,128]{2,1,0:T(8,128)S(1)} %all-to-all-done.mine_in, f32[72,256]{1,0:T(8,128)S(1)} %copy-done.1, f32[3,4,8,256]{3,2,1,0:T(8,128)S(1)} %get-tuple-element.43.rock, ...), custom_call_target="tpu_custom_call" | custom-call | bytes 3600000 | tf_op jit(solution)/shard_map/edge/pallas_call | solution.py:753
  25.4 0.0 collective-permute-done.3.mate_in
  25.4 2.6 %final.1 = (f32[3,4,8,256]{3,2,1,0:T(8,128)}, f32[3,2176]{1,0:T(4,128)}) custom-call(s32[2]{0:T(128)S(1)} %pad_add_fusion.info, s32[1,256]{1,0:T(1,128)S(1)} %get-tuple-element.26.pairs, s32[8,17]{1,0:T(8,128)S(1)} %get-tuple-element.54.codes, f32[8,64,128]{2,1,0:T(8,128)S(1)} %collective-permute-done.3.mate_in, f32[72,256]{1,0:T(8,128)S(1)} %copy-done.1, ...), custom_call_target="tpu_custom_call" | custom-call | bytes 9360000 | tf_op jit(solution)/shard_map/final/pallas_call | solution.py:753
  (18 shorter events, 0.2 us)
Async XLA Ops:
  2.7 10.8 %collective-permute-start.1 = (f32[72,256]{1,0:T(8,128)}, f32[72,256]{1,0:T(8,128)S(1)}, u32[]{:S(2)}, u32[]{:S(2)}) collective-permute-start(f32[72,256]{1,0:T(8,128)} %get-tuple-element.30.own.own_side), channel_id=1, source_target_pairs={{0,1},{1,0},{2,3},{3,2},{4,5},{5,4},{6,7},{7,6},{8,9},{9,8},{10,11... | collective-permute-start | bytes 221192 | tf_op jit(solution)/shard_map/ppermute | solution.py:828
  3.2 10.3 %collective-permute-start = (f32[64,256]{1,0:T(8,128)}, f32[64,256]{1,0:T(8,128)S(1)}, u32[]{:S(2)}, u32[]{:S(2)}) collective-permute-start(f32[64,256]{1,0:T(8,128)} %get-tuple-element.28), channel_id=1, source_target_pairs={{1,2},{3,4},{5,6},{7,8},{9,10},{11,12},{13,14},{2,1},{4,3},{6,5},{... | collective-permute-start | bytes 196616 | tf_op jit(solution)/shard_map/ppermute | solution.py:827
  3.9 8.9 %copy-start = (f32[3,4,8,256]{3,2,1,0:T(8,128)S(1)}, f32[3,4,8,256]{3,2,1,0:T(8,128)}, u32[]{:S(2)}) copy-start(f32[3,4,8,256]{3,2,1,0:T(8,128)} %fem_disp_in.1) | copy-start | bytes 294916
  3.9 8.9 %copy-start.3 = (f32[4,8,256]{2,1,0:T(8,128)S(1)}, f32[4,8,256]{2,1,0:T(8,128)}, u32[]{:S(2)}) copy-start(f32[4,8,256]{2,1,0:T(8,128)} %modulus.3) | copy-start | bytes 98308
  3.9 18.0 %all-to-all-start = ((f32[8,64,128]{2,1,0:T(8,128)}), f32[8,64,128]{2,1,0:T(8,128)S(1)}, u32[]{:S(2)}, u32[]{:S(2)}) async-start(f32[8,64,128]{2,1,0:T(8,128)} %get-tuple-element.27), calls=%async_computation | async-start | bytes 524288 | tf_op jit(solution)/shard_map/all_to_all | solution.py:830
  12.8 0.7 %copy-start.7 = (s32[17,8]{0,1:T(8,128)S(1)}, s32[17,8]{0,1:T(8,128)}, u32[]{:S(2)}) copy-start(s32[17,8]{0,1:T(8,128)} %param.25) | copy-start | bytes 1636
  13.6 1.7 %copy-start.1 = (f32[72,256]{1,0:T(8,128)S(1)}, f32[72,256]{1,0:T(8,128)}, u32[]{:S(2)}) copy-start(f32[72,256]{1,0:T(8,128)} %get-tuple-element.30.own.own_side) | copy-start | bytes 221188
  13.7 5.1 %collective-permute-start.2 = (f32[4,10,256]{2,1,0:T(8,128)S(1)}, f32[4,10,256]{2,1,0:T(8,128)S(1)}, u32[]{:S(2)}, u32[]{:S(2)}) collective-permute-start(f32[4,10,256]{2,1,0:T(8,128)S(1)} %bitcast.31), channel_id=1, source_target_pairs={{0,16},{16,0},{1,17},{17,1},{2,18},{18,2},{3,19},{19,3},{4,20},{20... | collective-permute-start | bytes 122888 | tf_op jit(solution)/shard_map/ppermute | solution.py:872
  15.3 6.7 %copy-start.2 = (f32[4,8,256]{2,1,0:T(8,128)S(1)}, f32[4,8,256]{2,1,0:T(8,128)}, u32[]{:S(2)}) copy-start(f32[4,8,256]{2,1,0:T(8,128)} %inv_mass.7) | copy-start | bytes 98308
  15.3 6.7 %copy-start.4 = (f32[3,4,8,256]{3,2,1,0:T(8,128)S(1)}, f32[3,4,8,256]{3,2,1,0:T(8,128)}, u32[]{:S(2)}) copy-start(f32[3,4,8,256]{3,2,1,0:T(8,128)} %fem_vel.1) | copy-start | bytes 294916
  15.3 6.7 %copy-start.6 = (f32[24,24]{1,0:T(8,128)S(1)}, f32[24,24]{1,0:T(8,128)}, u32[]{:S(2)}) copy-start(f32[24,24]{1,0:T(8,128)} %stiffness.1) | copy-start | bytes 6916
  21.9 3.5 %collective-permute-start.3 = (f32[8,64,128]{2,1,0:T(8,128)S(1)}, f32[8,64,128]{2,1,0:T(8,128)S(1)}, u32[]{:S(2)}, u32[]{:S(2)}) collective-permute-start(f32[8,64,128]{2,1,0:T(8,128)S(1)} %all-to-all-done.mine_in), channel_id=1, source_target_pairs={{0,1},{1,0},{2,3},{3,2},{4,5},{5,4},{6,7},{7,6},{8,9},{9,8},{10,11... | collective-permute-start | bytes 786440 | tf_op jit(solution)/shard_map/ppermute | solution.py:887
  24.4 1.1 %copy-start.5 = (f32[3,2048]{1,0:T(4,128)S(1)}, f32[3,2048]{1,0:T(4,128)}, u32[]{:S(2)}) copy-start(f32[3,2048]{1,0:T(4,128)} %pd_vel.1) | copy-start | bytes 73732

commit v4 on v3

--- a/solution.py
+++ b/solution.py
@@ -294,8 +294,9 @@
 
 
 def bond_kernel(
-    peers, tail_blocks, members, info, codes, own, even_side, odd_side, after, sums_out, tables, left_ref, sums_ref
+    peers, tail_blocks, members, info, codes, own, even_side, odd_side, flat, after, sums_out, tables, pairs, left_ref, sums_ref
 ):
+    list_tail_pairs(flat, pairs, tail_blocks)
     blocks = sums_out.shape[0]
     mine = []
     for block in range(blocks):
@@ -405,8 +406,6 @@
 
 
 def rock_kernel(
-    tail_blocks,
-    flat,
     fem_disp,
     fem_vel,
     modulus,
@@ -417,12 +416,10 @@
     left_out,
     first_ref,
     second_ref,
-    pairs,
     nodes,
     force_ref,
 ):
     nx, ny, nz = modulus.shape
-    list_tail_pairs(flat, pairs, tail_blocks)
     halves = [slice(h * BLOCK, (h + 1) * BLOCK) for h in range(nz // BLOCK)]
     left = stiffness_rows(stiffness[...])
     left_out[...] = left
@@ -834,23 +831,22 @@
     block_of = jnp.arange(table, dtype=jnp.int32)[None, :]
     flat = codes >> PAIR_SHIFT
     flat = ((flat >> PAIR_SHIFT) << (2 * PAIR_SHIFT)) + (block_of << PAIR_SHIFT) + low_bits(flat)
-    rock, edge_nodes, left, first_parts, second_parts, pairs = call(
-        functools.partial(rock_kernel, tail_blocks),
+    rock, edge_nodes, left, first_parts, second_parts = call(
+        rock_kernel,
         (
             shaped(fem_vel.shape, F32),
             shaped((2, nx, 8, nz), F32),
             shaped((32, 192), BF16),
             shaped((node_count, 16, nz), BF16),
             shaped((node_count, 16, nz), BF16),
-            shaped((1, PAIR_SLOTS), jnp.int32),
         ),
-        [VMEM] * 6,
+        [VMEM] * 5,
         [
             pltpu.VMEM((nz // BLOCK, node_count * 8, BLOCK), F32),
             pltpu.VMEM((nz // BLOCK, node_count * 8, BLOCK), F32),
         ],
         1.2,
-        (flat.reshape(1, -1), fem_disp, fem_vel, modulus, inv_mass, element_stiffness),
+        (fem_disp, fem_vel, modulus, inv_mass, element_stiffness),
         "rock",
     )
     count_faces = 2 if both_faces else 1
@@ -871,16 +867,17 @@
     else:
         low_x = high_x = lax.ppermute(faces[0], "depth", [(0, 1), (1, 0)])
 
-    sums, tables = call(
+    sums, tables, pairs = call(
         functools.partial(bond_kernel, peers, tail_blocks, members),
         (
             shaped((blocks, 8, BLOCK), F32),
             shaped((3 * blocks + 1, 8, BLOCK), F32),
+            shaped((1, PAIR_SLOTS), jnp.int32),
         ),
-        [SMEM, SMEM] + [VMEM] * 3 + [ANY],
+        [SMEM, SMEM] + [VMEM] * 4 + [ANY],
         [pltpu.VMEM((3 * blocks + 1, BLOCK, 48), BF16), pltpu.VMEM((3 * blocks + 1, 32, BLOCK), BF16)],
         4.3,
-        (info, codes, pay_even, even_side, odd_side, faces),
+        (info, codes, pay_even, even_side, odd_side, flat.reshape(1, -1), faces),
         "bond",
     )
     mine, sums, low_x, high_x = lax.optimization_barrier((mine, sums, low_x, high_x))

time: 28.4 us -> 28.1 us (0.989)
  waiting for transfers between devices: 3.13 us -> 2.81 us
    all_to_all x1, waiting for transfers between devices: 3.11 us -> 2.79 us  [shards(): lax.all_to_all(chunk, 'lat', split_axis=0, concat_axis=0, tiled=True, axi...]
  transfers between devices with their start and end apart: 5 -> 5, of which waited for: 1 -> 1; matrix products, arithmetic and copies ran while one was open for 1% -> 1% of each run, Pallas kernels for 24% -> 25%
where the time goes in v4:
time: 28.1 us; the launch traced here: 27.7 us
  starting transfers between devices  11.6 us (41%)
  Pallas kernels  11.5 us (41%)
  waiting for transfers between devices  2.81 us (10%)
  between operations  0.85 us (3%)
  local copies, waits for them, and re-layouts  0.84 us (3%)
    pallas_call x6, Pallas kernels, call(): pl.pallas_call(kernel, out_shape=outs, in_specs=specs, out_specs=out_spec...  11.5 us
    all_to_all x1, starting transfers between devices, shards(): lax.all_to_all(chunk, 'lat', split_axis=0, concat_axis=0, tiled=True, axi...  8.84 us
    all_to_all x1, waiting for transfers between devices, shards(): lax.all_to_all(chunk, 'lat', split_axis=0, concat_axis=0, tiled=True, axi...  2.79 us
    ppermute x1, starting transfers between devices, shards(): low_x = high_x = lax.ppermute(faces[0], 'depth', [(0, 1), (1, 0)])  1.55 us
    unnamed x16, local copies, waits for them, and re-layouts  0.71 us
    ppermute x1, starting transfers between devices, shards(): odd_side = lax.ppermute(pay_odd, 'lat', cross)  0.65 us
  transfers between devices with their start and end apart: 5, of which 1 were waited for; matrix products, arithmetic and copies ran while one was open for 1% of the time, Pallas kernels for 25%

profile of v4, /device:TPU:0, one launch (start us, length us, event | category | flops | bytes accessed | tf_op | source)
XLA Modules:
  0.0 27.7 jit_solution(7525025990365631740)
XLA Ops:
  0.6 2.1 %pack.1 = (f32[8,64,128]{2,1,0:T(8,128)}, f32[72,256]{1,0:T(8,128)}, f32[64,256]{1,0:T(8,128)}) custom-call(s32[1,64]{1,0:T(1,128)} %bitcast.34, f32[3,4,8,256]{3,2,1,0:T(8,128)} %fem_disp.1, s32[1,64]{1,0:T(1,128)} %bitcast.35, s32[1,64]{1,0:T(1,128)} %bitcast.36, f32[9,64]{1,0:T(8,128)} %conv_state_in.1, s32[1,64]{1,0:T(1,128)} %bitcast.37, ...), custom_call_target="tpu_custom_call" | custom-call | bytes 9360000 | tf_op jit(solution)/shard_map/pack/pallas_call | solution.py:750
  2.7 0.5 %collective-permute-start.1 = (f32[72,256]{1,0:T(8,128)}, f32[72,256]{1,0:T(8,128)S(1)}, u32[]{:S(2)}, u32[]{:S(2)}) collective-permute-start(f32[72,256]{1,0:T(8,128)} %get-tuple-element.28.own.own_side), channel_id=1, source_target_pairs={{0,1},{1,0},{2,3},{3,2},{4,5},{5,4},{6,7},{7,6},{8,9},{9,8},{10,11... | collective-permute-start | bytes 221192 | tf_op jit(solution)/shard_map/ppermute | solution.py:825
  3.2 0.7 %collective-permute-start = (f32[64,256]{1,0:T(8,128)}, f32[64,256]{1,0:T(8,128)S(1)}, u32[]{:S(2)}, u32[]{:S(2)}) collective-permute-start(f32[64,256]{1,0:T(8,128)} %get-tuple-element.26), channel_id=1, source_target_pairs={{1,2},{3,4},{5,6},{7,8},{9,10},{11,12},{13,14},{2,1},{4,3},{6,5},{... | collective-permute-start | bytes 196616 | tf_op jit(solution)/shard_map/ppermute | solution.py:824
  3.9 0.0 copy-start
  3.9 0.0 copy-start.3
  3.9 8.8 %all-to-all-start = ((f32[8,64,128]{2,1,0:T(8,128)}), f32[8,64,128]{2,1,0:T(8,128)S(1)}, u32[]{:S(2)}, u32[]{:S(2)}) async-start(f32[8,64,128]{2,1,0:T(8,128)} %get-tuple-element.33), calls=%async_computation | async-start | bytes 524288 | tf_op jit(solution)/shard_map/all_to_all | solution.py:827
  12.8 0.0 copy-start.7
  12.8 0.7 %copy-done.7 = s32[17,8]{0,1:T(8,128)S(1)} copy-done((s32[17,8]{0,1:T(8,128)S(1)}, s32[17,8]{0,1:T(8,128)}, u32[]{:S(2)}) %copy-start.7) | copy-done | bytes 568
  13.5 0.0 collective-permute-done.odd_side
  13.6 0.0 copy-start.1
  13.7 1.6 %collective-permute-start.2 = (f32[4,10,256]{2,1,0:T(8,128)S(1)}, f32[4,10,256]{2,1,0:T(8,128)S(1)}, u32[]{:S(2)}, u32[]{:S(2)}) collective-permute-start(f32[4,10,256]{2,1,0:T(8,128)S(1)} %bitcast.31), channel_id=1, source_target_pairs={{0,16},{16,0},{1,17},{17,1},{2,18},{18,2},{3,19},{19,3},{4,20},{20... | collective-permute-start | bytes 122888 | tf_op jit(solution)/shard_map/ppermute | solution.py:868
  15.2 0.1 pad_add_fusion.info
  15.3 0.1 reshape.132.flat
  15.4 0.0 copy-start.4
  15.4 0.0 copy-start.6
  15.4 3.7 %bond.1 = (f32[16,8,128]{2,1,0:T(8,128)S(1)}, f32[49,8,128]{2,1,0:T(8,128)S(1)}, s32[1,256]{1,0:T(1,128)S(1)}) custom-call(s32[2]{0:T(128)S(1)} %pad_add_fusion.info, s32[8,17]{1,0:T(8,128)S(1)} %get-tuple-element.55.codes, f32[72,256]{1,0:T(8,128)S(1)} %copy-done.1, f32[72,256]{1,0:T(8,128)S(1)} %collective-permute-done.1.even_side, ...), custom_call_target="tpu_custom_call" | custom-call | bytes 15480000 | tf_op jit(solution)/shard_map/bond/pallas_call | solution.py:750
  19.1 0.0 collective-permute-done.2.low_x.high_x
  19.1 2.8 %all-to-all-done.mine_in = f32[8,64,128]{2,1,0:T(8,128)S(1)} async-done(((f32[8,64,128]{2,1,0:T(8,128)}), f32[8,64,128]{2,1,0:T(8,128)S(1)}, u32[]{:S(2)}, u32[]{:S(2)}) %all-to-all-start) | async-done | bytes 262176 | tf_op jit(solution)/shard_map/all_to_all | solution.py:827
  21.9 1.0 %rock.1 = (f32[3,4,8,256]{3,2,1,0:T(8,128)S(1)}, f32[2,4,8,256]{3,2,1,0:T(8,128)S(1)}, bf16[32,192]{1,0:T(8,128)(2,1)S(1)}, bf16[32,16,256]{2,1,0:T(8,128)(2,1)S(1)}, bf16[32,16,256]{2,1,0:T(8,128)(2,1)S(1)}) custom-call(f32[3,4,8,256]{3,2,1,0:T(8,128)S(1)} %copy-done, f32[3,4,8,256]{3,2,1,0:T(8,128)S(1)} %copy-done.4, f32[4,8,256]{2,1,0:T(8,128)S(1)} %copy-done.3, ...), custom_call_target="tpu_custom_call" | custom-call | bytes 4320000 | tf_op jit(solution)/shard_map/rock/pallas_call | solution.py:750
  23.0 1.1 %outer.1 = (f32[3,4,8,256]{3,2,1,0:T(8,128)S(1)}, f32[2,2,8,256]{3,2,1,0:T(8,128)S(1)}) custom-call(s32[2]{0:T(128)S(1)} %pad_add_fusion.info, f32[3,4,8,256]{3,2,1,0:T(8,128)S(1)} %get-tuple-element.36.rock, f32[4,8,256]{2,1,0:T(8,128)S(1)} %copy-done.2, f32[4,8,256]{2,1,0:T(8,128)S(1)} %copy-done.3, bf16[32,192]{1,0:T(8,128)(2,1)S(1)} %get-tuple-element.37.left_in, ...), custom_call_target="tpu_custom_call" | custom-call | bytes 2880000 | tf_op jit(solution)/shard_map/outer/pallas_call | solution.py:750
  24.1 0.0 copy-start.5
  24.1 1.0 %edge.1 = (f32[3,4,8,256]{3,2,1,0:T(8,128)S(1)}, f32[3,16,128]{2,1,0:T(8,128)S(1)}, f32[8,64]{1,0:T(8,128)S(1)}) custom-call(s32[2]{0:T(128)S(1)} %pad_add_fusion.info, f32[8,64,128]{2,1,0:T(8,128)S(1)} %all-to-all-done.mine_in, f32[72,256]{1,0:T(8,128)S(1)} %copy-done.1, f32[3,4,8,256]{3,2,1,0:T(8,128)S(1)} %get-tuple-element.43.rock, ...), custom_call_target="tpu_custom_call" | custom-call | bytes 3600000 | tf_op jit(solution)/shard_map/edge/pallas_call | solution.py:750
  25.1 0.0 collective-permute-done.3.mate_in
  25.1 2.6 %final.1 = (f32[3,4,8,256]{3,2,1,0:T(8,128)}, f32[3,2176]{1,0:T(4,128)}) custom-call(s32[2]{0:T(128)S(1)} %pad_add_fusion.info, s32[1,256]{1,0:T(1,128)S(1)} %get-tuple-element.32.pairs, s32[8,17]{1,0:T(8,128)S(1)} %get-tuple-element.55.codes, f32[8,64,128]{2,1,0:T(8,128)S(1)} %collective-permute-done.3.mate_in, f32[72,256]{1,0:T(8,128)S(1)} %copy-done.1, ...), custom_call_target="tpu_custom_call" | custom-call | bytes 9360000 | tf_op jit(solution)/shard_map/final/pallas_call | solution.py:750
  (18 shorter events, 0.2 us)
Async XLA Ops:
  2.7 10.8 %collective-permute-start.1 = (f32[72,256]{1,0:T(8,128)}, f32[72,256]{1,0:T(8,128)S(1)}, u32[]{:S(2)}, u32[]{:S(2)}) collective-permute-start(f32[72,256]{1,0:T(8,128)} %get-tuple-element.28.own.own_side), channel_id=1, source_target_pairs={{0,1},{1,0},{2,3},{3,2},{4,5},{5,4},{6,7},{7,6},{8,9},{9,8},{10,11... | collective-permute-start | bytes 221192 | tf_op jit(solution)/shard_map/ppermute | solution.py:825
  3.2 10.3 %collective-permute-start = (f32[64,256]{1,0:T(8,128)}, f32[64,256]{1,0:T(8,128)S(1)}, u32[]{:S(2)}, u32[]{:S(2)}) collective-permute-start(f32[64,256]{1,0:T(8,128)} %get-tuple-element.26), channel_id=1, source_target_pairs={{1,2},{3,4},{5,6},{7,8},{9,10},{11,12},{13,14},{2,1},{4,3},{6,5},{... | collective-permute-start | bytes 196616 | tf_op jit(solution)/shard_map/ppermute | solution.py:824
  3.9 8.9 %copy-start = (f32[3,4,8,256]{3,2,1,0:T(8,128)S(1)}, f32[3,4,8,256]{3,2,1,0:T(8,128)}, u32[]{:S(2)}) copy-start(f32[3,4,8,256]{3,2,1,0:T(8,128)} %fem_disp.1) | copy-start | bytes 294916
  3.9 8.9 %copy-start.3 = (f32[4,8,256]{2,1,0:T(8,128)S(1)}, f32[4,8,256]{2,1,0:T(8,128)}, u32[]{:S(2)}) copy-start(f32[4,8,256]{2,1,0:T(8,128)} %modulus.3) | copy-start | bytes 98308
  3.9 18.0 %all-to-all-start = ((f32[8,64,128]{2,1,0:T(8,128)}), f32[8,64,128]{2,1,0:T(8,128)S(1)}, u32[]{:S(2)}, u32[]{:S(2)}) async-start(f32[8,64,128]{2,1,0:T(8,128)} %get-tuple-element.33), calls=%async_computation | async-start | bytes 524288 | tf_op jit(solution)/shard_map/all_to_all | solution.py:827
  12.8 0.7 %copy-start.7 = (s32[17,8]{0,1:T(8,128)S(1)}, s32[17,8]{0,1:T(8,128)}, u32[]{:S(2)}) copy-start(s32[17,8]{0,1:T(8,128)} %param.25) | copy-start | bytes 1636
  13.6 1.8 %copy-start.1 = (f32[72,256]{1,0:T(8,128)S(1)}, f32[72,256]{1,0:T(8,128)}, u32[]{:S(2)}) copy-start(f32[72,256]{1,0:T(8,128)} %get-tuple-element.28.own.own_side) | copy-start | bytes 221188
  13.7 5.4 %collective-permute-start.2 = (f32[4,10,256]{2,1,0:T(8,128)S(1)}, f32[4,10,256]{2,1,0:T(8,128)S(1)}, u32[]{:S(2)}, u32[]{:S(2)}) collective-permute-start(f32[4,10,256]{2,1,0:T(8,128)S(1)} %bitcast.31), channel_id=1, source_target_pairs={{0,16},{16,0},{1,17},{17,1},{2,18},{18,2},{3,19},{19,3},{4,20},{20... | collective-permute-start | bytes 122888 | tf_op jit(solution)/shard_map/ppermute | solution.py:868
  15.4 6.5 %copy-start.2 = (f32[4,8,256]{2,1,0:T(8,128)S(1)}, f32[4,8,256]{2,1,0:T(8,128)}, u32[]{:S(2)}) copy-start(f32[4,8,256]{2,1,0:T(8,128)} %inv_mass.7) | copy-start | bytes 98308
  15.4 6.5 %copy-start.4 = (f32[3,4,8,256]{3,2,1,0:T(8,128)S(1)}, f32[3,4,8,256]{3,2,1,0:T(8,128)}, u32[]{:S(2)}) copy-start(f32[3,4,8,256]{3,2,1,0:T(8,128)} %fem_vel.1) | copy-start | bytes 294916
  15.4 6.5 %copy-start.6 = (f32[24,24]{1,0:T(8,128)S(1)}, f32[24,24]{1,0:T(8,128)}, u32[]{:S(2)}) copy-start(f32[24,24]{1,0:T(8,128)} %stiffness.1) | copy-start | bytes 6916
  21.9 3.2 %collective-permute-start.3 = (f32[8,64,128]{2,1,0:T(8,128)S(1)}, f32[8,64,128]{2,1,0:T(8,128)S(1)}, u32[]{:S(2)}, u32[]{:S(2)}) collective-permute-start(f32[8,64,128]{2,1,0:T(8,128)S(1)} %all-to-all-done.mine_in), channel_id=1, source_target_pairs={{0,1},{1,0},{2,3},{3,2},{4,5},{5,4},{6,7},{7,6},{8,9},{9,8},{10,11... | collective-permute-start | bytes 786440 | tf_op jit(solution)/shard_map/ppermute | solution.py:884
  24.1 1.1 %copy-start.5 = (f32[3,2048]{1,0:T(4,128)S(1)}, f32[3,2048]{1,0:T(4,128)}, u32[]{:S(2)}) copy-start(f32[3,2048]{1,0:T(4,128)} %pd_vel.1) | copy-start | bytes 73732

commit v5 on v4

--- a/solution.py
+++ b/solution.py
@@ -294,9 +294,10 @@
 
 
 def bond_kernel(
-    peers, tail_blocks, members, info, codes, own, even_side, odd_side, flat, after, sums_out, tables, pairs, left_ref, sums_ref
+    peers, tail_blocks, members, info, codes, own, even_side, odd_side, flat, stiffness, after, sums_out, tables, pairs, left_out, left_ref, sums_ref
 ):
     list_tail_pairs(flat, pairs, tail_blocks)
+    left_out[...] = stiffness_rows(stiffness[...])
     blocks = sums_out.shape[0]
     mine = []
     for block in range(blocks):
@@ -410,10 +411,9 @@
     fem_vel,
     modulus,
     inv_mass,
-    stiffness,
+    left_in,
     out,
     edge_nodes,
-    left_out,
     first_ref,
     second_ref,
     nodes,
@@ -421,8 +421,7 @@
 ):
     nx, ny, nz = modulus.shape
     halves = [slice(h * BLOCK, (h + 1) * BLOCK) for h in range(nz // BLOCK)]
-    left = stiffness_rows(stiffness[...])
-    left_out[...] = left
+    left = left_in[...]
     for x in range(nx):
         put_nodes(nodes, x * ny * 8, ny, [fem_disp[0, x], fem_disp[1, x], fem_disp[2, x], modulus[x]], halves)
     for x in range(nx):
@@ -831,24 +830,6 @@
     block_of = jnp.arange(table, dtype=jnp.int32)[None, :]
     flat = codes >> PAIR_SHIFT
     flat = ((flat >> PAIR_SHIFT) << (2 * PAIR_SHIFT)) + (block_of << PAIR_SHIFT) + low_bits(flat)
-    rock, edge_nodes, left, first_parts, second_parts = call(
-        rock_kernel,
-        (
-            shaped(fem_vel.shape, F32),
-            shaped((2, nx, 8, nz), F32),
-            shaped((32, 192), BF16),
-            shaped((node_count, 16, nz), BF16),
-            shaped((node_count, 16, nz), BF16),
-        ),
-        [VMEM] * 5,
-        [
-            pltpu.VMEM((nz // BLOCK, node_count * 8, BLOCK), F32),
-            pltpu.VMEM((nz // BLOCK, node_count * 8, BLOCK), F32),
-        ],
-        1.2,
-        (fem_disp, fem_vel, modulus, inv_mass, element_stiffness),
-        "rock",
-    )
     count_faces = 2 if both_faces else 1
     rows = jnp.stack([even_side[: 4 * blocks], odd_side]).reshape(2, blocks // 2, 2, 4, nz)[:, :, :, 3]
     rows = rows.reshape(2, blocks, nz)[:, : 4 * nx].reshape(2, nx, 4, nz)
@@ -867,18 +848,36 @@
     else:
         low_x = high_x = lax.ppermute(faces[0], "depth", [(0, 1), (1, 0)])
 
-    sums, tables, pairs = call(
+    sums, tables, pairs, left = call(
         functools.partial(bond_kernel, peers, tail_blocks, members),
         (
             shaped((blocks, 8, BLOCK), F32),
             shaped((3 * blocks + 1, 8, BLOCK), F32),
             shaped((1, PAIR_SLOTS), jnp.int32),
+            shaped((32, 192), BF16),
         ),
-        [SMEM, SMEM] + [VMEM] * 4 + [ANY],
+        [SMEM, SMEM] + [VMEM] * 5 + [ANY],
         [pltpu.VMEM((3 * blocks + 1, BLOCK, 48), BF16), pltpu.VMEM((3 * blocks + 1, 32, BLOCK), BF16)],
         4.3,
-        (info, codes, pay_even, even_side, odd_side, flat.reshape(1, -1), faces),
+        (info, codes, pay_even, even_side, odd_side, flat.reshape(1, -1), element_stiffness, faces),
         "bond",
+    )
+    rock, edge_nodes, first_parts, second_parts = call(
+        rock_kernel,
+        (
+            shaped(fem_vel.shape, F32),
+            shaped((2, nx, 8, nz), F32),
+            shaped((node_count, 16, nz), BF16),
+            shaped((node_count, 16, nz), BF16),
+        ),
+        [VMEM] * 5,
+        [
+            pltpu.VMEM((nz // BLOCK, node_count * 8, BLOCK), F32),
+            pltpu.VMEM((nz // BLOCK, node_count * 8, BLOCK), F32),
+        ],
+        1.2,
+        (fem_disp, fem_vel, modulus, inv_mass, left),
+        "rock",
     )
     mine, sums, low_x, high_x = lax.optimization_barrier((mine, sums, low_x, high_x))
     mate = lax.ppermute(mine, "lat", swap)

time: 28.1 us -> 27.8 us (0.989)
  Pallas kernels: 11.5 us -> 11.1 us
    pallas_call x6, Pallas kernels: 11.5 us -> 11.1 us  [call(): pl.pallas_call(kernel, out_shape=outs, in_specs=specs, out_specs=out_spec...]
  transfers between devices with their start and end apart: 5 -> 5, of which waited for: 1 -> 1; matrix products, arithmetic and copies ran while one was open for 1% -> 1% of each run, Pallas kernels for 25% -> 23%
where the time goes in v5:
time: 27.8 us; the launch traced here: 27.4 us
  starting transfers between devices  11.6 us (42%)
  Pallas kernels  11.1 us (40%)
  waiting for transfers between devices  2.87 us (10%)
  between operations  0.85 us (3%)
  local copies, waits for them, and re-layouts  0.84 us (3%)
    pallas_call x6, Pallas kernels, call(): pl.pallas_call(kernel, out_shape=outs, in_specs=specs, out_specs=out_spec...  11.1 us
    all_to_all x1, starting transfers between devices, shards(): lax.all_to_all(chunk, 'lat', split_axis=0, concat_axis=0, tiled=True, axi...  8.84 us
    all_to_all x1, waiting for transfers between devices, shards(): lax.all_to_all(chunk, 'lat', split_axis=0, concat_axis=0, tiled=True, axi...  2.85 us
    ppermute x1, starting transfers between devices, shards(): low_x = high_x = lax.ppermute(faces[0], 'depth', [(0, 1), (1, 0)])  1.55 us
    unnamed x16, local copies, waits for them, and re-layouts  0.71 us
    ppermute x1, starting transfers between devices, shards(): odd_side = lax.ppermute(pay_odd, 'lat', cross)  0.65 us
  transfers between devices with their start and end apart: 5, of which 1 were waited for; matrix products, arithmetic and copies ran while one was open for 1% of the time, Pallas kernels for 23%

profile of v5, /device:TPU:0, one launch (start us, length us, event | category | flops | bytes accessed | tf_op | source)
XLA Modules:
  0.0 27.4 jit_solution(8370144749843448309)
XLA Ops:
  0.6 2.1 %pack.1 = (f32[8,64,128]{2,1,0:T(8,128)}, f32[72,256]{1,0:T(8,128)}, f32[64,256]{1,0:T(8,128)}) custom-call(s32[1,64]{1,0:T(1,128)} %bitcast.34, f32[3,4,8,256]{3,2,1,0:T(8,128)} %fem_disp.1, s32[1,64]{1,0:T(1,128)} %bitcast.35, s32[1,64]{1,0:T(1,128)} %bitcast.36, f32[9,64]{1,0:T(8,128)} %conv_state_in.1, s32[1,64]{1,0:T(1,128)} %bitcast.37, ...), custom_call_target="tpu_custom_call" | custom-call | bytes 9360000 | tf_op jit(solution)/shard_map/pack/pallas_call | solution.py:749
  2.7 0.5 %collective-permute-start.1 = (f32[72,256]{1,0:T(8,128)}, f32[72,256]{1,0:T(8,128)S(1)}, u32[]{:S(2)}, u32[]{:S(2)}) collective-permute-start(f32[72,256]{1,0:T(8,128)} %get-tuple-element.28.own.own_side), channel_id=1, source_target_pairs={{0,1},{1,0},{2,3},{3,2},{4,5},{5,4},{6,7},{7,6},{8,9},{9,8},{10,11... | collective-permute-start | bytes 221192 | tf_op jit(solution)/shard_map/ppermute | solution.py:824
  3.2 0.7 %collective-permute-start = (f32[64,256]{1,0:T(8,128)}, f32[64,256]{1,0:T(8,128)S(1)}, u32[]{:S(2)}, u32[]{:S(2)}) collective-permute-start(f32[64,256]{1,0:T(8,128)} %get-tuple-element.26), channel_id=1, source_target_pairs={{1,2},{3,4},{5,6},{7,8},{9,10},{11,12},{13,14},{2,1},{4,3},{6,5},{... | collective-permute-start | bytes 196616 | tf_op jit(solution)/shard_map/ppermute | solution.py:823
  3.9 0.0 copy-start
  3.9 0.0 copy-start.3
  3.9 8.8 %all-to-all-start = ((f32[8,64,128]{2,1,0:T(8,128)}), f32[8,64,128]{2,1,0:T(8,128)S(1)}, u32[]{:S(2)}, u32[]{:S(2)}) async-start(f32[8,64,128]{2,1,0:T(8,128)} %get-tuple-element.33), calls=%async_computation | async-start | bytes 524288 | tf_op jit(solution)/shard_map/all_to_all | solution.py:826
  12.8 0.0 copy-start.7
  12.8 0.7 %copy-done.7 = s32[17,8]{0,1:T(8,128)S(1)} copy-done((s32[17,8]{0,1:T(8,128)S(1)}, s32[17,8]{0,1:T(8,128)}, u32[]{:S(2)}) %copy-start.7) | copy-done | bytes 568
  13.6 0.0 copy-start.1
  13.7 0.0 copy-start.6
  13.7 1.6 %collective-permute-start.2 = (f32[4,10,256]{2,1,0:T(8,128)S(1)}, f32[4,10,256]{2,1,0:T(8,128)S(1)}, u32[]{:S(2)}, u32[]{:S(2)}) collective-permute-start(f32[4,10,256]{2,1,0:T(8,128)S(1)} %bitcast.31), channel_id=1, source_target_pairs={{0,16},{16,0},{1,17},{17,1},{2,18},{18,2},{3,19},{19,3},{4,20},{20... | collective-permute-start | bytes 122888 | tf_op jit(solution)/shard_map/ppermute | solution.py:849
  15.2 0.1 pad_add_fusion.info
  15.3 0.1 reshape.132.flat
  15.4 0.0 copy-start.2
  15.4 0.0 copy-start.4
  15.4 3.6 %bond.1 = (f32[16,8,128]{2,1,0:T(8,128)S(1)}, f32[49,8,128]{2,1,0:T(8,128)S(1)}, s32[1,256]{1,0:T(1,128)S(1)}, bf16[32,192]{1,0:T(8,128)(2,1)S(1)}) custom-call(s32[2]{0:T(128)S(1)} %pad_add_fusion.info, s32[8,17]{1,0:T(8,128)S(1)} %get-tuple-element.55.codes, f32[72,256]{1,0:T(8,128)S(1)} %copy-done.1, f32[72,256]{1,0:T(8,128)S(1)} %collective-permute-done.1.even_side, ...), custom_call_target="tpu_custom_call" | custom-call | bytes 15480000 | tf_op jit(solution)/shard_map/bond/pallas_call | solution.py:749
  19.0 0.0 collective-permute-done.2.low_x.high_x
  19.1 2.8 %all-to-all-done.mine_in = f32[8,64,128]{2,1,0:T(8,128)S(1)} async-done(((f32[8,64,128]{2,1,0:T(8,128)}), f32[8,64,128]{2,1,0:T(8,128)S(1)}, u32[]{:S(2)}, u32[]{:S(2)}) %all-to-all-start) | async-done | bytes 262176 | tf_op jit(solution)/shard_map/all_to_all | solution.py:826
  21.9 0.7 %rock.1 = (f32[3,4,8,256]{3,2,1,0:T(8,128)S(1)}, f32[2,4,8,256]{3,2,1,0:T(8,128)S(1)}, bf16[32,16,256]{2,1,0:T(8,128)(2,1)S(1)}, bf16[32,16,256]{2,1,0:T(8,128)(2,1)S(1)}) custom-call(f32[3,4,8,256]{3,2,1,0:T(8,128)S(1)} %copy-done, f32[3,4,8,256]{3,2,1,0:T(8,128)S(1)} %copy-done.4, f32[4,8,256]{2,1,0:T(8,128)S(1)} %copy-done.3, f32[4,8,256]{2,1,0:T(8,128)S(1)} %copy-done.2, ...), custom_call_target="tpu_custom_call" | custom-call | bytes 4320000 | tf_op jit(solution)/shard_map/rock/pallas_call | solution.py:749
  22.6 1.1 %outer.1 = (f32[3,4,8,256]{3,2,1,0:T(8,128)S(1)}, f32[2,2,8,256]{3,2,1,0:T(8,128)S(1)}) custom-call(s32[2]{0:T(128)S(1)} %pad_add_fusion.info, f32[3,4,8,256]{3,2,1,0:T(8,128)S(1)} %get-tuple-element.37.rock, f32[4,8,256]{2,1,0:T(8,128)S(1)} %copy-done.2, f32[4,8,256]{2,1,0:T(8,128)S(1)} %copy-done.3, bf16[32,192]{1,0:T(8,128)(2,1)S(1)} %get-tuple-element.36.left_in, ...), custom_call_target="tpu_custom_call" | custom-call | bytes 2880000 | tf_op jit(solution)/shard_map/outer/pallas_call | solution.py:749
  23.7 0.0 copy-start.5
  23.7 1.0 %edge.1 = (f32[3,4,8,256]{3,2,1,0:T(8,128)S(1)}, f32[3,16,128]{2,1,0:T(8,128)S(1)}, f32[8,64]{1,0:T(8,128)S(1)}) custom-call(s32[2]{0:T(128)S(1)} %pad_add_fusion.info, f32[8,64,128]{2,1,0:T(8,128)S(1)} %all-to-all-done.mine_in, f32[72,256]{1,0:T(8,128)S(1)} %copy-done.1, f32[3,4,8,256]{3,2,1,0:T(8,128)S(1)} %get-tuple-element.43.rock, ...), custom_call_target="tpu_custom_call" | custom-call | bytes 3600000 | tf_op jit(solution)/shard_map/edge/pallas_call | solution.py:749
  24.8 0.0 collective-permute-done.3.mate_in
  24.8 2.6 %final.1 = (f32[3,4,8,256]{3,2,1,0:T(8,128)}, f32[3,2176]{1,0:T(4,128)}) custom-call(s32[2]{0:T(128)S(1)} %pad_add_fusion.info, s32[1,256]{1,0:T(1,128)S(1)} %get-tuple-element.32.pairs, s32[8,17]{1,0:T(8,128)S(1)} %get-tuple-element.55.codes, f32[8,64,128]{2,1,0:T(8,128)S(1)} %collective-permute-done.3.mate_in, f32[72,256]{1,0:T(8,128)S(1)} %copy-done.1, ...), custom_call_target="tpu_custom_call" | custom-call | bytes 9360000 | tf_op jit(solution)/shard_map/final/pallas_call | solution.py:749
  (18 shorter events, 0.2 us)
Async XLA Ops:
  2.7 10.8 %collective-permute-start.1 = (f32[72,256]{1,0:T(8,128)}, f32[72,256]{1,0:T(8,128)S(1)}, u32[]{:S(2)}, u32[]{:S(2)}) collective-permute-start(f32[72,256]{1,0:T(8,128)} %get-tuple-element.28.own.own_side), channel_id=1, source_target_pairs={{0,1},{1,0},{2,3},{3,2},{4,5},{5,4},{6,7},{7,6},{8,9},{9,8},{10,11... | collective-permute-start | bytes 221192 | tf_op jit(solution)/shard_map/ppermute | solution.py:824
  3.2 10.3 %collective-permute-start = (f32[64,256]{1,0:T(8,128)}, f32[64,256]{1,0:T(8,128)S(1)}, u32[]{:S(2)}, u32[]{:S(2)}) collective-permute-start(f32[64,256]{1,0:T(8,128)} %get-tuple-element.26), channel_id=1, source_target_pairs={{1,2},{3,4},{5,6},{7,8},{9,10},{11,12},{13,14},{2,1},{4,3},{6,5},{... | collective-permute-start | bytes 196616 | tf_op jit(solution)/shard_map/ppermute | solution.py:823
  3.9 8.9 %copy-start = (f32[3,4,8,256]{3,2,1,0:T(8,128)S(1)}, f32[3,4,8,256]{3,2,1,0:T(8,128)}, u32[]{:S(2)}) copy-start(f32[3,4,8,256]{3,2,1,0:T(8,128)} %fem_disp.1) | copy-start | bytes 294916
  3.9 8.9 %copy-start.3 = (f32[4,8,256]{2,1,0:T(8,128)S(1)}, f32[4,8,256]{2,1,0:T(8,128)}, u32[]{:S(2)}) copy-start(f32[4,8,256]{2,1,0:T(8,128)} %modulus.3) | copy-start | bytes 98308
  3.9 18.0 %all-to-all-start = ((f32[8,64,128]{2,1,0:T(8,128)}), f32[8,64,128]{2,1,0:T(8,128)S(1)}, u32[]{:S(2)}, u32[]{:S(2)}) async-start(f32[8,64,128]{2,1,0:T(8,128)} %get-tuple-element.33), calls=%async_computation | async-start | bytes 524288 | tf_op jit(solution)/shard_map/all_to_all | solution.py:826
  12.8 0.7 %copy-start.7 = (s32[17,8]{0,1:T(8,128)S(1)}, s32[17,8]{0,1:T(8,128)}, u32[]{:S(2)}) copy-start(s32[17,8]{0,1:T(8,128)} %param.25) | copy-start | bytes 1636
  13.6 1.8 %copy-start.1 = (f32[72,256]{1,0:T(8,128)S(1)}, f32[72,256]{1,0:T(8,128)}, u32[]{:S(2)}) copy-start(f32[72,256]{1,0:T(8,128)} %get-tuple-element.28.own.own_side) | copy-start | bytes 221188
  13.7 1.7 %copy-start.6 = (f32[24,24]{1,0:T(8,128)S(1)}, f32[24,24]{1,0:T(8,128)}, u32[]{:S(2)}) copy-start(f32[24,24]{1,0:T(8,128)} %stiffness.1) | copy-start | bytes 6916
  13.7 5.4 %collective-permute-start.2 = (f32[4,10,256]{2,1,0:T(8,128)S(1)}, f32[4,10,256]{2,1,0:T(8,128)S(1)}, u32[]{:S(2)}, u32[]{:S(2)}) collective-permute-start(f32[4,10,256]{2,1,0:T(8,128)S(1)} %bitcast.31), channel_id=1, source_target_pairs={{0,16},{16,0},{1,17},{17,1},{2,18},{18,2},{3,19},{19,3},{4,20},{20... | collective-permute-start | bytes 122888 | tf_op jit(solution)/shard_map/ppermute | solution.py:849
  15.4 6.5 %copy-start.2 = (f32[4,8,256]{2,1,0:T(8,128)S(1)}, f32[4,8,256]{2,1,0:T(8,128)}, u32[]{:S(2)}) copy-start(f32[4,8,256]{2,1,0:T(8,128)} %inv_mass.7) | copy-start | bytes 98308
  15.4 6.5 %copy-start.4 = (f32[3,4,8,256]{3,2,1,0:T(8,128)S(1)}, f32[3,4,8,256]{3,2,1,0:T(8,128)}, u32[]{:S(2)}) copy-start(f32[3,4,8,256]{3,2,1,0:T(8,128)} %fem_vel.1) | copy-start | bytes 294916
  21.9 2.8 %collective-permute-start.3 = (f32[8,64,128]{2,1,0:T(8,128)S(1)}, f32[8,64,128]{2,1,0:T(8,128)S(1)}, u32[]{:S(2)}, u32[]{:S(2)}) collective-permute-start(f32[8,64,128]{2,1,0:T(8,128)S(1)} %all-to-all-done.mine_in), channel_id=1, source_target_pairs={{0,1},{1,0},{2,3},{3,2},{4,5},{5,4},{6,7},{7,6},{8,9},{9,8},{10,11... | collective-permute-start | bytes 786440 | tf_op jit(solution)/shard_map/ppermute | solution.py:883
  23.7 1.1 %copy-start.5 = (f32[3,2048]{1,0:T(4,128)S(1)}, f32[3,2048]{1,0:T(4,128)}, u32[]{:S(2)}) copy-start(f32[3,2048]{1,0:T(4,128)} %pd_vel.1) | copy-start | bytes 73732
